TPU v7x, 32 devices: a whole 2x2x4 slice. The times are simulated.
32 devices in a mesh: dp: 8 (over z, x), seq: 4 (over y, core).
Axes of the slice: x: 2, y: 2, z: 4, core: 2. Of those that a mesh axis runs over, the one named last changes fastest.
Arguments:
- inputs: bfloat16 [8, 1024, 512], P('dp', 'seq'), may hold values from -6 to 6
- cotangent: bfloat16 [8, 1024, 512], P('dp', 'seq'), may hold values from -6 to 6
- w_qkv: bfloat16 [512, 1536], P(('dp', 'seq')), may hold values from -0.25 to 0.25
- b_qkv: bfloat16 [1536], P(('dp', 'seq')), may hold values from -2.5 to 2.5
- w_out: bfloat16 [512, 512], P(('dp', 'seq')), may hold values from -2 to 2
- b_out: bfloat16 [512], P(('dp', 'seq')), may hold values from -2.5 to 2.5
- w_up: bfloat16 [512, 2048], P(('dp', 'seq')), may hold values from -0.25 to 0.25
- b_up: bfloat16 [2048], P(('dp', 'seq')), may hold values from -2.5 to 2.5
- w_down: bfloat16 [2048, 512], P(('dp', 'seq')), may hold values from -0.125 to 0.125
- b_down: bfloat16 [512], P(('dp', 'seq')), may hold values from -2.5 to 2.5
- gain_one: bfloat16 [512], P(('dp', 'seq')), may hold values from 0.5 to 1.5
- shift_one: bfloat16 [512], P(('dp', 'seq')), may hold values from -2.5 to 2.5
- gain_two: bfloat16 [512], P(('dp', 'seq')), may hold values from 0.5 to 1.5
- shift_two: bfloat16 [512], P(('dp', 'seq')), may hold values from -2.5 to 2.5
Outputs:
- outputs: bfloat16 [8, 1024, 512], P('dp', 'seq')
- grad_inputs: bfloat16 [8, 1024, 512], P('dp', 'seq')
- grad_w_qkv: float32 [512, 1536], P(('dp', 'seq'))
- grad_b_qkv: float32 [1536], P(('dp', 'seq'))
- grad_w_out: float32 [512, 512], P(('dp', 'seq'))
- grad_b_out: float32 [512], P(('dp', 'seq'))
- grad_w_up: float32 [512, 2048], P(('dp', 'seq'))
- grad_b_up: float32 [2048], P(('dp', 'seq'))
- grad_w_down: float32 [2048, 512], P(('dp', 'seq'))
- grad_b_down: float32 [512], P(('dp', 'seq'))
- grad_gain_one: float32 [512], P(('dp', 'seq'))
- grad_shift_one: float32 [512], P(('dp', 'seq'))
- grad_gain_two: float32 [512], P(('dp', 'seq'))
- grad_shift_two: float32 [512], P(('dp', 'seq'))
All inputs are finite; a program needn't handle non-finite values.
Results may differ from a plain program's by a relative error of at most 0.009.
Values may be sent and summed in bfloat16 or wider, within the bound.
No kernel may reach another device: no remote copies, remote signals or barrier semaphores. Data moves between devices by JAX's collectives and lax.ppermute only.
A program may use at most 128 MiB of HBM per device.

v0:
```python
import math

import jax
import jax.numpy as jnp
from jax import lax
from jax.sharding import PartitionSpec as P

H = 8
HD = 64
ROT = 16


EPS = 1e-05


def norm_rows(values, gain_vec, shifts):
    average = jnp.mean(values, axis=-1, keepdims=True)
    centered = values - average
    variance = jnp.mean(centered * centered, axis=-1, keepdims=True)
    return centered * lax.rsqrt(variance + EPS) * gain_vec + shifts


def rotate(values, cosine_table, sine_table):
    half_width = cosine_table.shape[-1]
    front_part = values[..., :half_width]
    second = values[..., half_width : 2 * half_width]
    remainder = values[..., 2 * half_width :]
    return jnp.concatenate(
        [
            front_part * cosine_table - second * sine_table,
            second * cosine_table + front_part * sine_table,
            remainder,
        ],
        axis=-1,
    )


def rotary_tables(positions):
    ladder = jnp.arange(ROT // 2).astype(jnp.float32)
    frequency = jnp.exp(ladder * (-2.0 * math.log(10000.0) / ROT))
    angles = positions.astype(jnp.float32)[:, None] * frequency[None, :]
    return (jnp.cos(angles)[:, None, :], jnp.sin(angles)[:, None, :])


def gelu_exact(values):
    return jax.nn.gelu(values, approximate=False)


def cross_rows(left, right):
    return lax.dot_general(
        left, right, (((0,), (0,)), ((), ())), preferred_element_type=jnp.float32
    )


def against(left, right):
    return lax.dot_general(
        left, right, (((1,), (1,)), ((), ())), preferred_element_type=jnp.float32
    )


def split_heads(block_rows, row_count):
    return block_rows.reshape(row_count, H // 4, 4, HD).transpose(1, 0, 2, 3)


def merge_heads(grouped, row_count):
    return grouped.transpose(1, 0, 2, 3).reshape(row_count, H * HD)


def attend_forward(query_g, key_g, value_g, allowed):
    factor = query_g.shape[-1] ** (-0.5)
    scores = jnp.einsum("qhd,khd->hqk", query_g, key_g, preferred_element_type=jnp.float32) * factor
    scores = jnp.where(allowed[None], scores, -1e30)
    highest = jnp.max(scores, axis=-1, keepdims=True)
    raised = jnp.exp(scores - highest)
    totals = jnp.sum(raised, axis=-1, keepdims=True)
    weights_low = (raised / totals).astype(jnp.bfloat16)
    attended = jnp.einsum("hqk,khd->qhd", weights_low, value_g, preferred_element_type=jnp.float32)
    return (attended, highest + jnp.log(totals))


def attend_backward(query_g, key_g, value_g, grad_g, log_total, allowed):
    factor = query_g.shape[-1] ** (-0.5)
    scores = jnp.einsum("qhd,khd->hqk", query_g, key_g, preferred_element_type=jnp.float32) * factor
    scores = jnp.where(allowed[None], scores, -1e30)
    weights_full = jnp.exp(scores - log_total)
    grad_weights = jnp.einsum("qhd,khd->hqk", grad_g, value_g, preferred_element_type=jnp.float32)
    inner_sum = jnp.sum(weights_full * grad_weights, axis=-1, keepdims=True)
    grad_scores = (weights_full * (grad_weights - inner_sum)).astype(jnp.bfloat16)
    grad_query = (
        jnp.einsum("hqk,khd->qhd", grad_scores, key_g, preferred_element_type=jnp.float32) * factor
    )
    grad_key = (
        jnp.einsum("hqk,qhd->khd", grad_scores, query_g, preferred_element_type=jnp.float32)
        * factor
    )
    grad_value = jnp.einsum(
        "hqk,qhd->khd",
        weights_full.astype(jnp.bfloat16),
        grad_g,
        preferred_element_type=jnp.float32,
    )
    return (grad_query, grad_key, grad_value, inner_sum)


def shards(
    inputs,
    cotangent,
    w_qkv,
    b_qkv,
    w_out,
    b_out,
    w_up,
    b_up,
    w_down,
    b_down,
    gain_one,
    shift_one,
    gain_two,
    shift_two,
):
    weights = (
        lax.all_gather(w_qkv, ("dp", "seq"), axis=0, tiled=True),
        lax.all_gather(b_qkv, ("dp", "seq"), axis=0, tiled=True),
        lax.all_gather(w_out, ("dp", "seq"), axis=0, tiled=True),
        lax.all_gather(b_out, ("dp", "seq"), axis=0, tiled=True),
        lax.all_gather(w_up, ("dp", "seq"), axis=0, tiled=True),
        lax.all_gather(b_up, ("dp", "seq"), axis=0, tiled=True),
        lax.all_gather(w_down, ("dp", "seq"), axis=0, tiled=True),
        lax.all_gather(b_down, ("dp", "seq"), axis=0, tiled=True),
        lax.all_gather(gain_one, ("dp", "seq"), axis=0, tiled=True),
        lax.all_gather(shift_one, ("dp", "seq"), axis=0, tiled=True),
        lax.all_gather(gain_two, ("dp", "seq"), axis=0, tiled=True),
        lax.all_gather(shift_two, ("dp", "seq"), axis=0, tiled=True),
    )
    full_qkv, full_bqkv, full_wout, full_bout, full_wup, full_bup, full_wdown, full_bdown = weights[
        :8
    ]
    full_gone, full_sone, full_gtwo, full_stwo = weights[8:]
    local_rows = inputs.shape[1]
    model_width = H * HD
    rows_in = inputs[0].astype(jnp.float32)
    positions = lax.axis_index("seq") * local_rows + jnp.arange(local_rows, dtype=jnp.int32)
    cosine_table, sine_table = rotary_tables(positions)
    normed_a, back_norm_a = jax.vjp(
        norm_rows, rows_in, full_gone.astype(jnp.float32), full_sone.astype(jnp.float32)
    )
    normed_a = normed_a.astype(jnp.bfloat16)
    projected = jnp.dot(normed_a, full_qkv, preferred_element_type=jnp.float32) + full_bqkv.astype(
        jnp.float32
    )
    raw_query = projected[:, :model_width].reshape(local_rows, H, HD)
    raw_key = projected[:, model_width : 2 * model_width].reshape(local_rows, H, HD)
    value_rows = projected[:, 2 * model_width :].astype(jnp.bfloat16)

    def turn_both(query_in, key_in):
        return (
            rotate(query_in, cosine_table, sine_table),
            rotate(key_in, cosine_table, sine_table),
        )

    (turned_query, turned_key), back_turn = jax.vjp(turn_both, raw_query, raw_key)
    queries = turned_query.reshape(local_rows, model_width).astype(jnp.bfloat16)
    keys = turned_key.reshape(local_rows, model_width).astype(jnp.bfloat16)
    all_keys, all_values = (
        lax.all_gather(keys, "seq", axis=0, tiled=True),
        lax.all_gather(value_rows, "seq", axis=0, tiled=True),
    )
    length = all_keys.shape[0]
    allowed = positions[:, None] >= jnp.arange(length, dtype=jnp.int32)[None, :]
    query_g = split_heads(queries, local_rows)
    key_g = split_heads(all_keys, length)
    value_g = split_heads(all_values, length)
    attended_g, log_total = lax.map(
        lambda members: attend_forward(members[0], members[1], members[2], allowed),
        (query_g, key_g, value_g),
    )
    attended_low = merge_heads(attended_g, local_rows).astype(jnp.bfloat16)
    normed_b, back_norm_b = jax.vjp(
        norm_rows, rows_in, full_gtwo.astype(jnp.float32), full_stwo.astype(jnp.float32)
    )
    normed_b = normed_b.astype(jnp.bfloat16)
    hidden = jnp.dot(normed_b, full_wup, preferred_element_type=jnp.float32) + full_bup.astype(
        jnp.float32
    )
    activated, back_gelu = jax.vjp(gelu_exact, hidden)
    activated = activated.astype(jnp.bfloat16)
    branch_attn = jnp.dot(
        attended_low, full_wout, preferred_element_type=jnp.float32
    ) + full_bout.astype(jnp.float32)
    branch_mlp = jnp.dot(
        activated, full_wdown, preferred_element_type=jnp.float32
    ) + full_bdown.astype(jnp.float32)
    outputs = (rows_in + branch_attn + branch_mlp).astype(jnp.bfloat16)[None]
    matrices = (
        lax.all_gather(w_qkv, ("dp", "seq"), axis=0, tiled=True),
        lax.all_gather(w_out, ("dp", "seq"), axis=0, tiled=True),
        lax.all_gather(w_up, ("dp", "seq"), axis=0, tiled=True),
        lax.all_gather(w_down, ("dp", "seq"), axis=0, tiled=True),
    )
    back_qkv, back_wout, back_wup, back_wdown = matrices
    grad_rows = cotangent[0]
    grad_full = grad_rows.astype(jnp.float32)
    grad_bdown = jnp.sum(grad_full, axis=0)
    grad_active = against(grad_rows, back_wdown)
    grad_hidden = back_gelu(grad_active)[0].astype(jnp.bfloat16)
    grad_bup = jnp.sum(grad_hidden.astype(jnp.float32), axis=0)
    grad_normed_b = against(grad_hidden, back_wup)
    grad_x_b, grad_gtwo, grad_stwo = back_norm_b(grad_normed_b)
    grad_attended = against(grad_rows, back_wout).astype(jnp.bfloat16)
    grad_att_g = split_heads(grad_attended, local_rows)
    grad_query_g, grad_key_g, grad_value_g, inner_sum = lax.map(
        lambda members: attend_backward(
            members[0], members[1], members[2], members[3], members[4], allowed
        ),
        (query_g, key_g, value_g, grad_att_g, log_total),
    )
    key_part = merge_heads(grad_key_g, length)
    value_part = merge_heads(grad_value_g, length)
    grad_keys, grad_values = (
        lax.psum_scatter(key_part, "seq", scatter_dimension=0, tiled=True),
        lax.psum_scatter(value_part, "seq", scatter_dimension=0, tiled=True),
    )
    grad_raw_query, grad_raw_key = back_turn(
        (
            merge_heads(grad_query_g, local_rows).reshape(local_rows, H, HD),
            grad_keys.reshape(local_rows, H, HD),
        )
    )
    grad_proj = jnp.concatenate(
        [
            grad_raw_query.reshape(local_rows, model_width),
            grad_raw_key.reshape(local_rows, model_width),
            grad_values,
        ],
        axis=1,
    ).astype(jnp.bfloat16)
    grad_bqkv = jnp.sum(grad_proj.astype(jnp.float32), axis=0)
    grad_normed_a = against(grad_proj, back_qkv)
    grad_x_a, grad_gone, grad_sone = back_norm_a(grad_normed_a)
    grad_inputs = (grad_full + grad_x_a + grad_x_b).astype(jnp.bfloat16)[None]
    owned_width = lax.psum_scatter(
        jnp.concatenate(
            [
                cross_rows(normed_a, grad_proj),
                cross_rows(attended_low, grad_rows),
                cross_rows(normed_b, grad_hidden),
            ],
            axis=1,
        ),
        ("dp", "seq"),
        scatter_dimension=0,
        tiled=True,
    )
    owned_down = lax.psum_scatter(
        cross_rows(activated, grad_rows), ("dp", "seq"), scatter_dimension=0, tiled=True
    )
    own_wqkv = owned_width[:, : 3 * model_width]
    own_wout = owned_width[:, 3 * model_width : 4 * model_width]
    own_wup = owned_width[:, 4 * model_width :]
    small = (
        lax.psum_scatter(grad_bqkv, ("dp", "seq"), scatter_dimension=0, tiled=True),
        lax.psum_scatter(grad_bdown, ("dp", "seq"), scatter_dimension=0, tiled=True),
        lax.psum_scatter(grad_bup, ("dp", "seq"), scatter_dimension=0, tiled=True),
        lax.psum_scatter(grad_gone, ("dp", "seq"), scatter_dimension=0, tiled=True),
        lax.psum_scatter(grad_sone, ("dp", "seq"), scatter_dimension=0, tiled=True),
        lax.psum_scatter(grad_gtwo, ("dp", "seq"), scatter_dimension=0, tiled=True),
        lax.psum_scatter(grad_stwo, ("dp", "seq"), scatter_dimension=0, tiled=True),
    )
    return (
        outputs,
        grad_inputs,
        own_wqkv,
        small[0],
        own_wout,
        small[1],
        own_wup,
        small[2],
        owned_down,
        small[1],
        small[3],
        small[4],
        small[5],
        small[6],
    )


def solution(mesh):
    in_specs = (
        P("dp", "seq", None),
        P("dp", "seq", None),
        P(("dp", "seq"), None),
        P(("dp", "seq")),
        P(("dp", "seq"), None),
        P(("dp", "seq")),
        P(("dp", "seq"), None),
        P(("dp", "seq")),
        P(("dp", "seq"), None),
        P(("dp", "seq")),
        P(("dp", "seq")),
        P(("dp", "seq")),
        P(("dp", "seq")),
        P(("dp", "seq")),
    )
    out_specs = (
        P("dp", "seq", None),
        P("dp", "seq", None),
        P(("dp", "seq"), None),
        P(("dp", "seq")),
        P(("dp", "seq"), None),
        P(("dp", "seq")),
        P(("dp", "seq"), None),
        P(("dp", "seq")),
        P(("dp", "seq"), None),
        P(("dp", "seq")),
        P(("dp", "seq")),
        P(("dp", "seq")),
        P(("dp", "seq")),
        P(("dp", "seq")),
    )
    return jax.shard_map(shards, mesh=mesh, in_specs=in_specs, out_specs=out_specs, check_vma=False)
```

profile of v0, /device:TPU:0, one launch (start us, length us, event | category | flops | bytes accessed | tf_op | source)
XLA Modules:
  0.0 595.6 jit_solution(6928824130854129474)
XLA Ops:
  14.8 42.3 %all-reduce.22 = (bf16[1536]{0:T(1024)(128)(2,1)S(1)}, bf16[512]{0:T(512)(128)(2,1)S(1)}, bf16[512]{0:T(512)(128)(2,1)S(1)}, bf16[512]{0:T(512)(128)(2,1)S(1)}, ...) all-reduce(bf16[1536]{0:T(1024)(128)(2,1)S(1)} %dynamic-update-slic, ...), channel_id=1, replica_groups=mesh['dp'=8,'seq'=4] {'dp','seq'}, use_global_device_ids=true, to_apply=%add.8 | all-reduce | flops 6656 | bytes 26624
  59.3 9.5 %all-gather.6.cloned.1.call-done = bf16[512,1536]{1,0:T(8,128)(2,1)} async-done(((bf16[16,1536]{1,0:T(8,128)(2,1)}), bf16[512,1536]{1,0:T(8,128)(2,1)}) %all-gather.6.cloned.1.call-update) | async-done | bytes 1572880 | tf_op jit(solution)/shard_map/all_gather | solution.py:122
  68.8 2.1 convolution_add_fusion
  74.5 41.1 %all_gather.52 = bf16[512,512]{1,0:T(8,128)(2,1)S(1)} all-gather(bf16[16,512]{1,0:T(8,128)(2,1)S(1)} %copy-done.13), channel_id=1, replica_groups=mesh['dp'=8,'seq'=4] {'dp','seq'}, dimensions={0}, use_global_device_ids=true | all-gather | bytes 540672 | tf_op jit(solution)/shard_map/all_gather | solution.py:124
  117.7 9.8 %while.30 = (s32[]{:T(128)}, bf16[2,256,4,64]{1,3,2,0:T(8,128)(2,1)S(1)}, f32[2,4,256,1]{2,1,3,0:T(4,128)S(1)}, bf16[2,1024,4,64]{1,3,2,0:T(8,128)(2,1)S(1)}, bf...) while((s32[]{:T(128)}, ...), condition=%wide.region_5.6_spmd.clone.clone, body=%wide.region_2.5_spmd.clone.sunk.clone | while | flops 281279488 | bytes 15109201 | solution.py:173
  117.9 2.0 fusion.164
  122.9 2.0 fusion.164
  128.2 18.9 %while.31 = (s32[]{:T(128)}, f32[2,256,4,64]{1,3,2,0:T(8,128)S(1)}, f32[2,1024,4,64]{1,3,2,0:T(8,128)}, f32[2,1024,4,64]{1,3,2,0:T(8,128)}, bf16[2,1024,4,64]{1,...) while((s32[]{:T(128)}, f32[2,256,4,64]{1,3,2,0:T(8,128)S(1)}, ...), condition=%wide.region_8.9_spmd.clone.clone, body=%wide.region_6.8_spmd.clone.sunk.clone | while | flops 687406080 | bytes 57968828 | solution.py:211
  135.4 2.3 fusion.178
  144.8 2.3 fusion.178
  148.2 19.6 %all-gather.12.cloned.1.call-done = bf16[512,2048]{1,0:T(8,128)(2,1)} async-done(((bf16[16,2048]{1,0:T(8,128)(2,1)}), bf16[512,2048]{1,0:T(8,128)(2,1)}) %all-gather.12.cloned.1.call-update) | async-done | bytes 2097168 | tf_op jit(solution)/shard_map/all_gather | solution.py:126
  167.7 8.2 %multiply_convert_fusion.1 = (bf16[256,2048]{1,0:T(8,128)(2,1)S(1)}, f32[256,2048]{1,0:T(8,128)}, f32[256,2048]{1,0:T(8,128)}) fusion(f32[2048]{0:T(1024)S(1)} %convert_element_type.122, bf16[512,2048]{1,0:T(8,128)(2,1)} %all-gather.12.cloned.1.call-done, bf16[1,256,512]{2,1,0:T(8,128)(2,1)S(1)} %copy-done.2, f32[512]{0:T(512)S(1)} %convert_element_type.120, ...), kind=kOutput, calls=%fused_computation.69 | convolution fusion | flops 572260352 | bytes 7616512 | tf_op jit(solution)/shard_map/dot_general | solution.py:182
  175.9 49.8 %all-gather.14.cloned.1.call-done = bf16[2048,512]{1,0:T(8,128)(2,1)} async-done(((bf16[64,512]{1,0:T(8,128)(2,1)}), bf16[2048,512]{1,0:T(8,128)(2,1)}) %all-gather.14.cloned.1.call-update) | async-done | bytes 2097168 | tf_op jit(solution)/shard_map/all_gather | solution.py:128
  225.7 4.1 convert_reduce_fusion
  229.9 2.8 fusion.101
  233.8 24.6 %reduce-scatter.5.cloned.1.call-done = f32[256,512]{0,1:T(8,128)} async-done(((f32[1024,512]{0,1:T(8,128)}), f32[256,512]{0,1:T(8,128)}) %reduce-scatter.5.cloned.1.call-update) | async-done | bytes 524304 | tf_op jit(solution)/shard_map/reduce_scatter | solution.py:220
  262.3 30.3 %reduce-scatter.7.cloned.1.call-done = f32[256,512]{0,1:T(8,128)} async-done(((f32[1024,512]{0,1:T(8,128)}), f32[256,512]{0,1:T(8,128)}) %reduce-scatter.7.cloned.1.call-update) | async-done | bytes 524304 | tf_op jit(solution)/shard_map/reduce_scatter | solution.py:221
  293.7 1.9 fusion.104
  296.0 3.5 pad_maximum_fusion
  299.6 2.7 fusion.90
  302.4 2.8 fusion.114
  309.8 42.6 %all-reduce.21 = (f32[1536]{0:T(1024)S(1)}, f32[512]{0:T(512)S(1)}, f32[2048]{0:T(1024)S(1)}, f32[512]{0:T(512)S(1)}, f32[512]{0:T(512)S(1)}, /*index=5*/f32[512]{0:T(512)S(1)}, f32[512]{0:T(512)S(1)}) all-reduce(f32[1536]{0:T(1024)S(1)} %convert_reduce_fusion.1, ...), channel_id=5, replica_groups=mesh['dp'=8,'seq'=4] {'dp','seq'}, use_global_device_ids=true, to_apply=%region_17.18.clone | all-reduce | flops 6144 | bytes 49152
  356.0 92.5 %reduce-scatter.9.cloned.1.call-done = f32[16,4096]{1,0:T(8,128)} async-done(((f32[512,4096]{1,0:T(8,128)}), f32[16,4096]{1,0:T(8,128)}) %reduce-scatter.9.cloned.1.call-update) | async-done | bytes 262160 | tf_op jit(solution)/shard_map/reduce_scatter | solution.py:241
  452.9 135.7 %reduce-scatter.11.cloned.1.call-done = f32[64,512]{1,0:T(8,128)} async-done(((f32[2048,512]{1,0:T(8,128)}), f32[64,512]{1,0:T(8,128)}) %reduce-scatter.11.cloned.1.call-update) | async-done | bytes 131088 | tf_op jit(solution)/shard_map/reduce_scatter | solution.py:254
  (158 shorter events, 56.4 us)
Async XLA Ops:
  7.2 61.6 %all-gather.6.cloned.1.call-start = ((), (), s32[]{:S(2)}) async-start(), calls=%async_computation.4 | async-start | bytes 1622016 | tf_op jit(solution)/shard_map/all_gather | solution.py:122
  7.9 108.3 %all-gather.8.cloned.1.call-start = ((), (), s32[]{:S(2)}) async-start(), calls=%async_computation.5 | async-start | bytes 1310720 | tf_op jit(solution)/shard_map/all_gather | solution.py:166
  71.7 46.0 %all-gather.10.cloned.1.call-start = ((), (), s32[]{:S(2)}) async-start(), calls=%async_computation.6 | async-start | bytes 1310720 | tf_op jit(solution)/shard_map/all_gather | solution.py:165
  72.0 2.5 copy-start.13
  72.0 43.6 %copy-start.3 = (bf16[1,256,512]{2,1,0:T(8,128)(2,1)S(1)}, bf16[1,256,512]{2,1,0:T(8,128)(2,1)}, u32[]{:S(2)}) copy-start(bf16[1,256,512]{2,1,0:T(8,128)(2,1)} %param.19) | copy-start | bytes 786436
  73.2 94.5 %all-gather.12.cloned.1.call-start = ((), (), s32[]{:S(2)}) async-start(), calls=%async_computation.7 | async-start | bytes 2162688 | tf_op jit(solution)/shard_map/all_gather | solution.py:126
  73.8 151.9 %all-gather.14.cloned.1.call-start = ((), (), s32[]{:S(2)}) async-start(), calls=%async_computation.8 | async-start | bytes 2162688 | tf_op jit(solution)/shard_map/all_gather | solution.py:128
  74.4 184.0 %reduce-scatter.5.cloned.1.call-start = ((), (), s32[]{:S(2)}) async-start(), calls=%async_computation.9 | async-start | bytes 2621440 | tf_op jit(solution)/shard_map/reduce_scatter | solution.py:220
  132.0 1.6 copy-start.9
  141.4 1.6 copy-start.9
  147.1 85.6 %copy-start.12 = (f32[2,256,4,64]{1,3,2,0:T(8,128)}, f32[2,256,4,64]{1,3,2,0:T(8,128)S(1)}, u32[]{:S(2)}) copy-start(f32[2,256,4,64]{1,3,2,0:T(8,128)S(1)} %get-tuple-element.108) | copy-start | bytes 1572868
  147.1 20.6 %copy-start.2 = (bf16[1,256,512]{2,1,0:T(8,128)(2,1)S(1)}, bf16[1,256,512]{2,1,0:T(8,128)(2,1)}, u32[]{:S(2)}) copy-start(bf16[1,256,512]{2,1,0:T(8,128)(2,1)} %param.18) | copy-start | bytes 786436
  147.1 145.5 %reduce-scatter.7.cloned.1.call-start = ((), (), s32[]{:S(2)}) async-start(), calls=%async_computation.10 | async-start | bytes 2621440 | tf_op jit(solution)/shard_map/reduce_scatter | solution.py:221
  147.9 300.6 %reduce-scatter.9.cloned.1.call-start = ((), (), s32[]{:S(2)}) async-start(), calls=%async_computation.11 | async-start | bytes 8650752 | tf_op jit(solution)/shard_map/reduce_scatter | solution.py:241
  229.9 2.8 copy-start.11
  229.9 3.6 copy-start.7
  293.7 2.3 copy-start.1
  299.5 289.1 %reduce-scatter.11.cloned.1.call-start = ((), (), s32[]{:S(2)}) async-start(), calls=%async_computation.12 | async-start | bytes 4325376 | tf_op jit(solution)/shard_map/reduce_scatter | solution.py:254
  302.3 2.9 copy-start.8
  302.4 3.2 copy-start.14
  305.5 1.5 copy-start.4
  305.6 1.5 copy-start.5
  305.6 1.7 copy-start.15
  352.5 236.6 %copy-start.16 = (f32[16]{0:T(128)}, f32[16]{0:T(128)S(1)}, u32[]{:S(2)}) copy-start(f32[16]{0:T(128)S(1)} %dynamic-slice.1) | copy-start | bytes 196
  (5 other events, 6.0 us)
Sparse Core Ops, SparseCore 0:
  10.9 57.8 all-gather.5
  71.8 16.6 all-gather.7
  90.6 18.2 all-gather.9
  111.6 56.0 all-gather.11
  170.5 55.2 all-gather.13
  228.1 30.2 reduce-scatter.4
  261.1 31.4 reduce-scatter.6
  299.7 148.7 reduce-scatter.8
  451.3 137.2 reduce-scatter.10
where the time goes:
time: 597 us; the launch traced here: 596 us
  waiting for transfers between devices  364 us (61%)
  blocking collectives  126 us (21%)
  matrix products  48.7 us (8%)
  local copies, waits for them, and re-layouts  22.9 us (4%)
  other arithmetic  18.4 us (3%)
  between operations  14.3 us (2%)
    reduce_scatter x1, waiting for transfers between devices, shards(): lax.psum_scatter(cross_rows(activated, grad_rows), ('dp', 'seq'), scatter...  136 us
    reduce_scatter x1, waiting for transfers between devices, shards(): lax.psum_scatter(jnp.concatenate([cross_rows(normed_a, grad_proj), cross_...  92.5 us
    unnamed x2, blocking collectives  84.9 us
    all_gather x1, waiting for transfers between devices, shards(): lax.all_gather(w_down, ('dp', 'seq'), axis=0, tiled=True)  49.8 us
    all_gather x1, blocking collectives, shards(): lax.all_gather(w_out, ('dp', 'seq'), axis=0, tiled=True)  41.1 us
    reduce_scatter x1, waiting for transfers between devices, shards(): lax.psum_scatter(value_part, 'seq', scatter_dimension=0, tiled=True)  30.3 us
    reduce_scatter x1, waiting for transfers between devices, shards(): lax.psum_scatter(key_part, 'seq', scatter_dimension=0, tiled=True)  24.6 us
    all_gather x1, waiting for transfers between devices, shards(): lax.all_gather(w_up, ('dp', 'seq'), axis=0, tiled=True)  19.6 us
  transfers between devices with their start and end apart: 9, of which 7 were waited for; matrix products, arithmetic and copies ran while one was open for 13% of the time, Pallas kernels for 0%

commit v1 on v0

v1 whole, which is shorter than its diff:
```python
import functools
import math

import jax
import jax.numpy as jnp
import numpy as np
from jax import lax
from jax.experimental import pallas as pl
from jax.experimental.pallas import tpu as pltpu
from jax.sharding import PartitionSpec as P

HD = 64
ROT = 16
EPS = 1e-05
BLOCK = 256
F32 = jnp.float32
BF16 = jnp.bfloat16
PARAMS = pltpu.CompilerParams(vmem_limit_bytes=48 * 1024 * 1024)


def log2(count):
    assert count & (count - 1) == 0
    return count.bit_length() - 1


def exchange(value, axis, size, bit):
    return lax.ppermute(value, axis, [(i, i ^ (1 << bit)) for i in range(size)])


def flag_of(axis, bit):
    return (lax.axis_index(axis) >> bit) & 1 == 1


def gather_bits(value, axis, size):
    shape = value.shape
    for done, bit in enumerate(reversed(range(log2(size)))):
        other = exchange(value, axis, size, bit)
        upper = flag_of(axis, bit)
        value = jnp.where(
            upper,
            jnp.stack([other, value], done),
            jnp.stack([value, other], done),
        )
    return value.reshape((size,) + shape)


def swap_bits(blocks, axis, size):
    count = log2(size)
    rest = blocks.shape[1:]
    value = blocks.reshape((2,) * count + rest)
    for bit in range(count):
        place = count - 1 - bit
        low = lax.index_in_dim(value, 0, place, keepdims=False)
        high = lax.index_in_dim(value, 1, place, keepdims=False)
        upper = flag_of(axis, bit)
        other = exchange(jnp.where(upper, low, high), axis, size, bit)
        value = jnp.stack([jnp.where(upper, other, low), jnp.where(upper, high, other)], place)
    return value.reshape((size,) + rest)


def scatter_bits(blocks, axis, size):
    count = log2(size)
    rest = blocks.shape[1:]
    value = blocks.reshape((2,) * count + rest)
    for bit in range(count):
        place = count - 1 - bit
        low = lax.index_in_dim(value, 0, place, keepdims=False)
        high = lax.index_in_dim(value, 1, place, keepdims=False)
        upper = flag_of(axis, bit)
        sent = jnp.where(upper, low, high).astype(BF16)
        value = jnp.where(upper, high, low).astype(F32) + exchange(sent, axis, size, bit).astype(F32)
    return value


def dot(left, right):
    return lax.dot_general(left, right, (((1,), (0,)), ((), ())), preferred_element_type=F32)


def dot_rows(left, right):
    return lax.dot_general(left, right, (((0,), (0,)), ((), ())), preferred_element_type=F32)


def dot_last(left, right):
    return lax.dot_general(left, right, (((1,), (1,)), ((), ())), preferred_element_type=F32)


def standardize(rows):
    average = jnp.mean(rows, axis=-1, keepdims=True)
    centered = rows - average
    variance = jnp.mean(centered * centered, axis=-1, keepdims=True)
    scale = lax.rsqrt(variance + EPS)
    return centered * scale, scale


def norm_back(normal, scale, gain, upstream):
    inner = gain * upstream
    first = jnp.mean(inner, axis=-1, keepdims=True)
    second = jnp.mean(inner * normal, axis=-1, keepdims=True)
    return scale * (inner - first - normal * second)


def attention_kernel(
    xg_ref, wq_ref, wo_ref, vec_ref, bias_ref, cos_ref, sin_ref,
    out_ref, dx_ref, grad_ref,
    na_ref, q_ref, k_ref, v_ref, da_ref, qt_ref, dat_ref, att_ref, dq_ref, dkt_ref, dvt_ref, dp_ref,
):
    tokens = xg_ref.shape[0]
    width = xg_ref.shape[1] // 2
    part = wo_ref.shape[0]
    heads = part // HD
    owners, _, _ = grad_ref.shape
    own_rows = width // owners
    out_rows = part // owners
    gain = vec_ref[0:1, :]
    shift = vec_ref[1:2, :]
    lane = lax.broadcasted_iota(jnp.int32, (BLOCK, part), 1)
    turn = lane % HD < ROT // 2

    def partner(value):
        return jnp.where(
            turn, pltpu.roll(value, part - ROT // 2, 1), pltpu.roll(value, ROT // 2, 1)
        )

    for block in range(tokens // BLOCK):
        rows = pl.ds(block * BLOCK, BLOCK)
        normal, _ = standardize(xg_ref[rows, :width].astype(F32))
        normed = (normal * gain + shift).astype(BF16)
        na_ref[rows, :] = normed
        projected = dot(normed, wq_ref[...]) + bias_ref[...]
        cosine, sine = cos_ref[rows, :], sin_ref[rows, :]
        query = projected[:, :part]
        query = query * cosine + partner(query) * sine
        key = projected[:, part : 2 * part]
        key = key * cosine + partner(key) * sine
        query = query.astype(BF16).astype(F32) * HD**-0.5
        q_ref[rows, :] = query.astype(BF16)
        qt_ref[:, rows] = query.T.astype(BF16)
        k_ref[rows, :] = key.astype(BF16)
        v_ref[rows, :] = projected[:, 2 * part :].astype(BF16)
        grad_att = dot_last(xg_ref[rows, width:], wo_ref[...]).astype(BF16)
        da_ref[rows, :] = grad_att
        dat_ref[:, rows] = grad_att.astype(F32).T.astype(BF16)

    dkt_ref[...] = jnp.zeros_like(dkt_ref)
    dvt_ref[...] = jnp.zeros_like(dvt_ref)
    below = lax.broadcasted_iota(jnp.int32, (BLOCK, BLOCK), 0) >= lax.broadcasted_iota(
        jnp.int32, (BLOCK, BLOCK), 1
    )
    zero = jnp.zeros((), BF16)
    for block in range(tokens // BLOCK):
        rows = pl.ds(block * BLOCK, BLOCK)
        seen = (block + 1) * BLOCK
        attended = jnp.zeros((BLOCK, part), F32)
        grad_query = jnp.zeros((BLOCK, part), F32)
        for head in range(heads):
            mine = lane // HD == head
            mine_t = lax.broadcasted_iota(jnp.int32, (part, BLOCK), 0) // HD == head
            query = jnp.where(mine, q_ref[rows, :], zero)
            grad_att = jnp.where(mine, da_ref[rows, :], zero)
            scores = dot_last(query, k_ref[:seen, :])
            last = jnp.where(below, scores[:, seen - BLOCK :], -1e30)
            scores = last if block == 0 else jnp.concatenate([scores[:, : seen - BLOCK], last], 1)
            raised = jnp.exp(scores - jnp.max(scores, axis=-1, keepdims=True))
            probs = raised * (1.0 / jnp.sum(raised, axis=-1, keepdims=True))
            probs_low = probs.astype(BF16)
            attended = jnp.where(mine, dot(probs_low, v_ref[:seen, :]), attended)
            grad_probs = dot_last(grad_att, v_ref[:seen, :])
            inner = jnp.sum(probs * grad_probs, axis=-1, keepdims=True)
            grad_scores = (probs * (grad_probs - inner)).astype(BF16)
            grad_query = jnp.where(mine, dot(grad_scores, k_ref[:seen, :]), grad_query)
            query_t = jnp.where(mine_t, qt_ref[:, rows], zero)
            grad_att_t = jnp.where(mine_t, dat_ref[:, rows], zero)
            dkt_ref[:, :seen] += dot(query_t, grad_scores)
            dvt_ref[:, :seen] += dot(grad_att_t, probs_low)
        att_ref[rows, :] = attended.astype(BF16)
        dq_ref[rows, :] = grad_query * HD**-0.5

    vectors = [jnp.zeros((1, width), F32) for _ in range(3)]
    grad_bias = jnp.zeros((1, 3 * part), F32)
    for block in range(tokens // BLOCK):
        rows = pl.ds(block * BLOCK, BLOCK)
        cosine, sine = cos_ref[rows, :], sin_ref[rows, :]
        grad_query = dq_ref[rows, :]
        grad_query = grad_query * cosine - partner(grad_query) * sine
        grad_key = dkt_ref[:, rows].T
        grad_key = grad_key * cosine - partner(grad_key) * sine
        grad_value = dvt_ref[:, rows].T
        grad_proj = jnp.concatenate([grad_query, grad_key, grad_value], 1).astype(BF16)
        dp_ref[rows, :] = grad_proj
        grad_bias += jnp.sum(grad_proj.astype(F32), axis=0, keepdims=True)
        out_ref[rows, :] = dot(att_ref[rows, :], wo_ref[...])
        upstream = dot_last(grad_proj, wq_ref[...])
        normal, scale = standardize(xg_ref[rows, :width].astype(F32))
        vectors[0] += jnp.sum(normal * upstream, axis=0, keepdims=True)
        vectors[1] += jnp.sum(upstream, axis=0, keepdims=True)
        vectors[2] += jnp.sum(xg_ref[rows, width:].astype(F32), axis=0, keepdims=True)
        dx_ref[rows, :] = norm_back(normal, scale, gain, upstream)

    grad_qkv = dot_rows(na_ref[...], dp_ref[...])
    grad_out = dot_rows(att_ref[...], xg_ref[:, width:])
    rest = grad_ref.shape[1] - own_rows - out_rows
    tail = jnp.concatenate(
        [jnp.concatenate([grad_bias, jnp.zeros((1, width - 3 * part), F32)], 1)]
        + vectors
        + [jnp.zeros((rest - 4, width), F32)],
        0,
    )
    for owner in range(owners):
        grad_ref[owner, :own_rows, : 3 * part] = grad_qkv[owner * own_rows : (owner + 1) * own_rows, :]
        grad_ref[owner, :own_rows, 3 * part :] = jnp.zeros((own_rows, width - 3 * part), F32)
        grad_ref[owner, own_rows : own_rows + out_rows, :] = grad_out[
            owner * out_rows : (owner + 1) * out_rows, :
        ]
        grad_ref[owner, own_rows + out_rows :, :] = tail


def mlp_kernel(
    xg_ref, up_ref, down_ref, vec_ref, bias_ref, out_part_ref, dx_part_ref,
    out_ref, dx_ref, grad_ref,
    nb_ref, act_ref, dh_ref,
):
    tokens = xg_ref.shape[0]
    width = xg_ref.shape[1] // 2
    hidden_width = up_ref.shape[1]
    owners = grad_ref.shape[0]
    up_rows = width // owners
    down_rows = hidden_width // owners
    gain = vec_ref[2:3, :]
    shift = vec_ref[3:4, :]
    vectors = [jnp.zeros((1, width), F32) for _ in range(2)]
    grad_bias = jnp.zeros((1, hidden_width), F32)
    for block in range(tokens // BLOCK):
        rows = pl.ds(block * BLOCK, BLOCK)
        grad_rows = xg_ref[rows, width:]
        normal, scale = standardize(xg_ref[rows, :width].astype(F32))
        normed = (normal * gain + shift).astype(BF16)
        nb_ref[rows, :] = normed
        hidden = dot(normed, up_ref[...]) + bias_ref[...]
        half = 0.5 * (1.0 + lax.erf(hidden * math.sqrt(0.5)))
        active = (hidden * half).astype(BF16)
        act_ref[rows, :] = active
        slope = half + hidden * jnp.exp(-0.5 * hidden * hidden) * (1.0 / math.sqrt(2.0 * math.pi))
        grad_hidden = (dot_last(grad_rows, down_ref[...]) * slope).astype(BF16)
        dh_ref[rows, :] = grad_hidden
        grad_bias += jnp.sum(grad_hidden.astype(F32), axis=0, keepdims=True)
        out_ref[rows, :] = (out_part_ref[rows, :] + dot(active, down_ref[...])).astype(out_ref.dtype)
        upstream = dot_last(grad_hidden, up_ref[...])
        vectors[0] += jnp.sum(normal * upstream, axis=0, keepdims=True)
        vectors[1] += jnp.sum(upstream, axis=0, keepdims=True)
        dx_ref[rows, :] = (dx_part_ref[rows, :] + norm_back(normal, scale, gain, upstream)).astype(dx_ref.dtype)
    grad_up = dot_rows(nb_ref[...], dh_ref[...])
    grad_down = dot_rows(act_ref[...], xg_ref[:, width:])
    rest = grad_ref.shape[1] - up_rows - down_rows
    tail = jnp.concatenate([grad_bias] + vectors + [jnp.zeros((rest - 3, width), F32)], 0)
    for owner in range(owners):
        grad_ref[owner, :up_rows, :] = grad_up[owner * up_rows : (owner + 1) * up_rows, :]
        grad_ref[owner, up_rows : up_rows + down_rows, :] = grad_down[
            owner * down_rows : (owner + 1) * down_rows, :
        ]
        grad_ref[owner, up_rows + down_rows :, :] = tail


def whole(count):
    return [pl.BlockSpec(memory_space=pltpu.VMEM)] * count


def attention(xg, w_qkv, w_out, vectors, bias, cosine, sine, owners):
    tokens, width = xg.shape[0], xg.shape[1] // 2
    part = w_out.shape[0]
    rows = width // owners + part // owners + 16
    shape = jax.ShapeDtypeStruct
    flops = 2 * tokens * width * part * 12 + 2 * 5 * tokens * tokens * part
    return pl.pallas_call(
        attention_kernel,
        out_shape=(
            shape((tokens, width), F32),
            shape((tokens, width), F32),
            shape((owners, rows, width), F32),
        ),
        in_specs=whole(7),
        out_specs=tuple(whole(3)),
        scratch_shapes=[
            pltpu.VMEM((tokens, width), BF16),
            pltpu.VMEM((tokens, part), BF16),
            pltpu.VMEM((tokens, part), BF16),
            pltpu.VMEM((tokens, part), BF16),
            pltpu.VMEM((tokens, part), BF16),
            pltpu.VMEM((part, tokens), BF16),
            pltpu.VMEM((part, tokens), BF16),
            pltpu.VMEM((tokens, part), BF16),
            pltpu.VMEM((tokens, part), F32),
            pltpu.VMEM((part, tokens), F32),
            pltpu.VMEM((part, tokens), F32),
            pltpu.VMEM((tokens, 3 * part), BF16),
        ],
        compiler_params=PARAMS,
        cost_estimate=pl.CostEstimate(
            flops=4 * flops, bytes_accessed=8 * tokens * width * 4, transcendentals=tokens * tokens * 2
        ),
    )(xg, w_qkv, w_out, vectors, bias, cosine, sine)


def feed_forward(xg, w_up, w_down, vectors, bias, out_part, dx_part, owners):
    tokens, width = xg.shape[0], xg.shape[1] // 2
    hidden_width = w_up.shape[1]
    rows = width // owners + hidden_width // owners + 16
    shape = jax.ShapeDtypeStruct
    return pl.pallas_call(
        mlp_kernel,
        out_shape=(
            shape((tokens, width), F32),
            shape((tokens, width), F32),
            shape((owners, rows, width), F32),
        ),
        in_specs=whole(7),
        out_specs=tuple(whole(3)),
        scratch_shapes=[
            pltpu.VMEM((tokens, width), BF16),
            pltpu.VMEM((tokens, hidden_width), BF16),
            pltpu.VMEM((tokens, hidden_width), BF16),
        ],
        compiler_params=PARAMS,
        cost_estimate=pl.CostEstimate(
            flops=12 * tokens * width * hidden_width,
            bytes_accessed=8 * tokens * width * 4,
            transcendentals=2 * tokens * hidden_width,
        ),
    )(xg, w_up, w_down, vectors, bias, out_part, dx_part)


def rotary(tokens, heads):
    ladder = np.arange(ROT // 2, dtype=np.float32)
    frequency = np.exp(ladder * np.float32(-2.0 * math.log(10000.0) / ROT)).astype(np.float32)
    angles = np.arange(tokens, dtype=np.float32)[:, None] * frequency[None, :]
    cosine = np.ones((tokens, HD), np.float32)
    sine = np.zeros((tokens, HD), np.float32)
    half = ROT // 2
    cosine[:, :half] = cosine[:, half:ROT] = np.cos(angles)
    sine[:, half:ROT] = np.sin(angles)
    sine[:, :half] = -sine[:, half:ROT]
    return np.tile(cosine, (1, heads)), np.tile(sine, (1, heads))


def shards(
    owners, groups,
    inputs, cotangent, w_qkv, b_qkv, w_out, b_out, w_up, b_up, w_down, b_down,
    gain_one, shift_one, gain_two, shift_two,
):
    rows, width = w_qkv.shape[0], w_qkv.shape[1] // 3
    hidden = w_up.shape[1]
    down_rows = w_down.shape[0]
    local = inputs.shape[1]
    tokens = local * groups
    part = width // groups
    slice_width = hidden // groups
    dp_rows = rows * groups
    group = lax.axis_index("seq")
    owner = lax.axis_index("dp")

    xg = jnp.concatenate([inputs[0], cotangent[0]], axis=1)
    xg = gather_bits(xg, "seq", groups).reshape(tokens, 2 * width)

    devices = owners * groups
    place = [(f % owners) * groups + f // owners for f in range(devices)]
    out_rows = lax.ppermute(w_out, ("dp", "seq"), [(f, place[f]) for f in range(devices)])

    small = jnp.concatenate(
        [b_qkv.reshape(rows, -1), b_up.reshape(rows, -1)]
        + [v[:, None] for v in (b_out, b_down, gain_one, shift_one, gain_two, shift_two)],
        axis=1,
    )
    n_small = small.shape[1]
    n_up = b_up.shape[0] // rows
    small = jnp.pad(small, ((0, 0), (0, width - 3 * part - n_small)))
    blocks = jnp.concatenate(
        [
            w_qkv.reshape(rows, 3, groups, part).transpose(2, 0, 1, 3).reshape(groups, rows, 3 * part),
            jnp.broadcast_to(small[None], (groups,) + small.shape),
            w_up.reshape(rows, owners, groups, -1).transpose(2, 0, 1, 3).reshape(groups, rows, slice_width),
        ],
        axis=2,
    )
    blocks = swap_bits(blocks, "seq", groups).reshape(dp_rows, width + slice_width)
    first = gather_bits(jnp.concatenate([blocks[:, :width], out_rows], axis=0), "dp", owners)
    second = gather_bits(jnp.concatenate([blocks[:, width:], w_down], axis=0), "dp", owners)

    full_qkv = first[:, :dp_rows, : 3 * part].reshape(width, 3 * part)
    full_out = first[:, dp_rows:, :].reshape(part, width)
    small = first[:, :dp_rows, 3 * part : 3 * part + n_small].reshape(width, n_small).astype(F32)
    bias_qkv = lax.dynamic_index_in_dim(
        small[:, :3].reshape(3, groups, part), group, 1, keepdims=False
    ).reshape(1, 3 * part)
    bias_up = lax.dynamic_index_in_dim(
        small[:, 3 : 3 + n_up].reshape(owners, groups, -1), group, 1, keepdims=False
    ).reshape(1, slice_width)
    vectors = small[:, 3 + n_up :].T
    biases = vectors[0] + vectors[1]
    vectors = jnp.concatenate([vectors[2:], jnp.zeros((4, width), F32)], 0)
    full_up = second[:, :dp_rows, :].reshape(width, slice_width)
    full_down = second[:, dp_rows:, :].reshape(slice_width, width)

    cosine, sine = rotary(tokens, part // HD)
    out_part, dx_part, grad_a = attention(
        xg, full_qkv, full_out, vectors, bias_qkv, jnp.asarray(cosine), jnp.asarray(sine), owners
    )
    out_part, dx_part, grad_b = feed_forward(
        xg, full_up, full_down, vectors, bias_up, out_part, dx_part, owners
    )

    grad_a = scatter_bits(grad_a, "dp", owners)
    grad_b = scatter_bits(grad_b, "dp", owners)
    both = jnp.concatenate([out_part, dx_part], axis=1).reshape(groups, local, 2 * width)
    both = scatter_bits(both, "seq", groups)
    outputs = (inputs[0].astype(F32) + both[:, :width] + biases[None]).astype(BF16)[None]
    grad_inputs = (cotangent[0].astype(F32) + both[:, width:]).astype(BF16)[None]

    own_wout = lax.ppermute(
        grad_a[dp_rows : dp_rows + rows, :], ("dp", "seq"), [(place[f], f) for f in range(devices)]
    )
    tail_a = grad_a[dp_rows + rows :, :]
    tail_b = grad_b[dp_rows + down_rows :, :]
    small = jnp.concatenate([tail_a[:4], tail_b[1:3], jnp.zeros((2, width), F32)], 0)
    send = jnp.concatenate(
        [
            grad_a[:dp_rows, : 3 * part].reshape(groups, rows, 3 * part),
            grad_b[:dp_rows, :].reshape(groups, rows, slice_width),
        ],
        axis=2,
    )
    small = jnp.pad(small, ((0, 0), (0, send.shape[2] - width)))
    send = jnp.concatenate([send, jnp.broadcast_to(small[None], (groups,) + small.shape)], axis=1)
    send = swap_bits(send, "seq", groups)
    own_wqkv = send[:, :rows, : 3 * part].reshape(groups, rows, 3, part).transpose(1, 2, 0, 3).reshape(rows, -1)
    own_wup = (
        send[:, :rows, 3 * part :].reshape(groups, rows, owners, -1).transpose(1, 2, 0, 3).reshape(rows, -1)
    )
    small = send[:, rows:, :width]
    index = owner * groups + group
    own_bqkv = lax.dynamic_slice_in_dim(
        small[:, 0, : 3 * part].reshape(groups, 3, part).transpose(1, 0, 2).reshape(-1),
        index * b_qkv.shape[0],
        b_qkv.shape[0],
    )
    sums = jnp.sum(small, axis=0)
    own = lax.dynamic_slice_in_dim(sums, index * rows, rows, axis=1)
    own_bias = lax.dynamic_slice_in_dim(small[0, 3], index * rows, rows)
    own_bup = lax.dynamic_slice_in_dim(tail_b[0], owner * b_up.shape[0], b_up.shape[0])
    return (
        outputs,
        grad_inputs,
        own_wqkv,
        own_bqkv,
        own_wout,
        own_bias,
        own_wup,
        own_bup,
        grad_b[dp_rows : dp_rows + down_rows, :],
        own_bias,
        own[1],
        own[2],
        own[4],
        own[5],
    )


def solution(mesh):
    rows = P("dp", "seq", None)
    matrix, vector = P(("dp", "seq"), None), P(("dp", "seq"))
    weights = (matrix, vector) * 4
    return jax.shard_map(
        functools.partial(shards, mesh.shape["dp"], mesh.shape["seq"]),
        mesh=mesh,
        in_specs=(rows, rows) + weights + (vector,) * 4,
        out_specs=(rows, rows) + weights + (vector,) * 4,
        check_vma=False,
    )
```

time: 597 us -> 142 us (0.24)
  waiting for transfers between devices: 364 us -> 57.3 us
  blocking collectives: 126 us -> 0 us
  matrix products: 48.7 us -> 0 us
  starting transfers between devices: 0.58 us -> 29 us
  Pallas kernels: 0 us -> 24.1 us
  between operations: 14.3 us -> 1.34 us
  other arithmetic: 18.4 us -> 10.4 us
    reduce_scatter x4 -> x0, waiting for transfers between devices: 283 us -> none  [the longest x1 136 us: shards(): lax.psum_scatter(cross_rows(activated, grad_rows), ('dp', 'seq'), scatter...]
    unnamed x2 -> x0, blocking collectives: 84.9 us -> none
    all_gather x5 -> x0, waiting for transfers between devices: 78.9 us -> none  [the longest x1 49.8 us: shards(): lax.all_gather(w_down, ('dp', 'seq'), axis=0, tiled=True)]
    ppermute x0 -> x22, waiting for transfers between devices: none -> 57.3 us  [the longest x20 57.3 us: exchange(): return lax.ppermute(value, axis, [(i, i ^ 1 << bit) for i in range(size)])]
    dot_general x26 -> x0, matrix products: 48.7 us -> none  [the longest x1 8.18 us: shards(): jnp.dot(normed_b, full_wup, preferred_element_type=jnp.float32)]
    all_gather x1 -> x0, blocking collectives: 41.1 us -> none  [shards(): lax.all_gather(w_out, ('dp', 'seq'), axis=0, tiled=True)]
    ppermute x0 -> x22, starting transfers between devices: none -> 29 us  [the longest x20 27 us: exchange(): return lax.ppermute(value, axis, [(i, i ^ 1 << bit) for i in range(size)])]
    pallas_call x0 -> x2, Pallas kernels: none -> 24.1 us  [the longest x1 14.5 us: attention(): pl.pallas_call(attention_kernel, out_shape=(shape((tokens, width), F32),...]
  transfers between devices with their start and end apart: 9 -> 22, of which waited for: 7 -> 14; matrix products, arithmetic and copies ran while one was open for 13% -> 11% of each run, Pallas kernels for 0% -> 7%
where the time goes in v1:
time: 142 us
  waiting for transfers between devices  57.3 us (40%)
  starting transfers between devices  29 us (20%)
  Pallas kernels  24.1 us (17%)
  local copies, waits for them, and re-layouts  19.5 us (14%)
  other arithmetic  10.4 us (7%)
    ppermute x20, waiting for transfers between devices, exchange(): return lax.ppermute(value, axis, [(i, i ^ 1 << bit) for i in range(size)])  57.3 us
    ppermute x20, starting transfers between devices, exchange(): return lax.ppermute(value, axis, [(i, i ^ 1 << bit) for i in range(size)])  27 us
    pallas_call x1, Pallas kernels, attention(): pl.pallas_call(attention_kernel, out_shape=(shape((tokens, width), F32),...  14.5 us
    pallas_call x1, Pallas kernels, feed_forward(): pl.pallas_call(mlp_kernel, out_shape=(shape((tokens, width), F32), shape(...  9.64 us
    broadcast_in_dim x6, local copies, waits for them, and re-layouts, shards(): v[:, None]  4.47 us
    select_n x13, other arithmetic, gather_bits(): jnp.where(upper, jnp.stack([other, value], done), jnp.stack([value, other...  4.27 us
  transfers between devices with their start and end apart: 22, of which 14 were waited for; matrix products, arithmetic and copies ran while one was open for 11% of the time, Pallas kernels for 7%

profile of v1, /device:TPU:0, one launch (start us, length us, event | category | flops | bytes accessed | tf_op | source)
XLA Modules:
  0.0 141.6 jit_solution(16827784270054969901)
XLA Ops:
  10.9 4.7 %collective-permute-start.3 = (bf16[2,16,1024]{2,1,0:T(8,128)(2,1)S(1)}, bf16[2,16,1024]{2,1,0:T(8,128)(2,1)S(1)}, u32[]{:S(2)}, u32[]{:S(2)}) collective-permute-start(bf16[2,16,1024]{2,1,0:T(8,128)(2,1)S(1)} %broadcast_select_fusion.2), channel_id=1, source_target_pairs={{0,2},{1,3},{2,0},{3,1},{4,6},{5,7},{6,4},{7,5},{8,10},{9,11},{10,... | collective-permute-start | bytes 196616 | tf_op jit(solution)/shard_map/ppermute | solution.py:27
  15.9 2.3 %collective-permute-done.3 = bf16[2,16,1024]{2,1,0:T(8,128)(2,1)S(1)} collective-permute-done((bf16[2,16,1024]{2,1,0:T(8,128)(2,1)S(1)}, bf16[2,16,1024]{2,1,0:T(8,128)(2,1)S(1)}, u32[]{:S(2)}, u32[]{:S(2)}) %collective-permute-start.3) | collective-permute-done | bytes 65568 | tf_op jit(solution)/shard_map/ppermute | solution.py:27
  18.4 3.1 %collective-permute-start.8 = (bf16[80,512]{1,0:T(8,128)(2,1)S(1)}, bf16[80,512]{1,0:T(8,128)(2,1)S(1)}, u32[]{:S(2)}, u32[]{:S(2)}) collective-permute-start(bf16[80,512]{1,0:T(8,128)(2,1)S(1)} %get-tuple-element.56), channel_id=1, source_target_pairs={{0,16},{4,20},{8,24},{12,28},{16,0},{20,4},{24,8},{28,12},{1,17},{... | collective-permute-start | bytes 245768 | tf_op jit(solution)/shard_map/ppermute | solution.py:27
  21.6 3.7 %collective-permute-done.8 = bf16[80,512]{1,0:T(8,128)(2,1)S(1)} collective-permute-done((bf16[80,512]{1,0:T(8,128)(2,1)S(1)}, bf16[80,512]{1,0:T(8,128)(2,1)S(1)}, u32[]{:S(2)}, u32[]{:S(2)}) %collective-permute-start.8) | collective-permute-done | bytes 81952 | tf_op jit(solution)/shard_map/ppermute | solution.py:27
  25.4 4.4 %collective-permute-start.9 = (bf16[2,80,512]{2,1,0:T(8,128)(2,1)S(1)}, bf16[2,80,512]{2,1,0:T(8,128)(2,1)S(1)}, u32[]{:S(2)}, u32[]{:S(2)}) collective-permute-start(bf16[2,80,512]{2,1,0:T(8,128)(2,1)S(1)} %maximum_select_fusion.10), channel_id=1, source_target_pairs={{0,8},{4,12},{8,0},{12,4},{16,24},{20,28},{24,16},{28,20},{1,9},{5... | collective-permute-start | bytes 491528 | tf_op jit(solution)/shard_map/ppermute | solution.py:27
  29.9 2.0 %collective-permute-done.4 = bf16[128,512]{1,0:T(8,128)(2,1)S(1)} collective-permute-done((bf16[128,512]{1,0:T(8,128)(2,1)S(1)}, bf16[128,512]{1,0:T(8,128)(2,1)S(1)}, u32[]{:S(2)}, u32[]{:S(2)}) %collective-permute-start.4) | collective-permute-done | bytes 131104 | tf_op jit(solution)/shard_map/ppermute | solution.py:27
  32.6 2.7 %collective-permute-done.9 = bf16[2,80,512]{2,1,0:T(8,128)(2,1)S(1)} collective-permute-done((bf16[2,80,512]{2,1,0:T(8,128)(2,1)S(1)}, bf16[2,80,512]{2,1,0:T(8,128)(2,1)S(1)}, u32[]{:S(2)}, u32[]{:S(2)}) %collective-permute-start.9) | collective-permute-done | bytes 163872 | tf_op jit(solution)/shard_map/ppermute | solution.py:27
  35.4 3.4 %collective-permute-start.10 = (bf16[2,2,80,512]{3,2,0,1:T(8,128)(2,1)S(1)}, bf16[2,2,80,512]{3,2,0,1:T(8,128)(2,1)S(1)}, u32[]{:S(2)}, u32[]{:S(2)}) collective-permute-start(bf16[2,2,80,512]{3,2,0,1:T(8,128)(2,1)S(1)} %maximum_select_fusion.7), channel_id=1, source_target_pairs={{0,4},{4,0},{8,12},{12,8},{16,20},{20,16},{24,28},{28,24},{1,5},{5... | collective-permute-start | bytes 983048 | tf_op jit(solution)/shard_map/ppermute | solution.py:27
  41.8 2.2 %collective-permute-start.6 = (bf16[2,2,128,512]{3,2,0,1:T(8,128)(2,1)}, bf16[2,2,128,512]{3,2,0,1:T(8,128)(2,1)}, u32[]{:S(2)}, u32[]{:S(2)}) collective-permute-start(bf16[2,2,128,512]{3,2,0,1:T(8,128)(2,1)} %maximum_select_fusion.5), channel_id=1, source_target_pairs={{0,4},{4,0},{8,12},{12,8},{16,20},{20,16},{24,28},{28,24},{1,5},{5... | collective-permute-start | bytes 1572872 | tf_op jit(solution)/shard_map/ppermute | solution.py:27
  44.2 1.5 %collective-permute-done.10 = bf16[2,2,80,512]{3,2,0,1:T(8,128)(2,1)S(1)} collective-permute-done((bf16[2,2,80,512]{3,2,0,1:T(8,128)(2,1)S(1)}, bf16[2,2,80,512]{3,2,0,1:T(8,128)(2,1)S(1)}, u32[]{:S(2)}, u32[]{:S(2)}) %collective-permute-start.10) | collective-permute-done | bytes 327712 | tf_op jit(solution)/shard_map/ppermute | solution.py:27
  46.9 9.4 %collective-permute-done.6 = bf16[2,2,128,512]{3,2,0,1:T(8,128)(2,1)} collective-permute-done((bf16[2,2,128,512]{3,2,0,1:T(8,128)(2,1)}, bf16[2,2,128,512]{3,2,0,1:T(8,128)(2,1)}, u32[]{:S(2)}, u32[]{:S(2)}) %collective-permute-start.6) | collective-permute-done | bytes 524320 | tf_op jit(solution)/shard_map/ppermute | solution.py:27
  57.7 1.7 %maximum_select_fusion = bf16[2,2,256,1024]{3,2,1,0:T(8,128)(2,1)} fusion(bf16[2,1,256,1024]{3,2,1,0:T(8,128)(2,1)S(1)} %maximum_select_fusion.2, bf16[2,1,256,1024]{3,2,1,0:T(8,128)(2,1)S(1)} %bitcast.261, pred[]{:T(512)S(6)} %eq.11), kind=kLoop, calls=%fused_computation.3 | loop fusion | flops 3145728 | bytes 4194305 | tf_op jit(solution)/shard_map/jit(_where)/select_n | solution.py:39
  59.4 14.5 %shard_map.263 = (f32[1024,512]{1,0:T(8,128)S(1)}, f32[1024,512]{1,0:T(8,128)}, f32[8,96,512]{2,1,0:T(8,128)S(1)}) custom-call(bf16[1024,1024]{1,0:T(8,128)(2,1)} %bitcast.251, bf16[512,384]{1,0:T(8,128)(2,1)S(1)} %bitcast.237, bf16[128,512]{1,0:T(8,128)(2,1)S(1)} %bitcast.238, f32[8,512]{1,0:T(8,128)S(1)} %concatenate.148.vec_ref, ...), custom_call_target="tpu_custom_call" | custom-call | flops 11811160064 | bytes 16777216 | tf_op jit(solution)/shard_map/pallas_call | solution.py:273
  76.0 9.6 %shard_map.264 = (f32[1024,512]{1,0:T(8,128)S(1)}, f32[1024,512]{1,0:T(8,128)S(1)}, f32[8,144,512]{2,1,0:T(8,128)}) custom-call(bf16[1024,1024]{1,0:T(8,128)(2,1)} %bitcast.252, bf16[512,512]{1,0:T(8,128)(2,1)S(1)} %bitcast.236, bf16[512,512]{1,0:T(8,128)(2,1)S(1)} %bitcast.235, f32[8,512]{1,0:T(8,128)S(1)} %concatenate.148.vec_ref, ...), custom_call_target="tpu_custom_call" | custom-call | flops 3221225472 | bytes 16777216 | tf_op jit(solution)/shard_map/pallas_call | solution.py:308
  85.7 1.9 %fusion.31 = (f32[2,2,1,144,512]{4,3,2,1,0:T(8,128)S(1)}, f32[2,2,1,144,512]{4,3,2,1,0:T(8,128)S(1)}) fusion(f32[2,2,2,144,512]{4,3,2,1,0:T(8,128)} %bitcast.247), kind=kLoop, calls=%fused_computation.112 | loop fusion | bytes 4718592 | tf_op jit(solution)/shard_map/slice | solution.py:67
  89.3 5.6 %collective-permute-done.14 = bf16[2,96,512]{2,1,0:T(8,128)(2,1)S(1)} collective-permute-done((bf16[2,96,512]{2,1,0:T(8,128)(2,1)S(1)}, bf16[2,96,512]{2,1,0:T(8,128)(2,1)S(1)}, u32[]{:S(2)}, u32[]{:S(2)}) %collective-permute-start.14) | collective-permute-done | bytes 196640 | tf_op jit(solution)/shard_map/ppermute | solution.py:27
  95.1 1.6 %collective-permute-start.15 = (bf16[96,512]{1,0:T(8,128)(2,1)S(1)}, bf16[96,512]{1,0:T(8,128)(2,1)S(1)}, u32[]{:S(2)}, u32[]{:S(2)}) collective-permute-start(bf16[96,512]{1,0:T(8,128)(2,1)S(1)} %fusion.17), channel_id=1, source_target_pairs={{0,16},{4,20},{8,24},{12,28},{16,0},{20,4},{24,8},{28,12},{1,17},{... | collective-permute-start | bytes 294920 | tf_op jit(solution)/shard_map/ppermute | solution.py:27
  96.7 4.9 %collective-permute-done.16 = bf16[2,2,144,512]{3,2,0,1:T(8,128)(2,1)S(1)} collective-permute-done((bf16[2,2,144,512]{3,2,0,1:T(8,128)(2,1)S(1)}, bf16[2,2,144,512]{3,2,0,1:T(8,128)(2,1)S(1)}, u32[]{:S(2)}, u32[]{:S(2)}) %collective-permute-start.16) | collective-permute-done | bytes 589856 | tf_op jit(solution)/shard_map/ppermute | solution.py:27
  103.1 5.7 %collective-permute-done.17 = bf16[2,144,512]{2,1,0:T(8,128)(2,1)S(1)} collective-permute-done((bf16[2,144,512]{2,1,0:T(8,128)(2,1)S(1)}, bf16[2,144,512]{2,1,0:T(8,128)(2,1)S(1)}, u32[]{:S(2)}, u32[]{:S(2)}) %collective-permute-start.17) | collective-permute-done | bytes 294944 | tf_op jit(solution)/shard_map/ppermute | solution.py:27
  109.0 1.6 %collective-permute-start.18 = (bf16[144,512]{1,0:T(8,128)(2,1)S(1)}, bf16[144,512]{1,0:T(8,128)(2,1)S(1)}, u32[]{:S(2)}, u32[]{:S(2)}) collective-permute-start(bf16[144,512]{1,0:T(8,128)(2,1)S(1)} %fusion.16), channel_id=1, source_target_pairs={{0,16},{4,20},{8,24},{12,28},{16,0},{20,4},{24,8},{28,12},{1,17},{... | collective-permute-start | bytes 442376 | tf_op jit(solution)/shard_map/ppermute | solution.py:27
  110.9 6.8 %collective-permute-done.18 = bf16[144,512]{1,0:T(8,128)(2,1)S(1)} collective-permute-done((bf16[144,512]{1,0:T(8,128)(2,1)S(1)}, bf16[144,512]{1,0:T(8,128)(2,1)S(1)}, u32[]{:S(2)}, u32[]{:S(2)}) %collective-permute-start.18) | collective-permute-done | bytes 147488 | tf_op jit(solution)/shard_map/ppermute | solution.py:27
  121.2 1.8 %collective-permute-start.12 = (bf16[256,1024]{1,0:T(8,128)(2,1)}, bf16[256,1024]{1,0:T(8,128)(2,1)}, u32[]{:S(2)}, u32[]{:S(2)}) collective-permute-start(bf16[256,1024]{1,0:T(8,128)(2,1)} %fusion.2), channel_id=1, source_target_pairs={{0,2},{1,3},{2,0},{3,1},{4,6},{5,7},{6,4},{7,5},{8,10},{9,11},{10,... | collective-permute-start | bytes 1572872 | tf_op jit(solution)/shard_map/ppermute | solution.py:27
  123.1 4.3 %collective-permute-done.20 = f32[2,24,896]{2,1,0:T(8,128)S(1)} collective-permute-done((f32[2,24,896]{2,1,0:T(8,128)S(1)}, f32[2,24,896]{2,1,0:T(8,128)S(1)}, u32[]{:S(2)}, u32[]{:S(2)}) %collective-permute-start.20) | collective-permute-done | bytes 172064 | tf_op jit(solution)/shard_map/ppermute | solution.py:27
  130.8 7.3 %collective-permute-done.12 = bf16[256,1024]{1,0:T(8,128)(2,1)} collective-permute-done((bf16[256,1024]{1,0:T(8,128)(2,1)}, bf16[256,1024]{1,0:T(8,128)(2,1)}, u32[]{:S(2)}, u32[]{:S(2)}) %collective-permute-start.12) | collective-permute-done | bytes 524320 | tf_op jit(solution)/shard_map/ppermute | solution.py:27
  (159 shorter events, 33.4 us)
Async XLA Ops:
  0.6 15.0 %copy-start.5 = (bf16[1,256,512]{2,1,0:T(8,128)(2,1)S(1)}, bf16[1,256,512]{2,1,0:T(8,128)(2,1)}, u32[]{:S(2)}) copy-start(bf16[1,256,512]{2,1,0:T(8,128)(2,1)} %param.16) | copy-start | bytes 786436
  0.7 15.0 %copy-start.3 = (bf16[1,256,512]{2,1,0:T(8,128)(2,1)S(1)}, bf16[1,256,512]{2,1,0:T(8,128)(2,1)}, u32[]{:S(2)}) copy-start(bf16[1,256,512]{2,1,0:T(8,128)(2,1)} %param.17) | copy-start | bytes 786436
  9.0 1.9 %collective-permute-start.2 = (bf16[2,16,1024]{2,1,0:T(8,128)(2,1)S(1)}, bf16[2,16,1024]{2,1,0:T(8,128)(2,1)S(1)}, u32[]{:S(2)}, u32[]{:S(2)}) collective-permute-start(bf16[2,16,1024]{2,1,0:T(8,128)(2,1)S(1)} %broadcast_select_fusion.1), channel_id=1, source_target_pairs={{0,1},{1,0},{2,3},{3,2},{4,5},{5,4},{6,7},{7,6},{8,9},{9,8},{10,11... | collective-permute-start | bytes 196616 | tf_op jit(solution)/shard_map/ppermute | solution.py:27
  9.5 8.8 %collective-permute-start.7 = (bf16[16,512]{1,0:T(8,128)(2,1)}, bf16[16,512]{1,0:T(8,128)(2,1)S(1)}, u32[]{:S(2)}, u32[]{:S(2)}) collective-permute-start(bf16[16,512]{1,0:T(8,128)(2,1)} %param.20), channel_id=1, source_target_pairs={{0,0},{1,4},{2,8},{3,12},{4,16},{5,20},{6,24},{7,28},{8,1},{9,5},{... | collective-permute-start | bytes 49160 | tf_op jit(solution)/shard_map/ppermute | solution.py:365
  10.9 7.4 %collective-permute-start.3 = (bf16[2,16,1024]{2,1,0:T(8,128)(2,1)S(1)}, bf16[2,16,1024]{2,1,0:T(8,128)(2,1)S(1)}, u32[]{:S(2)}, u32[]{:S(2)}) collective-permute-start(bf16[2,16,1024]{2,1,0:T(8,128)(2,1)S(1)} %broadcast_select_fusion.2), channel_id=1, source_target_pairs={{0,2},{1,3},{2,0},{3,1},{4,6},{5,7},{6,4},{7,5},{8,10},{9,11},{10,... | collective-permute-start | bytes 196616 | tf_op jit(solution)/shard_map/ppermute | solution.py:27
  15.8 23.1 %collective-permute-start = (bf16[256,1024]{1,0:T(8,128)(2,1)S(1)}, bf16[256,1024]{1,0:T(8,128)(2,1)S(1)}, u32[]{:S(2)}, u32[]{:S(2)}) collective-permute-start(bf16[256,1024]{1,0:T(8,128)(2,1)S(1)} %get-tuple-element.36), channel_id=1, source_target_pairs={{0,2},{1,3},{2,0},{3,1},{4,6},{5,7},{6,4},{7,5},{8,10},{9,11},{10,... | collective-permute-start | bytes 1572872 | tf_op jit(solution)/shard_map/ppermute | solution.py:27
  18.4 7.0 %collective-permute-start.8 = (bf16[80,512]{1,0:T(8,128)(2,1)S(1)}, bf16[80,512]{1,0:T(8,128)(2,1)S(1)}, u32[]{:S(2)}, u32[]{:S(2)}) collective-permute-start(bf16[80,512]{1,0:T(8,128)(2,1)S(1)} %get-tuple-element.56), channel_id=1, source_target_pairs={{0,16},{4,20},{8,24},{12,28},{16,0},{20,4},{24,8},{28,12},{1,17},{... | collective-permute-start | bytes 245768 | tf_op jit(solution)/shard_map/ppermute | solution.py:27
  21.6 10.3 %collective-permute-start.4 = (bf16[128,512]{1,0:T(8,128)(2,1)S(1)}, bf16[128,512]{1,0:T(8,128)(2,1)S(1)}, u32[]{:S(2)}, u32[]{:S(2)}) collective-permute-start(bf16[128,512]{1,0:T(8,128)(2,1)S(1)} %get-tuple-element.53), channel_id=1, source_target_pairs={{0,16},{4,20},{8,24},{12,28},{16,0},{20,4},{24,8},{28,12},{1,17},{... | collective-permute-start | bytes 393224 | tf_op jit(solution)/shard_map/ppermute | solution.py:27
  25.4 9.9 %collective-permute-start.9 = (bf16[2,80,512]{2,1,0:T(8,128)(2,1)S(1)}, bf16[2,80,512]{2,1,0:T(8,128)(2,1)S(1)}, u32[]{:S(2)}, u32[]{:S(2)}) collective-permute-start(bf16[2,80,512]{2,1,0:T(8,128)(2,1)S(1)} %maximum_select_fusion.10), channel_id=1, source_target_pairs={{0,8},{4,12},{8,0},{12,4},{16,24},{20,28},{24,16},{28,20},{1,9},{5... | collective-permute-start | bytes 491528 | tf_op jit(solution)/shard_map/ppermute | solution.py:27
  31.9 9.0 %collective-permute-start.5 = (bf16[2,128,512]{2,1,0:T(8,128)(2,1)S(1)}, bf16[2,128,512]{2,1,0:T(8,128)(2,1)S(1)}, u32[]{:S(2)}, u32[]{:S(2)}) collective-permute-start(bf16[2,128,512]{2,1,0:T(8,128)(2,1)S(1)} %maximum_select_fusion.9), channel_id=1, source_target_pairs={{0,8},{4,12},{8,0},{12,4},{16,24},{20,28},{24,16},{28,20},{1,9},{5... | collective-permute-start | bytes 786440 | tf_op jit(solution)/shard_map/ppermute | solution.py:27
  35.4 10.3 %collective-permute-start.10 = (bf16[2,2,80,512]{3,2,0,1:T(8,128)(2,1)S(1)}, bf16[2,2,80,512]{3,2,0,1:T(8,128)(2,1)S(1)}, u32[]{:S(2)}, u32[]{:S(2)}) collective-permute-start(bf16[2,2,80,512]{3,2,0,1:T(8,128)(2,1)S(1)} %maximum_select_fusion.7), channel_id=1, source_target_pairs={{0,4},{4,0},{8,12},{12,8},{16,20},{20,16},{24,28},{28,24},{1,5},{5... | collective-permute-start | bytes 983048 | tf_op jit(solution)/shard_map/ppermute | solution.py:27
  40.0 17.6 %collective-permute-start.1 = (bf16[2,256,1024]{2,1,0:T(8,128)(2,1)}, bf16[2,256,1024]{2,1,0:T(8,128)(2,1)S(1)}, u32[]{:S(2)}, u32[]{:S(2)}) collective-permute-start(bf16[2,256,1024]{2,1,0:T(8,128)(2,1)} %maximum_select_fusion.1), channel_id=1, source_target_pairs={{0,1},{1,0},{2,3},{3,2},{4,5},{5,4},{6,7},{7,6},{8,9},{9,8},{10,11... | collective-permute-start | bytes 3145736 | tf_op jit(solution)/shard_map/ppermute | solution.py:27
  41.8 14.6 %collective-permute-start.6 = (bf16[2,2,128,512]{3,2,0,1:T(8,128)(2,1)}, bf16[2,2,128,512]{3,2,0,1:T(8,128)(2,1)}, u32[]{:S(2)}, u32[]{:S(2)}) collective-permute-start(bf16[2,2,128,512]{3,2,0,1:T(8,128)(2,1)} %maximum_select_fusion.5), channel_id=1, source_target_pairs={{0,4},{4,0},{8,12},{12,8},{16,20},{20,16},{24,28},{28,24},{1,5},{5... | collective-permute-start | bytes 1572872 | tf_op jit(solution)/shard_map/ppermute | solution.py:27
  75.2 13.7 %collective-permute-start.13 = (bf16[2,2,96,512]{3,2,0,1:T(8,128)(2,1)S(1)}, bf16[2,2,96,512]{3,2,0,1:T(8,128)(2,1)S(1)}, u32[]{:S(2)}, u32[]{:S(2)}) collective-permute-start(bf16[2,2,96,512]{3,2,0,1:T(8,128)(2,1)S(1)} %fusion.6), channel_id=1, source_target_pairs={{0,4},{4,0},{8,12},{12,8},{16,20},{20,16},{24,28},{28,24},{1,5},{5... | collective-permute-start | bytes 1179656 | tf_op jit(solution)/shard_map/ppermute | solution.py:27
  87.7 13.9 %collective-permute-start.16 = (bf16[2,2,144,512]{3,2,0,1:T(8,128)(2,1)S(1)}, bf16[2,2,144,512]{3,2,0,1:T(8,128)(2,1)S(1)}, u32[]{:S(2)}, u32[]{:S(2)}) collective-permute-start(bf16[2,2,144,512]{3,2,0,1:T(8,128)(2,1)S(1)} %fusion.1), channel_id=1, source_target_pairs={{0,4},{4,0},{8,12},{12,8},{16,20},{20,16},{24,28},{28,24},{1,5},{5... | collective-permute-start | bytes 1769480 | tf_op jit(solution)/shard_map/ppermute | solution.py:27
  89.2 5.7 %collective-permute-start.14 = (bf16[2,96,512]{2,1,0:T(8,128)(2,1)S(1)}, bf16[2,96,512]{2,1,0:T(8,128)(2,1)S(1)}, u32[]{:S(2)}, u32[]{:S(2)}) collective-permute-start(bf16[2,96,512]{2,1,0:T(8,128)(2,1)S(1)} %fusion.11), channel_id=1, source_target_pairs={{0,8},{4,12},{8,0},{12,4},{16,24},{20,28},{24,16},{28,20},{1,9},{5... | collective-permute-start | bytes 589832 | tf_op jit(solution)/shard_map/ppermute | solution.py:27
  95.1 7.3 %collective-permute-start.15 = (bf16[96,512]{1,0:T(8,128)(2,1)S(1)}, bf16[96,512]{1,0:T(8,128)(2,1)S(1)}, u32[]{:S(2)}, u32[]{:S(2)}) collective-permute-start(bf16[96,512]{1,0:T(8,128)(2,1)S(1)} %fusion.17), channel_id=1, source_target_pairs={{0,16},{4,20},{8,24},{12,28},{16,0},{20,4},{24,8},{28,12},{1,17},{... | collective-permute-start | bytes 294920 | tf_op jit(solution)/shard_map/ppermute | solution.py:27
  102.0 6.8 %collective-permute-start.17 = (bf16[2,144,512]{2,1,0:T(8,128)(2,1)S(1)}, bf16[2,144,512]{2,1,0:T(8,128)(2,1)S(1)}, u32[]{:S(2)}, u32[]{:S(2)}) collective-permute-start(bf16[2,144,512]{2,1,0:T(8,128)(2,1)S(1)} %fusion.7), channel_id=1, source_target_pairs={{0,8},{4,12},{8,0},{12,4},{16,24},{20,28},{24,16},{28,20},{1,9},{5... | collective-permute-start | bytes 884744 | tf_op jit(solution)/shard_map/ppermute | solution.py:27
  102.4 8.4 %collective-permute-start.21 = (f32[16,512]{1,0:T(8,128)S(1)}, f32[16,512]{1,0:T(8,128)S(1)}, u32[]{:S(2)}, u32[]{:S(2)}) collective-permute-start(f32[16,512]{1,0:T(8,128)S(1)} %slice.272), channel_id=1, source_target_pairs={{0,0},{4,1},{8,2},{12,3},{16,4},{20,5},{24,6},{28,7},{1,8},{5,9},{... | collective-permute-start | bytes 98312 | tf_op jit(solution)/shard_map/ppermute | solution.py:417
  109.0 8.7 %collective-permute-start.18 = (bf16[144,512]{1,0:T(8,128)(2,1)S(1)}, bf16[144,512]{1,0:T(8,128)(2,1)S(1)}, u32[]{:S(2)}, u32[]{:S(2)}) collective-permute-start(bf16[144,512]{1,0:T(8,128)(2,1)S(1)} %fusion.16), channel_id=1, source_target_pairs={{0,16},{4,20},{8,24},{12,28},{16,0},{20,4},{24,8},{28,12},{1,17},{... | collective-permute-start | bytes 442376 | tf_op jit(solution)/shard_map/ppermute | solution.py:27
  110.8 8.5 %collective-permute-start.11 = (bf16[2,256,1024]{2,1,0:T(8,128)(2,1)S(1)}, bf16[2,256,1024]{2,1,0:T(8,128)(2,1)S(1)}, u32[]{:S(2)}, u32[]{:S(2)}) collective-permute-start(bf16[2,256,1024]{2,1,0:T(8,128)(2,1)S(1)} %fusion), channel_id=1, source_target_pairs={{0,1},{1,0},{2,3},{3,2},{4,5},{5,4},{6,7},{7,6},{8,9},{9,8},{10,11... | collective-permute-start | bytes 3145736 | tf_op jit(solution)/shard_map/ppermute | solution.py:27
  118.6 1.5 %collective-permute-start.19 = (f32[2,24,896]{2,1,0:T(8,128)S(1)}, f32[2,24,896]{2,1,0:T(8,128)S(1)}, u32[]{:S(2)}, u32[]{:S(2)}) collective-permute-start(f32[2,24,896]{2,1,0:T(8,128)S(1)} %fusion.15), channel_id=1, source_target_pairs={{0,1},{1,0},{2,3},{3,2},{4,5},{5,4},{6,7},{7,6},{8,9},{9,8},{10,11... | collective-permute-start | bytes 516104 | tf_op jit(solution)/shard_map/ppermute | solution.py:27
  120.1 7.3 %collective-permute-start.20 = (f32[2,24,896]{2,1,0:T(8,128)S(1)}, f32[2,24,896]{2,1,0:T(8,128)S(1)}, u32[]{:S(2)}, u32[]{:S(2)}) collective-permute-start(f32[2,24,896]{2,1,0:T(8,128)S(1)} %broadcast_select_fusion), channel_id=1, source_target_pairs={{0,2},{1,3},{2,0},{3,1},{4,6},{5,7},{6,4},{7,5},{8,10},{9,11},{10,... | collective-permute-start | bytes 516104 | tf_op jit(solution)/shard_map/ppermute | solution.py:27
  121.2 16.9 %collective-permute-start.12 = (bf16[256,1024]{1,0:T(8,128)(2,1)}, bf16[256,1024]{1,0:T(8,128)(2,1)}, u32[]{:S(2)}, u32[]{:S(2)}) collective-permute-start(bf16[256,1024]{1,0:T(8,128)(2,1)} %fusion.2), channel_id=1, source_target_pairs={{0,2},{1,3},{2,0},{3,1},{4,6},{5,7},{6,4},{7,5},{8,10},{9,11},{10,... | collective-permute-start | bytes 1572872 | tf_op jit(solution)/shard_map/ppermute | solution.py:27
  (7 other events, 49.6 us)

commit v2 on v1

--- a/solution.py
+++ b/solution.py
@@ -92,8 +92,7 @@
     return centered * scale, scale
 
 
-def norm_back(normal, scale, gain, upstream):
-    inner = gain * upstream
+def norm_back(normal, scale, inner):
     first = jnp.mean(inner, axis=-1, keepdims=True)
     second = jnp.mean(inner * normal, axis=-1, keepdims=True)
     return scale * (inner - first - normal * second)
@@ -194,7 +193,7 @@
         vectors[0] += jnp.sum(normal * upstream, axis=0, keepdims=True)
         vectors[1] += jnp.sum(upstream, axis=0, keepdims=True)
         vectors[2] += jnp.sum(xg_ref[rows, width:].astype(F32), axis=0, keepdims=True)
-        dx_ref[rows, :] = norm_back(normal, scale, gain, upstream)
+        dx_ref[rows, :] = norm_back(normal, scale, gain * upstream)
 
     grad_qkv = dot_rows(na_ref[...], dp_ref[...])
     grad_out = dot_rows(att_ref[...], xg_ref[:, width:])
@@ -247,7 +246,7 @@
         upstream = dot_last(grad_hidden, up_ref[...])
         vectors[0] += jnp.sum(normal * upstream, axis=0, keepdims=True)
         vectors[1] += jnp.sum(upstream, axis=0, keepdims=True)
-        dx_ref[rows, :] = (dx_part_ref[rows, :] + norm_back(normal, scale, gain, upstream)).astype(dx_ref.dtype)
+        dx_ref[rows, :] = (dx_part_ref[rows, :] + norm_back(normal, scale, gain * upstream)).astype(dx_ref.dtype)
     grad_up = dot_rows(nb_ref[...], dh_ref[...])
     grad_down = dot_rows(act_ref[...], xg_ref[:, width:])
     rest = grad_ref.shape[1] - up_rows - down_rows
@@ -341,7 +340,7 @@
     return np.tile(cosine, (1, heads)), np.tile(sine, (1, heads))
 
 
-def shards(
+def shards_any(
     owners, groups,
     inputs, cotangent, w_qkv, b_qkv, w_out, b_out, w_up, b_up, w_down, b_down,
     gain_one, shift_one, gain_two, shift_two,
@@ -463,6 +462,615 @@
     )
 
 
+def reversed_bits(value, count):
+    result = 0
+    for bit in range(count):
+        result = result | (((value >> bit) & 1) << (count - 1 - bit))
+    return result
+
+
+def after(value, *others):
+    return lax.optimization_barrier((value,) + others)[0]
+
+
+def spread(value, axis, size, gates=()):
+    value, seen = value[None], []
+    for step, bit in enumerate(reversed(range(log2(size)))):
+        seen.append(exchange(value, axis, size, bit))
+        if bit:
+            other = after(seen[-1], *gates[step]) if step < len(gates) else seen[-1]
+            value = jnp.concatenate([value, other], 0)
+    return (value, seen[-1]), seen
+
+
+def fold(kept, other):
+    total = kept + other.astype(F32)
+    half = total.shape[0] // 2
+    return total[half:].astype(BF16), total[:half]
+
+
+def finish(kept, other):
+    return kept[0] + other[0].astype(F32)
+
+
+def call(kernel, outs, scratch, flops, transcendentals, *operands, mib=8, far=0):
+    return pl.pallas_call(
+        kernel,
+        out_shape=tuple(outs),
+        in_specs=whole(len(operands) - far)
+        + [pl.BlockSpec(memory_space=pltpu.HBM)] * far,
+        out_specs=tuple(whole(len(outs))),
+        scratch_shapes=scratch,
+        compiler_params=pltpu.CompilerParams(vmem_limit_bytes=mib * 1024 * 1024),
+        cost_estimate=pl.CostEstimate(flops=1, bytes_accessed=1, transcendentals=0),
+    )(*operands)
+
+
+def fetch(pairs, sems):
+    copies = [pltpu.make_async_copy(source, to, sems.at[i]) for i, (source, to) in enumerate(pairs)]
+    for copy in copies:
+        copy.start()
+    for copy in copies:
+        copy.wait()
+
+
+def pack_kernel(*refs):
+    count = (len(refs) - 4) // 2
+    (sent_ref, kept_ref, block_ref, sems), held = refs[count : count + 4], refs[count + 4 :]
+    fetch(tuple(zip(refs[:count], held)), sems)
+    qkv_ref, up_ref, out_ref, small = held[0], held[1], held[2], held[3:]
+    me = lax.axis_index("seq")
+    groups, rows, _ = block_ref.shape
+    width = qkv_ref.shape[1] // 3
+    part = width // groups
+    piece = rows * groups
+    owners = up_ref.shape[1] // (groups * piece)
+    lines = []
+    for line in (small[:2], small[2:]):
+        values = [ref[...].reshape(1, ref.shape[0]).astype(F32) for ref in line]
+        used = sum(ref.shape[0] for ref in line)
+        lines.append(jnp.concatenate(values + [jnp.zeros((1, part - used), F32)], 1))
+    lines = jnp.concatenate(lines + [jnp.zeros((rows - 2, part), F32)], 0).astype(BF16)
+    for group in range(groups):
+        for c in range(3):
+            start = c * width + group * part
+            block_ref[group, :, c * part : (c + 1) * part] = qkv_ref[:, start : start + part]
+        block_ref[group, :, 3 * part : width] = lines
+        block_ref[group, :, width + up_ref.shape[1] // groups :] = out_ref[...]
+        block_ref[group, :, width : width + up_ref.shape[1] // groups] = jnp.concatenate(
+            [
+                up_ref[:, (k * groups + group) * piece : (k * groups + group + 1) * piece]
+                for k in range(owners)
+            ],
+            1,
+        )
+    for half in range(groups // 2):
+        kept_ref[half] = block_ref[me ^ (2 * half)]
+        sent_ref[half] = block_ref[me ^ (2 * half + 1)]
+
+
+def payload_kernel(kept_ref, near_ref, far_ref, down_ref, first_ref, second_ref, sem):
+    me = lax.axis_index("seq")
+    width = down_ref.shape[1]
+    part, rows = width // 4, first_ref.shape[0] // 8
+    copy = pltpu.make_async_copy(down_ref, second_ref.at[pl.ds(4 * rows, down_ref.shape[0])], sem)
+    copy.start()
+    hidden = kept_ref.shape[2] - 2 * width
+    for step, block in enumerate((kept_ref.at[0], near_ref.at[0], far_ref.at[0], far_ref.at[1])):
+        group = me ^ step
+        lanes = pl.ds(pl.multiple_of(group * part, part), part)
+        second_ref[pl.ds(pl.multiple_of(group * rows, rows), rows), :] = block[:, width : width + hidden]
+        for c in range(3):
+            first_ref[c * rows : (c + 1) * rows, lanes] = block[:, c * part : (c + 1) * part]
+        first_ref[3 * rows : 4 * rows, lanes] = block[:, 3 * part : width]
+        first_ref[pl.ds(pl.multiple_of((4 + group) * rows, rows), rows), :] = block[:, width + hidden :]
+    copy.wait()
+
+
+def merge_kernel(bit, mine_ref, other_ref, out_ref):
+    last = mine_ref.shape[0] * 2 - out_ref.shape[0]
+    part = mine_ref.shape[0] - last
+    out_ref[:part, :] = mine_ref[:part, :]
+    out_ref[part : 2 * part, :] = other_ref[:part, :]
+    same = (lax.axis_index("dp") >> bit) & 1 == (lax.axis_index("seq") >> (bit - 1)) & 1
+
+    @pl.when(same)
+    def _():
+        out_ref[2 * part :, :] = mine_ref[part:, :]
+
+    @pl.when(jnp.logical_not(same))
+    def _():
+        out_ref[2 * part :, :] = other_ref[part:, :]
+
+
+def sources(pair, me):
+    half = pair[0].shape[0]
+    count = log2(2 * half)
+    for slot in range(2 * half):
+        ref = pair[slot // half]
+        yield ref.at[slot % half], me ^ reversed_bits(slot, count)
+
+
+def project_kernel(
+    first_ref, other_ref, x_ref, y_ref, cos_ref, sin_ref, table_ref,
+    xg_ref, na_ref, q_ref, qt_ref, k_ref, v_ref, da_ref, dat_ref, wq_ref, wo_ref, vec_ref,
+):
+    owner, group = lax.axis_index("dp"), lax.axis_index("seq")
+    width = first_ref.shape[1]
+    groups = 2 * x_ref.shape[0]
+    part = width // groups
+    rows = first_ref.shape[0] // 20
+    owners = width // (rows * groups)
+    local = x_ref.shape[1]
+    lines = []
+    for slot in range(owners):
+        block = (first_ref, other_ref)[slot // 4].at[pl.ds(slot % 4 * 4 * rows, 4 * rows)]
+        rank = owner ^ reversed_bits(slot, log2(owners))
+        for g in range(groups):
+            lanes = slice(g * part, (g + 1) * part)
+            to = pl.ds(pl.multiple_of((rank * groups + g) * rows, rows), rows)
+            for c in range(3):
+                wq_ref[to, c * part : (c + 1) * part] = block[c * rows : (c + 1) * rows, lanes]
+            lines.append(block[3 * rows : 4 * rows, lanes].astype(F32)[:8, :])
+    for slot, ref in enumerate((first_ref, other_ref)):
+        x = (owner & 1) ^ slot
+        wo_ref[pl.ds(pl.multiple_of(x * 4 * rows, 4 * rows), 4 * rows), :] = ref[16 * rows :, :]
+    devices = owners * groups
+    line_one = jnp.concatenate([line[0:1] for line in lines], 0).astype(BF16)
+    line_two = jnp.concatenate([line[1:2] for line in lines], 0).astype(BF16)
+
+    def device_of(shape):
+        slot = lax.broadcasted_iota(jnp.int32, shape, 0)
+        rank = owner ^ reversed_bits(slot // groups, log2(owners))
+        return rank * groups + slot % groups
+
+    def place_values(line, lane_of, device_of_column):
+        columns = lane_of.shape[1]
+        pick = lax.broadcasted_iota(jnp.int32, (line.shape[1], columns), 0) == lane_of
+        values = dot(line, jnp.where(pick, 1.0, 0.0).astype(BF16))
+        held = device_of((devices, columns)) == device_of_column
+        return jnp.sum(jnp.where(held, values, 0.0), axis=0, keepdims=True)
+
+    column = lax.broadcasted_iota(jnp.int32, (1, width), 1)
+    own = [place_values(line_two, column % rows + v * rows, column // rows) for v in range(6)]
+    piece = rows * groups
+    start = 3 * width // devices
+    bias_up = place_values(line_one, column % piece + start, column // piece * groups + group)
+    lane_of = jnp.concatenate(
+        [table_ref[0:1, pl.ds(pl.multiple_of(c * width + group * part, part), part)] for c in range(3)], 1
+    )
+    owner_of = jnp.concatenate(
+        [table_ref[1:2, pl.ds(pl.multiple_of(c * width + group * part, part), part)] for c in range(3)], 1
+    )
+    bias = place_values(line_one, lane_of, owner_of)
+    gain, shift = own[2], own[3]
+    vec_ref[...] = jnp.concatenate(
+        own[2:] + [own[0] + own[1], bias_up, jnp.zeros((2, width), F32)], 0
+    )
+
+    lane = lax.broadcasted_iota(jnp.int32, (local, part), 1)
+    turn = lane % HD < ROT // 2
+
+    def partner(value):
+        return jnp.where(
+            turn, pltpu.roll(value, part - ROT // 2, 1), pltpu.roll(value, ROT // 2, 1)
+        )
+
+    for block, rank in sources((x_ref, y_ref), group):
+        start = pl.multiple_of(rank * local, local)
+        to = pl.ds(start, local)
+        both = block[...]
+        xg_ref[to, :] = both
+        normal, _ = standardize(both[:, :width].astype(F32))
+        normed = (normal * gain + shift).astype(BF16)
+        na_ref[to, :] = normed
+        projected = dot(normed, wq_ref[...]) + bias
+        cosine, sine = cos_ref[to, :], sin_ref[to, :]
+        query = projected[:, :part]
+        query = query * cosine + partner(query) * sine
+        key = projected[:, part : 2 * part]
+        key = key * cosine + partner(key) * sine
+        query = query.astype(BF16).astype(F32) * HD**-0.5
+        q_ref[to, :] = query.astype(BF16)
+        qt_ref[:, to] = query.T.astype(BF16)
+        k_ref[to, :] = key.astype(BF16)
+        v_ref[to, :] = projected[:, 2 * part :].astype(BF16)
+        grad_att = dot_last(both[:, width:], wo_ref[...]).astype(BF16)
+        da_ref[to, :] = grad_att
+        dat_ref[:, to] = grad_att.astype(F32).T.astype(BF16)
+
+
+def attend_kernel(
+    xg_ref, na_ref, q_ref, qt_ref, k_ref, v_ref, da_ref, dat_ref, wq_ref, cos_ref, sin_ref,
+    att_ref, dp_ref, sent_ref, kept_ref,
+    dq_ref, dkt_ref, dvt_ref, gq_ref, go_ref,
+):
+    owner = lax.axis_index("dp")
+    tokens, part = q_ref.shape
+    width = na_ref.shape[1]
+    groups = width // part
+    owners = 2 * sent_ref.shape[0]
+    rows = part // owners
+    lane = lax.broadcasted_iota(jnp.int32, (BLOCK, part), 1)
+    turn = lane % HD < ROT // 2
+
+    def partner(value):
+        return jnp.where(
+            turn, pltpu.roll(value, part - ROT // 2, 1), pltpu.roll(value, ROT // 2, 1)
+        )
+
+    dkt_ref[...] = jnp.zeros_like(dkt_ref)
+    dvt_ref[...] = jnp.zeros_like(dvt_ref)
+    below = lax.broadcasted_iota(jnp.int32, (BLOCK, BLOCK), 0) >= lax.broadcasted_iota(
+        jnp.int32, (BLOCK, BLOCK), 1
+    )
+    zero = jnp.zeros((), BF16)
+    for block in range(tokens // BLOCK):
+        at = pl.ds(block * BLOCK, BLOCK)
+        seen = (block + 1) * BLOCK
+        attended = jnp.zeros((BLOCK, part), F32)
+        grad_query = jnp.zeros((BLOCK, part), F32)
+        for head in range(part // HD):
+            mine = lane // HD == head
+            mine_t = lax.broadcasted_iota(jnp.int32, (part, BLOCK), 0) // HD == head
+            query = jnp.where(mine, q_ref[at, :], zero)
+            grad_att = jnp.where(mine, da_ref[at, :], zero)
+            scores = dot_last(query, k_ref[:seen, :])
+            last = jnp.where(below, scores[:, seen - BLOCK :], -1e30)
+            scores = last if block == 0 else jnp.concatenate([scores[:, : seen - BLOCK], last], 1)
+            raised = jnp.exp(scores - jnp.max(scores, axis=-1, keepdims=True))
+            probs = raised * (1.0 / jnp.sum(raised, axis=-1, keepdims=True))
+            probs_low = probs.astype(BF16)
+            attended = jnp.where(mine, dot(probs_low, v_ref[:seen, :]), attended)
+            grad_probs = dot_last(grad_att, v_ref[:seen, :])
+            inner = jnp.sum(probs * grad_probs, axis=-1, keepdims=True)
+            grad_scores = (probs * (grad_probs - inner)).astype(BF16)
+            grad_query = jnp.where(mine, dot(grad_scores, k_ref[:seen, :]), grad_query)
+            query_t = jnp.where(mine_t, qt_ref[:, at], zero)
+            grad_att_t = jnp.where(mine_t, dat_ref[:, at], zero)
+            dkt_ref[:, :seen] += dot(query_t, grad_scores)
+            dvt_ref[:, :seen] += dot(grad_att_t, probs_low)
+        att_ref[at, :] = attended.astype(BF16)
+        dq_ref[at, :] = grad_query * HD**-0.5
+
+    vectors = [jnp.zeros((1, width), F32) for _ in range(3)]
+    grad_bias = jnp.zeros((1, 3 * part), F32)
+    for block in range(tokens // BLOCK):
+        at = pl.ds(block * BLOCK, BLOCK)
+        cosine, sine = cos_ref[at, :], sin_ref[at, :]
+        grad_query = dq_ref[at, :]
+        grad_query = grad_query * cosine - partner(grad_query) * sine
+        grad_key = dkt_ref[:, at].T
+        grad_key = grad_key * cosine - partner(grad_key) * sine
+        grad_proj = jnp.concatenate([grad_query, grad_key, dvt_ref[:, at].T], 1).astype(BF16)
+        dp_ref[at, :] = grad_proj
+        grad_bias += jnp.sum(grad_proj.astype(F32), axis=0, keepdims=True)
+        upstream = dot_last(grad_proj, wq_ref[...])
+        normal, _ = standardize(xg_ref[at, :width].astype(F32))
+        vectors[0] += jnp.sum(normal * upstream, axis=0, keepdims=True)
+        vectors[1] += jnp.sum(upstream, axis=0, keepdims=True)
+        vectors[2] += jnp.sum(xg_ref[at, width:].astype(F32), axis=0, keepdims=True)
+
+    gq_ref[...] = dot_rows(na_ref[...], dp_ref[...])
+    go_ref[...] = dot_rows(att_ref[...], xg_ref[:, width:])
+    tail = jnp.concatenate(
+        [jnp.concatenate([grad_bias, jnp.zeros((1, width - 3 * part), F32)], 1)]
+        + vectors
+        + [jnp.zeros((rows - 4, width), F32)],
+        0,
+    )
+    for ref, rank in sources((kept_ref, sent_ref), owner):
+        kind = ref.dtype
+        for g in range(groups):
+            at = pl.ds(pl.multiple_of((rank * groups + g) * rows, rows), rows)
+            for c in range(3):
+                ref[c * rows : (c + 1) * rows, g * part : (g + 1) * part] = gq_ref[
+                    at, c * part : (c + 1) * part
+                ].astype(kind)
+        ref[3 * rows : 4 * rows, :] = go_ref[pl.ds(pl.multiple_of(rank * rows, rows), rows), :].astype(kind)
+        ref[4 * rows :, :] = tail.astype(kind)
+
+
+def hidden_kernel(
+    second_ref, other_ref, xg_ref, vec_ref,
+    act_ref, dh_ref, up_ref, down_ref, sent_ref, kept_ref,
+    nb_ref, gu_ref,
+):
+    owner = lax.axis_index("dp")
+    tokens, hidden_width = act_ref.shape
+    width = vec_ref.shape[1]
+    rows = second_ref.shape[1] // 2
+    for block, rank in sources((second_ref, other_ref), owner):
+        at = pl.ds(pl.multiple_of(rank * rows, rows), rows)
+        up_ref[at, :] = block[:rows, :]
+        down_ref[at, :] = block[rows:, :]
+    gain, shift, bias = vec_ref[2:3, :], vec_ref[3:4, :], vec_ref[5:6, :]
+    vectors = [jnp.zeros((1, width), F32) for _ in range(2)]
+    grad_bias = jnp.zeros((1, hidden_width), F32)
+    for block in range(tokens // BLOCK):
+        at = pl.ds(block * BLOCK, BLOCK)
+        normal, _ = standardize(xg_ref[at, :width].astype(F32))
+        normed = (normal * gain + shift).astype(BF16)
+        nb_ref[at, :] = normed
+        hidden = dot(normed, up_ref[...]) + bias
+        half = 0.5 * (1.0 + lax.erf(hidden * math.sqrt(0.5)))
+        act_ref[at, :] = (hidden * half).astype(BF16)
+        slope = half + hidden * jnp.exp(-0.5 * hidden * hidden) * (1.0 / math.sqrt(2.0 * math.pi))
+        grad_hidden = (dot_last(xg_ref[at, width:], down_ref[...]) * slope).astype(BF16)
+        dh_ref[at, :] = grad_hidden
+        grad_bias += jnp.sum(grad_hidden.astype(F32), axis=0, keepdims=True)
+        upstream = dot_last(grad_hidden, up_ref[...])
+        vectors[0] += jnp.sum(normal * upstream, axis=0, keepdims=True)
+        vectors[1] += jnp.sum(upstream, axis=0, keepdims=True)
+    gu_ref[...] = dot_rows(nb_ref[...], dh_ref[...])
+    extra = sent_ref.shape[1] - rows
+    tail = jnp.concatenate([grad_bias] + vectors + [jnp.zeros((extra - 3, width), F32)], 0)
+    for ref, rank in sources((kept_ref, sent_ref), owner):
+        ref[:rows, :] = gu_ref[pl.ds(pl.multiple_of(rank * rows, rows), rows), :].astype(ref.dtype)
+        ref[rows:, :] = tail.astype(ref.dtype)
+
+
+def down_kernel(act_ref, xg_ref, sent_ref, kept_ref, gd_ref):
+    width = sent_ref.shape[2]
+    rows = sent_ref.shape[1]
+    gd_ref[...] = dot_rows(act_ref[...], xg_ref[:, width:])
+    for ref, rank in sources((kept_ref, sent_ref), lax.axis_index("dp")):
+        ref[...] = gd_ref[pl.ds(pl.multiple_of(rank * rows, rows), rows), :].astype(ref.dtype)
+
+
+def join_kernel(
+    xg_ref, att_ref, wo_ref, act_ref, down_ref, vec_ref, dp_ref, wq_ref, dh_ref, up_ref,
+    sent_ref, kept_ref,
+):
+    group = lax.axis_index("seq")
+    local = sent_ref.shape[1]
+    width = wo_ref.shape[1]
+    gain_one, gain_two, bias = vec_ref[0:1, :], vec_ref[2:3, :], vec_ref[4:5, :]
+    for step in range(2 * sent_ref.shape[0]):
+        at = pl.ds(pl.multiple_of((group ^ step) * local, local), local)
+        ref = (kept_ref, sent_ref)[step % 2].at[step // 2]
+        out = dot(att_ref[at, :], wo_ref[...]) + dot(act_ref[at, :], down_ref[...])
+        rows_in = xg_ref[at, :width].astype(F32)
+        normal, scale = standardize(rows_in)
+        inner = gain_one * dot_last(dp_ref[at, :], wq_ref[...]) + gain_two * dot_last(dh_ref[at, :], up_ref[...])
+        grad = norm_back(normal, scale, inner)
+        if step == 0:
+            out = out + rows_in + bias
+            grad = grad + xg_ref[at, width:].astype(F32)
+        ref[:, :width] = out.astype(ref.dtype)
+        ref[:, width:] = grad.astype(ref.dtype)
+
+
+def deal_kernel(a_ref, b_ref, sent_ref, kept_ref):
+    me = lax.axis_index("seq")
+    width = a_ref.shape[1]
+    part = width // 4
+    rows = a_ref.shape[0] // 5
+    kind = sent_ref.dtype
+    small = jnp.concatenate(
+        [a_ref[4 * rows : 4 * rows + 3, :], b_ref[4 * rows + 1 : 4 * rows + 3, :], jnp.zeros((rows - 5, width), F32)], 0
+    )
+    for step in range(4):
+        group = me ^ step
+        ref = (kept_ref, sent_ref)[step % 2].at[step // 2]
+        lanes = pl.ds(pl.multiple_of(group * part, part), part)
+        for c in range(3):
+            ref[:rows, c * part : (c + 1) * part] = a_ref[c * rows : (c + 1) * rows, lanes].astype(kind)
+        ref[:rows, 3 * part :] = b_ref[pl.ds(pl.multiple_of(group * rows, rows), rows), :].astype(kind)
+        ref[rows:, :width] = small.astype(kind)
+        ref[rows:, width:] = jnp.zeros((rows, 3 * part), kind)
+
+
+def collect_kernel(
+    kept_ref, near_ref, far_ref, a_ref, b_ref, out_ref,
+    qkv_ref, up_ref, wout_ref, bqkv_ref, bias_ref, twin_ref, bup_ref, gain_one_ref, shift_one_ref, gain_two_ref, shift_two_ref,
+    block_ref,
+):
+    me = lax.axis_index("seq")
+    place = lax.axis_index("dp") * 4 + me
+    rows = qkv_ref.shape[0]
+    width = qkv_ref.shape[1] // 3
+    part = width // 4
+    piece = 4 * rows
+    for step, block in enumerate((kept_ref.at[0], near_ref.at[0], far_ref.at[0], far_ref.at[1])):
+        block_ref[me ^ step] = block[...].astype(F32)
+    for g in range(4):
+        for c in range(3):
+            qkv_ref[:, c * width + g * part : c * width + (g + 1) * part] = block_ref[
+                g, :rows, c * part : (c + 1) * part
+            ]
+    for k in range(up_ref.shape[1] // (4 * piece)):
+        start = 3 * part + k * piece
+        up_ref[:, 4 * k * piece : 4 * (k + 1) * piece] = jnp.concatenate(
+            [block_ref[g, :rows, start : start + piece] for g in range(4)], 1
+        )
+    wout_ref[...] = out_ref[...]
+
+    def own(values, ref, index):
+        size, count = values.shape[1], ref.shape[0]
+        values = pltpu.roll(values, (size - index * count) % size, 1)[0:1, :count]
+        ref[...] = values.reshape(count)
+
+    sums = sum(block_ref[g, rows : rows + 8, :width] for g in range(4))
+    for i, ref in enumerate((gain_one_ref, shift_one_ref, gain_two_ref, shift_two_ref)):
+        own(sums[i + 1 : i + 2], ref, place)
+    bias = jnp.concatenate(
+        [block_ref[g, rows : rows + 1, c * part : (c + 1) * part] for c in range(3) for g in range(4)], 1
+    )
+    own(bias, bqkv_ref, place)
+    own(a_ref[4 * rows + 3 : 4 * rows + 4, :], bias_ref, place)
+    twin_ref[...] = bias_ref[...]
+    own(b_ref[4 * rows : 4 * rows + 1, :], bup_ref, lax.axis_index("dp"))
+
+
+def shards(
+    owners, groups,
+    inputs, cotangent, w_qkv, b_qkv, w_out, b_out, w_up, b_up, w_down, b_down,
+    gain_one, shift_one, gain_two, shift_two,
+):
+    rows, width = w_qkv.shape[0], w_qkv.shape[1] // 3
+    hidden = w_up.shape[1] // groups
+    local = inputs.shape[1]
+    if rows % 16 or groups != 4 or owners != 8 or local != BLOCK or hidden != width:
+        return shards_any(
+            owners, groups, inputs, cotangent, w_qkv, b_qkv, w_out, b_out, w_up, b_up, w_down, b_down,
+            gain_one, shift_one, gain_two, shift_two,
+        )
+    tokens = local * groups
+    part = width // groups
+    devices = owners * groups
+    half = owners // 2
+    heads = part // HD
+    shape = jax.ShapeDtypeStruct
+
+    target = [(f % owners) * groups + f // owners for f in range(devices)]
+
+    block = shape((2, rows, 2 * width + hidden), BF16)
+    params = (w_qkv, w_up, w_out, b_qkv, b_up, b_out, b_down, gain_one, shift_one, gain_two, shift_two)
+    sent, kept = call(
+        pack_kernel,
+        (block, block),
+        [pltpu.VMEM((groups, rows, 2 * width + hidden), BF16), pltpu.SemaphoreType.DMA((len(params),))]
+        + [pltpu.VMEM(p.shape, BF16) for p in params],
+        0, 0, *params, mib=63, far=len(params),
+    )
+    near = exchange(sent, "seq", groups, 0)
+    far = exchange(jnp.stack([kept[1], near[1]]), "seq", groups, 1)
+    first, second = call(
+        payload_kernel,
+        (shape((8 * rows, width), BF16), shape((4 * rows + w_down.shape[0], width), BF16)),
+        [pltpu.SemaphoreType.DMA], 0, 0, kept, near, far, w_down, mib=4, far=1,
+    )
+    def merged(bit, mine, other):
+        count = mine.shape[0] - 4 * rows
+        out = shape((2 * count + 4 * rows, width), BF16)
+        return call(functools.partial(merge_kernel, bit), (out,), [], 0, 0, mine, other, mib=4)[0]
+
+    x = jnp.concatenate([after(inputs[0], far), cotangent[0]], axis=1)[None]
+    x_other = exchange(x, "seq", groups, 1)
+    other = exchange(first, "dp", owners, 2)
+    second = after(second, other)[None]
+    first = merged(2, first, other)
+    other, second_other = exchange(first, "dp", owners, 1), exchange(second, "dp", owners, 2)
+    other, second_other, x_other = lax.optimization_barrier((other, second_other, x_other))
+    first, second = merged(1, first, other), jnp.concatenate([second, second_other], 0)
+    x = jnp.concatenate([x, x_other], 0)
+    first = (first, exchange(first, "dp", owners, 0))
+    x_pair = (x, exchange(x, "seq", groups, 0))
+    second_other = exchange(second, "dp", owners, 1)
+    second = jnp.concatenate([second, after(second_other, first[1])], 0)
+    second = (second, exchange(second, "dp", owners, 0))
+
+    cosine, sine = (jnp.asarray(t) for t in rotary(tokens, heads))
+    column = np.arange(3 * width, dtype=np.int32)
+    own = 3 * width // devices
+    table = np.zeros((8, 3 * width), np.int32)
+    table[0], table[1] = column % own, column // own
+    wide, narrow, turned = shape((tokens, width), BF16), shape((tokens, part), BF16), shape((part, tokens), BF16)
+    xg, normed_a, query, query_t, key, value, grad_att, grad_att_t, full_qkv, full_out, vectors = call(
+        project_kernel,
+        (shape((tokens, 2 * width), BF16), wide, narrow, turned, narrow, narrow, narrow, turned)
+        + (shape((width, 3 * part), BF16), shape((part, width), BF16), shape((8, width), F32)),
+        [], 2 * tokens * width * 4 * part, 0,
+        *first, *x_pair, cosine, sine, jnp.asarray(table),
+    )
+    chunk = 5 * rows
+    attended, grad_proj, sent_a, kept_a = call(
+        attend_kernel,
+        (narrow, shape((tokens, 3 * part), BF16), shape((half, chunk, width), BF16), shape((half, chunk, width), F32)),
+        [
+            pltpu.VMEM((tokens, part), F32),
+            pltpu.VMEM((part, tokens), F32),
+            pltpu.VMEM((part, tokens), F32),
+            pltpu.VMEM((width, 3 * part), F32),
+            pltpu.VMEM((part, width), F32),
+        ],
+        8 * tokens * tokens * part * 6, 2 * tokens * tokens,
+        xg, normed_a, after(query, second_other), query_t, key, value, grad_att, grad_att_t, full_qkv, cosine, sine,
+        mib=16,
+    )
+    other_a = exchange(sent_a, "dp", owners, 0)
+    active, grad_hidden, full_up, full_down, sent_u, kept_u = call(
+        hidden_kernel,
+        (wide, wide, shape((width, hidden), BF16), shape((hidden, width), BF16))
+        + (shape((half, chunk, width), BF16), shape((half, chunk, width), F32)),
+        [
+            pltpu.VMEM((tokens, width), BF16),
+            pltpu.VMEM((width, hidden), F32),
+        ],
+        8 * tokens * width * hidden, 2 * tokens * hidden,
+        *second, xg, after(vectors, attended),
+        mib=16,
+    )
+    other_u = exchange(sent_u, "dp", owners, 0)
+    down_rows = w_down.shape[0]
+    sent_d, kept_d = call(
+        down_kernel,
+        (shape((half, down_rows, width), BF16), shape((half, down_rows, width), F32)),
+        [pltpu.VMEM((hidden, width), F32)],
+        2 * tokens * width * hidden, 0,
+        after(active, other_a), xg,
+    )
+    other_d = exchange(sent_d, "dp", owners, 0)
+    sent_x, kept_x = call(
+        join_kernel,
+        (shape((2, local, 2 * width), BF16), shape((2, local, 2 * width), F32)),
+        [],
+        4 * tokens * width * hidden, 0,
+        xg, attended, full_out, active, full_down, vectors,
+        grad_proj, full_qkv, grad_hidden, full_up,
+    )
+    steps = log2(owners)
+    for bit in range(1, steps):
+        sent_a, kept_a = fold(kept_a, other_a)
+        other_a = exchange(sent_a, "dp", owners, bit)
+    grad_a = finish(kept_a, other_a)
+    other_x = exchange(sent_x, "seq", groups, 0)
+    sent_x, kept_x = fold(kept_x, other_x)
+    other_out = exchange(sent_x[..., :width], "seq", groups, 1)
+    other_grad = exchange(after(sent_x[..., width:], other_out), "seq", groups, 1)
+    outputs = finish(kept_x[..., :width], other_out).astype(BF16)[None]
+    grad_inputs = finish(kept_x[..., width:], other_grad).astype(BF16)[None]
+    for bit in range(1, steps):
+        sent_u, kept_u = fold(kept_u, other_u)
+        sent_u = sent_u if bit == 1 else after(sent_u, other_out)
+        other_u = exchange(sent_u, "dp", owners, bit)
+    grad_u, near_d = finish(kept_u, other_u), None
+    for bit in range(1, steps):
+        sent_d, kept_d = fold(kept_d, other_d)
+        other_d = exchange(sent_d, "dp", owners, bit)
+        near_d = near_d if bit > 1 else other_d
+    grad_d = finish(kept_d, other_d)
+    own_wout = lax.ppermute(
+        grad_a[3 * rows : 4 * rows, :], ("dp", "seq"), [(target[f], f) for f in range(devices)]
+    )
+    block = shape((2, 2 * rows, 3 * part + hidden), BF16)
+    sent, kept = call(deal_kernel, (block, block), [], 0, 0, grad_a, after(grad_u, other_grad, near_d))
+    near = exchange(sent, "seq", groups, 0)
+    far = exchange(jnp.stack([kept[1], near[1]]), "seq", groups, 1)
+    vector = shape((rows,), F32)
+    own_wqkv, own_wup, own_wout, own_bqkv, own_bias, twin_bias, own_bup, *own = call(
+        collect_kernel,
+        (shape(w_qkv.shape, F32), shape(w_up.shape, F32), shape(w_out.shape, F32))
+        + (shape(b_qkv.shape, F32), vector, vector, shape(b_up.shape, F32), vector, vector, vector, vector),
+        [pltpu.VMEM((groups, 2 * rows, 3 * part + hidden), F32)],
+        0, 0, kept, near, far, grad_a, grad_u, own_wout,
+    )
+    return (
+        outputs,
+        grad_inputs,
+        own_wqkv,
+        own_bqkv,
+        own_wout,
+        own_bias,
+        own_wup,
+        own_bup,
+        grad_d,
+        twin_bias,
+        *own,
+    )
+
+
 def solution(mesh):
     rows = P("dp", "seq", None)
     matrix, vector = P(("dp", "seq"), None), P(("dp", "seq"))

time: 142 us -> 106 us (0.75)
  local copies, waits for them, and re-layouts: 19.5 us -> 2.7 us
  waiting for transfers between devices: 57.3 us -> 42 us
  other arithmetic: 10.4 us -> 3.83 us
  starting transfers between devices: 29 us -> 34.3 us
  Pallas kernels: 24.1 us -> 21.7 us
    ppermute x20 -> x24, waiting for transfers between devices: 57.3 us -> 42 us  [exchange(): return lax.ppermute(value, axis, [(i, i ^ 1 << bit) for i in range(size)])]
    ppermute x20 -> x24, starting transfers between devices: 27 us -> 33.7 us  [exchange(): return lax.ppermute(value, axis, [(i, i ^ 1 << bit) for i in range(size)])]
    reshape x16 -> x0, local copies, waits for them, and re-layouts: 5.81 us -> none  [the longest x3 1.18 us: shards(): send[:, :rows, 3 * part:].reshape(groups, rows, owners, -1)]
    broadcast_in_dim x9 -> x0, local copies, waits for them, and re-layouts: 4.48 us -> none  [the longest x6 4.47 us: shards(): v[:, None]]
    select_n x17 -> x0, other arithmetic: 4.34 us -> none  [the longest x13 4.27 us: gather_bits(): jnp.where(upper, jnp.stack([other, value], done), jnp.stack([value, other...]
    pallas_call x2 -> x11, Pallas kernels: 24.1 us -> 21.7 us  [call(): pl.pallas_call(kernel, out_shape=tuple(outs), in_specs=whole(len(operands...]
    slice x23 -> x12, local copies, waits for them, and re-layouts: 3.25 us -> 0.96 us  [the longest x4 0.82 us: shards(): far = exchange(jnp.stack([kept[1], near[1]]), 'seq', groups, 1)]
    add x9, other arithmetic: 2.8 us -> 1.05 us  [the longest x3 0.71 us: finish(): return kept[0] + other[0].astype(F32)]
  transfers between devices with their start and end apart: 22 -> 25, of which waited for: 14 -> 15; matrix products, arithmetic and copies ran while one was open for 11% -> 3% of each run, Pallas kernels for 7% -> 18%
where the time goes in v2:
time: 106 us
  waiting for transfers between devices  42 us (40%)
  starting transfers between devices  34.3 us (32%)
  Pallas kernels  21.7 us (20%)
  other arithmetic  3.83 us (4%)
  local copies, waits for them, and re-layouts  2.7 us (3%)
    ppermute x24, waiting for transfers between devices, exchange(): return lax.ppermute(value, axis, [(i, i ^ 1 << bit) for i in range(size)])  42 us
    ppermute x24, starting transfers between devices, exchange(): return lax.ppermute(value, axis, [(i, i ^ 1 << bit) for i in range(size)])  33.7 us
    pallas_call x11, Pallas kernels, call(): pl.pallas_call(kernel, out_shape=tuple(outs), in_specs=whole(len(operands...  21.7 us
  transfers between devices with their start and end apart: 25, of which 15 were waited for; matrix products, arithmetic and copies ran while one was open for 3% of the time, Pallas kernels for 18%

profile of v2, /device:TPU:0, one launch (start us, length us, event | category | flops | bytes accessed | tf_op | source)
XLA Modules:
  0.0 105.5 jit_solution(10481840165304098752)
XLA Ops:
  4.1 2.9 %collective-permute-start.1 = (bf16[2,16,1536]{2,1,0:T(8,128)(2,1)S(1)}, bf16[2,16,1536]{2,1,0:T(8,128)(2,1)S(1)}, u32[]{:S(2)}, u32[]{:S(2)}) collective-permute-start(bf16[2,16,1536]{2,1,0:T(8,128)(2,1)S(1)} %pad_maximum_fusion.4), channel_id=1, source_target_pairs={{0,2},{1,3},{2,0},{3,1},{4,6},{5,7},{6,4},{7,5},{8,10},{9,11},{10,... | collective-permute-start | bytes 294920 | tf_op jit(solution)/shard_map/ppermute | solution.py:27
  7.0 3.1 %collective-permute-done.1.far_ref = bf16[2,16,1536]{2,1,0:T(8,128)(2,1)S(1)} collective-permute-done((bf16[2,16,1536]{2,1,0:T(8,128)(2,1)S(1)}, bf16[2,16,1536]{2,1,0:T(8,128)(2,1)S(1)}, u32[]{:S(2)}, u32[]{:S(2)}) %collective-permute-start.1) | collective-permute-done | bytes 98336 | tf_op jit(solution)/shard_map/ppermute | solution.py:27
  11.2 1.8 %collective-permute-start.5 = (bf16[1,256,1024]{2,1,0:T(8,128)(2,1)S(1)}, bf16[1,256,1024]{2,1,0:T(8,128)(2,1)S(1)}, u32[]{:S(2)}, u32[]{:S(2)}) collective-permute-start(bf16[1,256,1024]{2,1,0:T(8,128)(2,1)S(1)} %maximum_bitcast_fusion), channel_id=1, source_target_pairs={{0,2},{1,3},{2,0},{3,1},{4,6},{5,7},{6,4},{7,5},{8,10},{9,11},{10,... | collective-permute-start | bytes 1572872 | tf_op jit(solution)/shard_map/ppermute | solution.py:27
  14.9 2.7 %collective-permute-start.2 = (bf16[128,512]{1,0:T(8,128)(2,1)S(1)}, bf16[128,512]{1,0:T(8,128)(2,1)S(1)}, u32[]{:S(2)}, u32[]{:S(2)}) collective-permute-start(bf16[128,512]{1,0:T(8,128)(2,1)S(1)} %get-tuple-element.70.mine_ref), channel_id=1, source_target_pairs={{0,16},{4,20},{8,24},{12,28},{16,0},{20,4},{24,8},{28,12},{1,17},{... | collective-permute-start | bytes 393224 | tf_op jit(solution)/shard_map/ppermute | solution.py:27
  17.5 5.6 %collective-permute-done.2.other_ref = bf16[128,512]{1,0:T(8,128)(2,1)S(1)} collective-permute-done((bf16[128,512]{1,0:T(8,128)(2,1)S(1)}, bf16[128,512]{1,0:T(8,128)(2,1)S(1)}, u32[]{:S(2)}, u32[]{:S(2)}) %collective-permute-start.2) | collective-permute-done | bytes 131104 | tf_op jit(solution)/shard_map/ppermute | solution.py:27
  23.9 3.4 %collective-permute-start.4 = (bf16[1,128,512]{2,1,0:T(8,128)(2,1)S(1)}, bf16[1,128,512]{2,1,0:T(8,128)(2,1)S(1)}, u32[]{:S(2)}, u32[]{:S(2)}) collective-permute-start(bf16[1,128,512]{2,1,0:T(8,128)(2,1)S(1)} %bitcast.14), channel_id=1, source_target_pairs={{0,16},{4,20},{8,24},{12,28},{16,0},{20,4},{24,8},{28,12},{1,17},{... | collective-permute-start | bytes 393224 | tf_op jit(solution)/shard_map/ppermute | solution.py:27
  27.2 3.3 %collective-permute-done.4 = bf16[1,128,512]{2,1,0:T(8,128)(2,1)S(1)} collective-permute-done((bf16[1,128,512]{2,1,0:T(8,128)(2,1)S(1)}, bf16[1,128,512]{2,1,0:T(8,128)(2,1)S(1)}, u32[]{:S(2)}, u32[]{:S(2)}) %collective-permute-start.4) | collective-permute-done | bytes 131104 | tf_op jit(solution)/shard_map/ppermute | solution.py:27
  33.5 3.0 %collective-permute-start.8 = (bf16[2,128,512]{2,1,0:T(8,128)(2,1)S(1)}, bf16[2,128,512]{2,1,0:T(8,128)(2,1)S(1)}, u32[]{:S(2)}, u32[]{:S(2)}) collective-permute-start(bf16[2,128,512]{2,1,0:T(8,128)(2,1)S(1)} %pad_maximum_fusion.2), channel_id=1, source_target_pairs={{0,8},{4,12},{8,0},{12,4},{16,24},{20,28},{24,16},{28,20},{1,9},{5... | collective-permute-start | bytes 786440 | tf_op jit(solution)/shard_map/ppermute | solution.py:27
  36.5 6.7 %collective-permute-done.8 = bf16[2,128,512]{2,1,0:T(8,128)(2,1)S(1)} collective-permute-done((bf16[2,128,512]{2,1,0:T(8,128)(2,1)S(1)}, bf16[2,128,512]{2,1,0:T(8,128)(2,1)S(1)}, u32[]{:S(2)}, u32[]{:S(2)}) %collective-permute-start.8) | collective-permute-done | bytes 262176 | tf_op jit(solution)/shard_map/ppermute | solution.py:27
  43.9 2.1 %shard_map.276 = (bf16[1024,1024]{1,0:T(8,128)(2,1)S(1)}, bf16[1024,512]{1,0:T(8,128)(2,1)S(1)}, bf16[1024,128]{1,0:T(8,128)(2,1)S(1)}, bf16[128,1024]{1,0:T(8,1...) custom-call(bf16[320,512]{1,0:T(8,128)(2,1)S(1)} %shard_map.275.firs, ...), custom_call_target="tpu_custom_call" | custom-call | flops 1 | bytes 1 | tf_op jit(solution)/shard_map/pallas_call | solution.py:497
  46.0 9.7 %shard_map.277 = (bf16[1024,128]{1,0:T(8,128)(2,1)S(1)}, bf16[1024,384]{1,0:T(8,128)(2,1)S(1)}, bf16[4,80,512]{2,1,0:T(8,128)(2,1)S(1)}, f32[4,80,512]{2,1,0:T(8,128)S(1)}) custom-call(bf16[1024,1024]{1,0:T(8,128)(2,1)S(1)} %get-tuple-element.76.xg_ref, bf16[1024,512]{1,0:T(8,128)(2,1)S(1)} %get-tuple-element.77.na_ref, ...), custom_call_target="tpu_custom_call" | custom-call | flops 1 | bytes 1 | tf_op jit(solution)/shard_map/pallas_call | solution.py:497
  57.2 3.9 %shard_map.278 = (bf16[1024,512]{1,0:T(8,128)(2,1)S(1)}, bf16[1024,512]{1,0:T(8,128)(2,1)S(1)}, bf16[512,512]{1,0:T(8,128)(2,1)S(1)}, bf16[512,512]{1,0:T(8,128)...) custom-call(bf16[4,128,512]{2,1,0:T(8,128)(2,1)S(1)} %pad_maximum_fusion.1.second_ref, ...), custom_call_target="tpu_custom_call" | custom-call | flops 1 | bytes 1 | tf_op jit(solution)/shard_map/pallas_call | solution.py:497
  61.7 2.5 %shard_map.279 = (bf16[2,256,1024]{2,1,0:T(8,128)(2,1)S(1)}, f32[2,256,1024]{2,1,0:T(8,128)S(1)}) custom-call(bf16[1024,1024]{1,0:T(8,128)(2,1)S(1)} %get-tuple-element.76.xg_ref, bf16[1024,128]{1,0:T(8,128)(2,1)S(1)} %get-tuple-element.87.att_ref, bf16[128,512]{1,0:T(8,128)(2,1)S(1)} %get-tuple-element.88.wo_ref, ...), custom_call_target="tpu_custom_call" | custom-call | flops 1 | bytes 1 | tf_op jit(solution)/shard_map/pallas_call | solution.py:497
  64.3 2.1 %collective-permute-done.13 = bf16[4,80,512]{2,1,0:T(8,128)(2,1)S(1)} collective-permute-done((bf16[4,80,512]{2,1,0:T(8,128)(2,1)S(1)}, bf16[4,80,512]{2,1,0:T(8,128)(2,1)S(1)}, u32[]{:S(2)}, u32[]{:S(2)}) %collective-permute-start.13) | collective-permute-done | bytes 327712 | tf_op jit(solution)/shard_map/ppermute | solution.py:27
  66.5 2.9 %collective-permute-start.14 = (bf16[2,80,512]{2,1,0:T(8,128)(2,1)S(1)}, bf16[2,80,512]{2,1,0:T(8,128)(2,1)S(1)}, u32[]{:S(2)}, u32[]{:S(2)}) collective-permute-start(bf16[2,80,512]{2,1,0:T(8,128)(2,1)S(1)} %slice.144), channel_id=1, source_target_pairs={{0,8},{4,12},{8,0},{12,4},{16,24},{20,28},{24,16},{28,20},{1,9},{5... | collective-permute-start | bytes 491528 | tf_op jit(solution)/shard_map/ppermute | solution.py:27
  70.8 1.8 %collective-permute-done.16 = bf16[4,80,512]{2,1,0:T(8,128)(2,1)S(1)} collective-permute-done((bf16[4,80,512]{2,1,0:T(8,128)(2,1)S(1)}, bf16[4,80,512]{2,1,0:T(8,128)(2,1)S(1)}, u32[]{:S(2)}, u32[]{:S(2)}) %collective-permute-start.16) | collective-permute-done | bytes 327712 | tf_op jit(solution)/shard_map/ppermute | solution.py:27
  72.7 3.7 %collective-permute-start.17 = (bf16[2,80,512]{2,1,0:T(8,128)(2,1)S(1)}, bf16[2,80,512]{2,1,0:T(8,128)(2,1)S(1)}, u32[]{:S(2)}, u32[]{:S(2)}) collective-permute-start(bf16[2,80,512]{2,1,0:T(8,128)(2,1)S(1)} %slice.143), channel_id=1, source_target_pairs={{0,8},{4,12},{8,0},{12,4},{16,24},{20,28},{24,16},{28,20},{1,9},{5... | collective-permute-start | bytes 491528 | tf_op jit(solution)/shard_map/ppermute | solution.py:27
  76.4 1.8 %collective-permute-start.15 = (bf16[1,80,512]{2,1,0:T(8,128)(2,1)S(1)}, bf16[1,80,512]{2,1,0:T(8,128)(2,1)S(1)}, u32[]{:S(2)}, u32[]{:S(2)}) collective-permute-start(bf16[1,80,512]{2,1,0:T(8,128)(2,1)S(1)} %slice.147), channel_id=1, source_target_pairs={{0,16},{4,20},{8,24},{12,28},{16,0},{20,4},{24,8},{28,12},{1,17},{... | collective-permute-start | bytes 245768 | tf_op jit(solution)/shard_map/ppermute | solution.py:27
  78.3 1.8 %collective-permute-done.17 = bf16[2,80,512]{2,1,0:T(8,128)(2,1)S(1)} collective-permute-done((bf16[2,80,512]{2,1,0:T(8,128)(2,1)S(1)}, bf16[2,80,512]{2,1,0:T(8,128)(2,1)S(1)}, u32[]{:S(2)}, u32[]{:S(2)}) %collective-permute-start.17) | collective-permute-done | bytes 163872 | tf_op jit(solution)/shard_map/ppermute | solution.py:27
  80.1 2.6 %collective-permute-done.15 = bf16[1,80,512]{2,1,0:T(8,128)(2,1)S(1)} collective-permute-done((bf16[1,80,512]{2,1,0:T(8,128)(2,1)S(1)}, bf16[1,80,512]{2,1,0:T(8,128)(2,1)S(1)}, u32[]{:S(2)}, u32[]{:S(2)}) %collective-permute-start.15) | collective-permute-done | bytes 81952 | tf_op jit(solution)/shard_map/ppermute | solution.py:27
  84.7 5.1 %collective-permute-done.11 = bf16[1,256,512]{2,1,0:T(8,128)(2,1)S(1)} collective-permute-done((bf16[1,256,512]{2,1,0:T(8,128)(2,1)S(1)}, bf16[1,256,512]{2,1,0:T(8,128)(2,1)S(1)}, u32[]{:S(2)}, u32[]{:S(2)}) %collective-permute-start.11) | collective-permute-done | bytes 262176 | tf_op jit(solution)/shard_map/ppermute | solution.py:27
  91.2 2.0 %collective-permute-start.24 = (bf16[1,64,512]{2,1,0:T(8,128)(2,1)S(1)}, bf16[1,64,512]{2,1,0:T(8,128)(2,1)S(1)}, u32[]{:S(2)}, u32[]{:S(2)}) collective-permute-start(bf16[1,64,512]{2,1,0:T(8,128)(2,1)S(1)} %slice.148), channel_id=1, source_target_pairs={{0,16},{4,20},{8,24},{12,28},{16,0},{20,4},{24,8},{28,12},{1,17},{... | collective-permute-start | bytes 196616 | tf_op jit(solution)/shard_map/ppermute | solution.py:27
  93.2 4.7 %collective-permute-done.18 = bf16[1,80,512]{2,1,0:T(8,128)(2,1)S(1)} collective-permute-done((bf16[1,80,512]{2,1,0:T(8,128)(2,1)S(1)}, bf16[1,80,512]{2,1,0:T(8,128)(2,1)S(1)}, u32[]{:S(2)}, u32[]{:S(2)}) %collective-permute-start.18) | collective-permute-done | bytes 81952 | tf_op jit(solution)/shard_map/ppermute | solution.py:27
  101.6 3.1 %collective-permute-done.22.far_ref = bf16[2,32,896]{2,1,0:T(8,128)(2,1)S(1)} collective-permute-done((bf16[2,32,896]{2,1,0:T(8,128)(2,1)S(1)}, bf16[2,32,896]{2,1,0:T(8,128)(2,1)S(1)}, u32[]{:S(2)}, u32[]{:S(2)}) %collective-permute-start.22) | collective-permute-done | bytes 114720 | tf_op jit(solution)/shard_map/ppermute | solution.py:27
  (76 shorter events, 22.5 us)
Async XLA Ops:
  2.4 1.7 %collective-permute-start = (bf16[2,16,1536]{2,1,0:T(8,128)(2,1)}, bf16[2,16,1536]{2,1,0:T(8,128)(2,1)S(1)}, u32[]{:S(2)}, u32[]{:S(2)}) collective-permute-start(bf16[2,16,1536]{2,1,0:T(8,128)(2,1)} %get-tuple-element.69), channel_id=1, source_target_pairs={{0,1},{1,0},{2,3},{3,2},{4,5},{5,4},{6,7},{7,6},{8,9},{9,8},{10,11... | collective-permute-start | bytes 294920 | tf_op jit(solution)/shard_map/ppermute | solution.py:27
  4.1 6.1 %collective-permute-start.1 = (bf16[2,16,1536]{2,1,0:T(8,128)(2,1)S(1)}, bf16[2,16,1536]{2,1,0:T(8,128)(2,1)S(1)}, u32[]{:S(2)}, u32[]{:S(2)}) collective-permute-start(bf16[2,16,1536]{2,1,0:T(8,128)(2,1)S(1)} %pad_maximum_fusion.4), channel_id=1, source_target_pairs={{0,2},{1,3},{2,0},{3,1},{4,6},{5,7},{6,4},{7,5},{8,10},{9,11},{10,... | collective-permute-start | bytes 294920 | tf_op jit(solution)/shard_map/ppermute | solution.py:27
  11.2 20.5 %collective-permute-start.5 = (bf16[1,256,1024]{2,1,0:T(8,128)(2,1)S(1)}, bf16[1,256,1024]{2,1,0:T(8,128)(2,1)S(1)}, u32[]{:S(2)}, u32[]{:S(2)}) collective-permute-start(bf16[1,256,1024]{2,1,0:T(8,128)(2,1)S(1)} %maximum_bitcast_fusion), channel_id=1, source_target_pairs={{0,2},{1,3},{2,0},{3,1},{4,6},{5,7},{6,4},{7,5},{8,10},{9,11},{10,... | collective-permute-start | bytes 1572872 | tf_op jit(solution)/shard_map/ppermute | solution.py:27
  14.9 8.2 %collective-permute-start.2 = (bf16[128,512]{1,0:T(8,128)(2,1)S(1)}, bf16[128,512]{1,0:T(8,128)(2,1)S(1)}, u32[]{:S(2)}, u32[]{:S(2)}) collective-permute-start(bf16[128,512]{1,0:T(8,128)(2,1)S(1)} %get-tuple-element.70.mine_ref), channel_id=1, source_target_pairs={{0,16},{4,20},{8,24},{12,28},{16,0},{20,4},{24,8},{28,12},{1,17},{... | collective-permute-start | bytes 393224 | tf_op jit(solution)/shard_map/ppermute | solution.py:27
  23.1 8.6 %collective-permute-start.3 = (bf16[192,512]{1,0:T(8,128)(2,1)S(1)}, bf16[192,512]{1,0:T(8,128)(2,1)S(1)}, u32[]{:S(2)}, u32[]{:S(2)}) collective-permute-start(bf16[192,512]{1,0:T(8,128)(2,1)S(1)} %shard_map.274.mine_ref), channel_id=1, source_target_pairs={{0,8},{4,12},{8,0},{12,4},{16,24},{20,28},{24,16},{28,20},{1,9},{5... | collective-permute-start | bytes 589832 | tf_op jit(solution)/shard_map/ppermute | solution.py:27
  23.9 6.7 %collective-permute-start.4 = (bf16[1,128,512]{2,1,0:T(8,128)(2,1)S(1)}, bf16[1,128,512]{2,1,0:T(8,128)(2,1)S(1)}, u32[]{:S(2)}, u32[]{:S(2)}) collective-permute-start(bf16[1,128,512]{2,1,0:T(8,128)(2,1)S(1)} %bitcast.14), channel_id=1, source_target_pairs={{0,16},{4,20},{8,24},{12,28},{16,0},{20,4},{24,8},{28,12},{1,17},{... | collective-permute-start | bytes 393224 | tf_op jit(solution)/shard_map/ppermute | solution.py:27
  31.8 12.0 %collective-permute-start.7 = (bf16[2,256,1024]{2,1,0:T(8,128)(2,1)S(1)}, bf16[2,256,1024]{2,1,0:T(8,128)(2,1)S(1)}, u32[]{:S(2)}, u32[]{:S(2)}) collective-permute-start(bf16[2,256,1024]{2,1,0:T(8,128)(2,1)S(1)} %pad_maximum_fusion.x_ref), channel_id=1, source_target_pairs={{0,1},{1,0},{2,3},{3,2},{4,5},{5,4},{6,7},{7,6},{8,9},{9,8},{10,11... | collective-permute-start | bytes 3145736 | tf_op jit(solution)/shard_map/ppermute | solution.py:27
  32.0 11.2 %collective-permute-start.6 = (bf16[320,512]{1,0:T(8,128)(2,1)S(1)}, bf16[320,512]{1,0:T(8,128)(2,1)S(1)}, u32[]{:S(2)}, u32[]{:S(2)}) collective-permute-start(bf16[320,512]{1,0:T(8,128)(2,1)S(1)} %shard_map.275.first_ref), channel_id=1, source_target_pairs={{0,4},{4,0},{8,12},{12,8},{16,20},{20,16},{24,28},{28,24},{1,5},{5... | collective-permute-start | bytes 983048 | tf_op jit(solution)/shard_map/ppermute | solution.py:27
  33.5 9.7 %collective-permute-start.8 = (bf16[2,128,512]{2,1,0:T(8,128)(2,1)S(1)}, bf16[2,128,512]{2,1,0:T(8,128)(2,1)S(1)}, u32[]{:S(2)}, u32[]{:S(2)}) collective-permute-start(bf16[2,128,512]{2,1,0:T(8,128)(2,1)S(1)} %pad_maximum_fusion.2), channel_id=1, source_target_pairs={{0,8},{4,12},{8,0},{12,4},{16,24},{20,28},{24,16},{28,20},{1,9},{5... | collective-permute-start | bytes 786440 | tf_op jit(solution)/shard_map/ppermute | solution.py:27
  43.3 14.0 %collective-permute-start.9 = (bf16[4,128,512]{2,1,0:T(8,128)(2,1)S(1)}, bf16[4,128,512]{2,1,0:T(8,128)(2,1)S(1)}, u32[]{:S(2)}, u32[]{:S(2)}) collective-permute-start(bf16[4,128,512]{2,1,0:T(8,128)(2,1)S(1)} %pad_maximum_fusion.1.second_ref), channel_id=1, source_target_pairs={{0,4},{4,0},{8,12},{12,8},{16,20},{20,16},{24,28},{28,24},{1,5},{5... | collective-permute-start | bytes 1572872 | tf_op jit(solution)/shard_map/ppermute | solution.py:27
  55.7 10.7 %collective-permute-start.13 = (bf16[4,80,512]{2,1,0:T(8,128)(2,1)S(1)}, bf16[4,80,512]{2,1,0:T(8,128)(2,1)S(1)}, u32[]{:S(2)}, u32[]{:S(2)}) collective-permute-start(bf16[4,80,512]{2,1,0:T(8,128)(2,1)S(1)} %get-tuple-element.101), channel_id=1, source_target_pairs={{0,4},{4,0},{8,12},{12,8},{16,20},{20,16},{24,28},{28,24},{1,5},{5... | collective-permute-start | bytes 983048 | tf_op jit(solution)/shard_map/ppermute | solution.py:27
  61.1 11.4 %collective-permute-start.16 = (bf16[4,80,512]{2,1,0:T(8,128)(2,1)S(1)}, bf16[4,80,512]{2,1,0:T(8,128)(2,1)S(1)}, u32[]{:S(2)}, u32[]{:S(2)}) collective-permute-start(bf16[4,80,512]{2,1,0:T(8,128)(2,1)S(1)} %get-tuple-element.103), channel_id=1, source_target_pairs={{0,4},{4,0},{8,12},{12,8},{16,20},{20,16},{24,28},{28,24},{1,5},{5... | collective-permute-start | bytes 983048 | tf_op jit(solution)/shard_map/ppermute | solution.py:27
  64.2 18.5 %collective-permute-start.10 = (bf16[2,256,1024]{2,1,0:T(8,128)(2,1)S(1)}, bf16[2,256,1024]{2,1,0:T(8,128)(2,1)S(1)}, u32[]{:S(2)}, u32[]{:S(2)}) collective-permute-start(bf16[2,256,1024]{2,1,0:T(8,128)(2,1)S(1)} %get-tuple-element.98), channel_id=1, source_target_pairs={{0,1},{1,0},{2,3},{3,2},{4,5},{5,4},{6,7},{7,6},{8,9},{9,8},{10,11... | collective-permute-start | bytes 3145736 | tf_op jit(solution)/shard_map/ppermute | solution.py:27
  66.5 9.9 %collective-permute-start.14 = (bf16[2,80,512]{2,1,0:T(8,128)(2,1)S(1)}, bf16[2,80,512]{2,1,0:T(8,128)(2,1)S(1)}, u32[]{:S(2)}, u32[]{:S(2)}) collective-permute-start(bf16[2,80,512]{2,1,0:T(8,128)(2,1)S(1)} %slice.144), channel_id=1, source_target_pairs={{0,8},{4,12},{8,0},{12,4},{16,24},{20,28},{24,16},{28,20},{1,9},{5... | collective-permute-start | bytes 491528 | tf_op jit(solution)/shard_map/ppermute | solution.py:27
  70.2 13.7 %collective-permute-start.19 = (bf16[4,64,512]{2,1,0:T(8,128)(2,1)S(1)}, bf16[4,64,512]{2,1,0:T(8,128)(2,1)S(1)}, u32[]{:S(2)}, u32[]{:S(2)}) collective-permute-start(bf16[4,64,512]{2,1,0:T(8,128)(2,1)S(1)} %get-tuple-element.107), channel_id=1, source_target_pairs={{0,4},{4,0},{8,12},{12,8},{16,20},{20,16},{24,28},{28,24},{1,5},{5... | collective-permute-start | bytes 786440 | tf_op jit(solution)/shard_map/ppermute | solution.py:27
  72.7 7.3 %collective-permute-start.17 = (bf16[2,80,512]{2,1,0:T(8,128)(2,1)S(1)}, bf16[2,80,512]{2,1,0:T(8,128)(2,1)S(1)}, u32[]{:S(2)}, u32[]{:S(2)}) collective-permute-start(bf16[2,80,512]{2,1,0:T(8,128)(2,1)S(1)} %slice.143), channel_id=1, source_target_pairs={{0,8},{4,12},{8,0},{12,4},{16,24},{20,28},{24,16},{28,20},{1,9},{5... | collective-permute-start | bytes 491528 | tf_op jit(solution)/shard_map/ppermute | solution.py:27
  76.4 6.2 %collective-permute-start.15 = (bf16[1,80,512]{2,1,0:T(8,128)(2,1)S(1)}, bf16[1,80,512]{2,1,0:T(8,128)(2,1)S(1)}, u32[]{:S(2)}, u32[]{:S(2)}) collective-permute-start(bf16[1,80,512]{2,1,0:T(8,128)(2,1)S(1)} %slice.147), channel_id=1, source_target_pairs={{0,16},{4,20},{8,24},{12,28},{16,0},{20,4},{24,8},{28,12},{1,17},{... | collective-permute-start | bytes 245768 | tf_op jit(solution)/shard_map/ppermute | solution.py:27
  83.3 6.4 %collective-permute-start.11 = (bf16[1,256,512]{2,1,0:T(8,128)(2,1)S(1)}, bf16[1,256,512]{2,1,0:T(8,128)(2,1)S(1)}, u32[]{:S(2)}, u32[]{:S(2)}) collective-permute-start(bf16[1,256,512]{2,1,0:T(8,128)(2,1)S(1)} %get-tuple-element.127), channel_id=1, source_target_pairs={{0,2},{1,3},{2,0},{3,1},{4,6},{5,7},{6,4},{7,5},{8,10},{9,11},{10,... | collective-permute-start | bytes 786440 | tf_op jit(solution)/shard_map/ppermute | solution.py:27
  83.9 7.2 %collective-permute-start.20 = (bf16[2,64,512]{2,1,0:T(8,128)(2,1)S(1)}, bf16[2,64,512]{2,1,0:T(8,128)(2,1)S(1)}, u32[]{:S(2)}, u32[]{:S(2)}) collective-permute-start(bf16[2,64,512]{2,1,0:T(8,128)(2,1)S(1)} %slice.145), channel_id=1, source_target_pairs={{0,8},{4,12},{8,0},{12,4},{16,24},{20,28},{24,16},{28,20},{1,9},{5... | collective-permute-start | bytes 393224 | tf_op jit(solution)/shard_map/ppermute | solution.py:27
  84.0 17.5 %collective-permute-start.23 = (f32[16,512]{1,0:T(8,128)S(1)}, f32[16,512]{1,0:T(8,128)S(1)}, u32[]{:S(2)}, u32[]{:S(2)}) collective-permute-start(f32[16,512]{1,0:T(8,128)S(1)} %slice_bitcast_fusion), channel_id=1, source_target_pairs={{0,0},{4,1},{8,2},{12,3},{16,4},{20,5},{24,6},{28,7},{1,8},{5,9},{... | collective-permute-start | bytes 98312 | tf_op jit(solution)/shard_map/ppermute | solution.py:1044
  89.7 8.2 %collective-permute-start.18 = (bf16[1,80,512]{2,1,0:T(8,128)(2,1)S(1)}, bf16[1,80,512]{2,1,0:T(8,128)(2,1)S(1)}, u32[]{:S(2)}, u32[]{:S(2)}) collective-permute-start(bf16[1,80,512]{2,1,0:T(8,128)(2,1)S(1)} %slice.146), channel_id=1, source_target_pairs={{0,16},{4,20},{8,24},{12,28},{16,0},{20,4},{24,8},{28,12},{1,17},{... | collective-permute-start | bytes 245768 | tf_op jit(solution)/shard_map/ppermute | solution.py:27
  91.1 6.8 %collective-permute-start.12 = (bf16[1,256,512]{2,1,0:T(8,128)(2,1)S(1)}, bf16[1,256,512]{2,1,0:T(8,128)(2,1)S(1)}, u32[]{:S(2)}, u32[]{:S(2)}) collective-permute-start(bf16[1,256,512]{2,1,0:T(8,128)(2,1)S(1)} %get-tuple-element.99), channel_id=1, source_target_pairs={{0,2},{1,3},{2,0},{3,1},{4,6},{5,7},{6,4},{7,5},{8,10},{9,11},{10,... | collective-permute-start | bytes 786440 | tf_op jit(solution)/shard_map/ppermute | solution.py:27
  91.2 7.4 %collective-permute-start.24 = (bf16[1,64,512]{2,1,0:T(8,128)(2,1)S(1)}, bf16[1,64,512]{2,1,0:T(8,128)(2,1)S(1)}, u32[]{:S(2)}, u32[]{:S(2)}) collective-permute-start(bf16[1,64,512]{2,1,0:T(8,128)(2,1)S(1)} %slice.148), channel_id=1, source_target_pairs={{0,16},{4,20},{8,24},{12,28},{16,0},{20,4},{24,8},{28,12},{1,17},{... | collective-permute-start | bytes 196616 | tf_op jit(solution)/shard_map/ppermute | solution.py:27
  99.4 5.3 %collective-permute-start.22 = (bf16[2,32,896]{2,1,0:T(8,128)(2,1)S(1)}, bf16[2,32,896]{2,1,0:T(8,128)(2,1)S(1)}, u32[]{:S(2)}, u32[]{:S(2)}) collective-permute-start(bf16[2,32,896]{2,1,0:T(8,128)(2,1)S(1)} %pad_maximum_fusion.3), channel_id=1, source_target_pairs={{0,2},{1,3},{2,0},{3,1},{4,6},{5,7},{6,4},{7,5},{8,10},{9,11},{10,... | collective-permute-start | bytes 344072 | tf_op jit(solution)/shard_map/ppermute | solution.py:27
  (6 other events, 63.2 us)

commit v3 on v2

--- a/solution.py
+++ b/solution.py
@@ -515,8 +515,15 @@
 
 
 def pack_kernel(*refs):
-    count = (len(refs) - 4) // 2
-    (sent_ref, kept_ref, block_ref, sems), held = refs[count : count + 4], refs[count + 4 :]
+    x_ref, g_ref, refs = refs[0], refs[1], refs[2:]
+    count = (len(refs) - 5) // 2
+    (sent_ref, kept_ref, both_ref, block_ref, sems), held = refs[count : count + 5], refs[count + 5 :]
+    joined = [
+        pltpu.make_async_copy(ref, both_ref.at[:, :, pl.ds(i * ref.shape[2], ref.shape[2])], sems.at[count + i])
+        for i, ref in enumerate((x_ref, g_ref))
+    ]
+    for copy in joined:
+        copy.start()
     fetch(tuple(zip(refs[:count], held)), sems)
     qkv_ref, up_ref, out_ref, small = held[0], held[1], held[2], held[3:]
     me = lax.axis_index("seq")
@@ -547,6 +554,8 @@
     for half in range(groups // 2):
         kept_ref[half] = block_ref[me ^ (2 * half)]
         sent_ref[half] = block_ref[me ^ (2 * half + 1)]
+    for copy in joined:
+        copy.wait()
 
 
 def payload_kernel(kept_ref, near_ref, far_ref, down_ref, first_ref, second_ref, sem):
@@ -556,31 +565,36 @@
     copy = pltpu.make_async_copy(down_ref, second_ref.at[pl.ds(4 * rows, down_ref.shape[0])], sem)
     copy.start()
     hidden = kept_ref.shape[2] - 2 * width
+    index = lax.broadcasted_iota(jnp.int32, (rows, part), 0)
+    mine = index // 2 == lax.axis_index("dp")
     for step, block in enumerate((kept_ref.at[0], near_ref.at[0], far_ref.at[0], far_ref.at[1])):
         group = me ^ step
         lanes = pl.ds(pl.multiple_of(group * part, part), part)
         second_ref[pl.ds(pl.multiple_of(group * rows, rows), rows), :] = block[:, width : width + hidden]
         for c in range(3):
             first_ref[c * rows : (c + 1) * rows, lanes] = block[:, c * part : (c + 1) * part]
-        first_ref[3 * rows : 4 * rows, lanes] = block[:, 3 * part : width]
+        line = block[:, 3 * part : width].astype(F32)
+        line = jnp.where(index % 2 == 0, line[0:1], line[1:2])
+        first_ref[3 * rows : 4 * rows, lanes] = jnp.where(mine, line, 0.0).astype(BF16)
         first_ref[pl.ds(pl.multiple_of((4 + group) * rows, rows), rows), :] = block[:, width + hidden :]
     copy.wait()
 
 
-def merge_kernel(bit, mine_ref, other_ref, out_ref):
-    last = mine_ref.shape[0] * 2 - out_ref.shape[0]
-    part = mine_ref.shape[0] - last
+def merge_kernel(bit, rows, mine_ref, other_ref, out_ref):
+    part = mine_ref.shape[0] - 5 * rows
+    small, last = slice(part, part + rows), slice(part + rows, part + 5 * rows)
     out_ref[:part, :] = mine_ref[:part, :]
     out_ref[part : 2 * part, :] = other_ref[:part, :]
+    out_ref[2 * part : 2 * part + rows, :] = mine_ref[small, :] + other_ref[small, :]
     same = (lax.axis_index("dp") >> bit) & 1 == (lax.axis_index("seq") >> (bit - 1)) & 1
 
     @pl.when(same)
     def _():
-        out_ref[2 * part :, :] = mine_ref[part:, :]
+        out_ref[2 * part + rows :, :] = mine_ref[last, :]
 
     @pl.when(jnp.logical_not(same))
     def _():
-        out_ref[2 * part :, :] = other_ref[part:, :]
+        out_ref[2 * part + rows :, :] = other_ref[last, :]
 
 
 def sources(pair, me):
@@ -599,36 +613,39 @@
     width = first_ref.shape[1]
     groups = 2 * x_ref.shape[0]
     part = width // groups
-    rows = first_ref.shape[0] // 20
+    rows = first_ref.shape[0] // 17
     owners = width // (rows * groups)
     local = x_ref.shape[1]
-    lines = []
     for slot in range(owners):
-        block = (first_ref, other_ref)[slot // 4].at[pl.ds(slot % 4 * 4 * rows, 4 * rows)]
+        block = (first_ref, other_ref)[slot // 4].at[pl.ds(slot % 4 * 3 * rows, 3 * rows)]
         rank = owner ^ reversed_bits(slot, log2(owners))
         for g in range(groups):
             lanes = slice(g * part, (g + 1) * part)
             to = pl.ds(pl.multiple_of((rank * groups + g) * rows, rows), rows)
             for c in range(3):
                 wq_ref[to, c * part : (c + 1) * part] = block[c * rows : (c + 1) * rows, lanes]
-            lines.append(block[3 * rows : 4 * rows, lanes].astype(F32)[:8, :])
     for slot, ref in enumerate((first_ref, other_ref)):
         x = (owner & 1) ^ slot
-        wo_ref[pl.ds(pl.multiple_of(x * 4 * rows, 4 * rows), 4 * rows), :] = ref[16 * rows :, :]
+        wo_ref[pl.ds(pl.multiple_of(x * 4 * rows, 4 * rows), 4 * rows), :] = ref[13 * rows :, :]
     devices = owners * groups
-    line_one = jnp.concatenate([line[0:1] for line in lines], 0).astype(BF16)
-    line_two = jnp.concatenate([line[1:2] for line in lines], 0).astype(BF16)
-
-    def device_of(shape):
-        slot = lax.broadcasted_iota(jnp.int32, shape, 0)
-        rank = owner ^ reversed_bits(slot // groups, log2(owners))
-        return rank * groups + slot % groups
+    small = first_ref[12 * rows : 13 * rows, :].astype(F32) + other_ref[12 * rows : 13 * rows, :].astype(F32)
+    line_one, line_two = (
+        jnp.concatenate(
+            [
+                small[2 * rank + i : 2 * rank + i + 1, g * part : (g + 1) * part]
+                for rank in range(owners)
+                for g in range(groups)
+            ],
+            0,
+        ).astype(BF16)
+        for i in range(2)
+    )
 
     def place_values(line, lane_of, device_of_column):
         columns = lane_of.shape[1]
         pick = lax.broadcasted_iota(jnp.int32, (line.shape[1], columns), 0) == lane_of
         values = dot(line, jnp.where(pick, 1.0, 0.0).astype(BF16))
-        held = device_of((devices, columns)) == device_of_column
+        held = lax.broadcasted_iota(jnp.int32, (devices, columns), 0) == device_of_column
         return jnp.sum(jnp.where(held, values, 0.0), axis=0, keepdims=True)
 
     column = lax.broadcasted_iota(jnp.int32, (1, width), 1)
@@ -682,7 +699,7 @@
 
 def attend_kernel(
     xg_ref, na_ref, q_ref, qt_ref, k_ref, v_ref, da_ref, dat_ref, wq_ref, cos_ref, sin_ref,
-    att_ref, dp_ref, sent_ref, kept_ref,
+    att_ref, dp_ref, small_ref, sent_ref, kept_ref,
     dq_ref, dkt_ref, dvt_ref, gq_ref, go_ref,
 ):
     owner = lax.axis_index("dp")
@@ -753,10 +770,10 @@
 
     gq_ref[...] = dot_rows(na_ref[...], dp_ref[...])
     go_ref[...] = dot_rows(att_ref[...], xg_ref[:, width:])
-    tail = jnp.concatenate(
+    small_ref[...] = jnp.concatenate(
         [jnp.concatenate([grad_bias, jnp.zeros((1, width - 3 * part), F32)], 1)]
         + vectors
-        + [jnp.zeros((rows - 4, width), F32)],
+        + [jnp.zeros((4, width), F32)],
         0,
     )
     for ref, rank in sources((kept_ref, sent_ref), owner):
@@ -767,12 +784,11 @@
                 ref[c * rows : (c + 1) * rows, g * part : (g + 1) * part] = gq_ref[
                     at, c * part : (c + 1) * part
                 ].astype(kind)
-        ref[3 * rows : 4 * rows, :] = go_ref[pl.ds(pl.multiple_of(rank * rows, rows), rows), :].astype(kind)
-        ref[4 * rows :, :] = tail.astype(kind)
+        ref[3 * rows : 4 * rows, :] = go_ref[pl.ds(pl.multiple_of((rank % 2 * 4 + rank // 2) * rows, rows), rows), :].astype(kind)
 
 
 def hidden_kernel(
-    second_ref, other_ref, xg_ref, vec_ref,
+    second_ref, other_ref, xg_ref, vec_ref, small_ref,
     act_ref, dh_ref, up_ref, down_ref, sent_ref, kept_ref,
     nb_ref, gu_ref,
 ):
@@ -804,7 +820,7 @@
         vectors[1] += jnp.sum(upstream, axis=0, keepdims=True)
     gu_ref[...] = dot_rows(nb_ref[...], dh_ref[...])
     extra = sent_ref.shape[1] - rows
-    tail = jnp.concatenate([grad_bias] + vectors + [jnp.zeros((extra - 3, width), F32)], 0)
+    tail = jnp.concatenate([grad_bias] + vectors + [small_ref[:4, :], jnp.zeros((extra - 7, width), F32)], 0)
     for ref, rank in sources((kept_ref, sent_ref), owner):
         ref[:rows, :] = gu_ref[pl.ds(pl.multiple_of(rank * rows, rows), rows), :].astype(ref.dtype)
         ref[rows:, :] = tail.astype(ref.dtype)
@@ -845,10 +861,10 @@
     me = lax.axis_index("seq")
     width = a_ref.shape[1]
     part = width // 4
-    rows = a_ref.shape[0] // 5
+    rows = a_ref.shape[0] // 4
     kind = sent_ref.dtype
     small = jnp.concatenate(
-        [a_ref[4 * rows : 4 * rows + 3, :], b_ref[4 * rows + 1 : 4 * rows + 3, :], jnp.zeros((rows - 5, width), F32)], 0
+        [b_ref[4 * rows + 3 : 4 * rows + 6, :], b_ref[4 * rows + 1 : 4 * rows + 3, :], jnp.zeros((rows - 5, width), F32)], 0
     )
     for step in range(4):
         group = me ^ step
@@ -862,8 +878,8 @@
 
 
 def collect_kernel(
-    kept_ref, near_ref, far_ref, a_ref, b_ref, out_ref,
-    qkv_ref, up_ref, wout_ref, bqkv_ref, bias_ref, twin_ref, bup_ref, gain_one_ref, shift_one_ref, gain_two_ref, shift_two_ref,
+    kept_ref, near_ref, far_ref, b_ref, out_ref, down_kept_ref, down_other_ref,
+    qkv_ref, up_ref, wout_ref, bqkv_ref, bias_ref, twin_ref, bup_ref, gain_one_ref, shift_one_ref, gain_two_ref, shift_two_ref, down_ref,
     block_ref,
 ):
     me = lax.axis_index("seq")
@@ -885,6 +901,7 @@
             [block_ref[g, :rows, start : start + piece] for g in range(4)], 1
         )
     wout_ref[...] = out_ref[...]
+    down_ref[...] = down_kept_ref[0] + down_other_ref[0].astype(F32)
 
     def own(values, ref, index):
         size, count = values.shape[1], ref.shape[0]
@@ -898,7 +915,7 @@
         [block_ref[g, rows : rows + 1, c * part : (c + 1) * part] for c in range(3) for g in range(4)], 1
     )
     own(bias, bqkv_ref, place)
-    own(a_ref[4 * rows + 3 : 4 * rows + 4, :], bias_ref, place)
+    own(b_ref[4 * rows + 6 : 4 * rows + 7, :], bias_ref, place)
     twin_ref[...] = bias_ref[...]
     own(b_ref[4 * rows : 4 * rows + 1, :], bup_ref, lax.axis_index("dp"))
 
@@ -923,16 +940,16 @@
     heads = part // HD
     shape = jax.ShapeDtypeStruct
 
-    target = [(f % owners) * groups + f // owners for f in range(devices)]
+    target = [(f % 4 * 2 + f // 4 % 2) * groups + f // owners for f in range(devices)]
 
     block = shape((2, rows, 2 * width + hidden), BF16)
     params = (w_qkv, w_up, w_out, b_qkv, b_up, b_out, b_down, gain_one, shift_one, gain_two, shift_two)
-    sent, kept = call(
+    sent, kept, x = call(
         pack_kernel,
-        (block, block),
-        [pltpu.VMEM((groups, rows, 2 * width + hidden), BF16), pltpu.SemaphoreType.DMA((len(params),))]
+        (block, block, shape((1, local, 2 * width), BF16)),
+        [pltpu.VMEM((groups, rows, 2 * width + hidden), BF16), pltpu.SemaphoreType.DMA((len(params) + 2,))]
         + [pltpu.VMEM(p.shape, BF16) for p in params],
-        0, 0, *params, mib=63, far=len(params),
+        0, 0, inputs, cotangent, *params, mib=63, far=len(params) + 2,
     )
     near = exchange(sent, "seq", groups, 0)
     far = exchange(jnp.stack([kept[1], near[1]]), "seq", groups, 1)
@@ -942,11 +959,10 @@
         [pltpu.SemaphoreType.DMA], 0, 0, kept, near, far, w_down, mib=4, far=1,
     )
     def merged(bit, mine, other):
-        count = mine.shape[0] - 4 * rows
-        out = shape((2 * count + 4 * rows, width), BF16)
-        return call(functools.partial(merge_kernel, bit), (out,), [], 0, 0, mine, other, mib=4)[0]
-
-    x = jnp.concatenate([after(inputs[0], far), cotangent[0]], axis=1)[None]
+        out = shape((2 * mine.shape[0] - 5 * rows, width), BF16)
+        return call(functools.partial(merge_kernel, bit, rows), (out,), [], 0, 0, mine, other, mib=4)[0]
+
+    x = after(x, far)
     x_other = exchange(x, "seq", groups, 1)
     other = exchange(first, "dp", owners, 2)
     second = after(second, other)[None]
@@ -958,8 +974,6 @@
     first = (first, exchange(first, "dp", owners, 0))
     x_pair = (x, exchange(x, "seq", groups, 0))
     second_other = exchange(second, "dp", owners, 1)
-    second = jnp.concatenate([second, after(second_other, first[1])], 0)
-    second = (second, exchange(second, "dp", owners, 0))
 
     cosine, sine = (jnp.asarray(t) for t in rotary(tokens, heads))
     column = np.arange(3 * width, dtype=np.int32)
@@ -974,10 +988,13 @@
         [], 2 * tokens * width * 4 * part, 0,
         *first, *x_pair, cosine, sine, jnp.asarray(table),
     )
+    second = jnp.concatenate([second, after(second_other, normed_a)], 0)
+    second = (second, exchange(second, "dp", owners, 0))
     chunk = 5 * rows
-    attended, grad_proj, sent_a, kept_a = call(
+    attended, grad_proj, small, sent_a, kept_a = call(
         attend_kernel,
-        (narrow, shape((tokens, 3 * part), BF16), shape((half, chunk, width), BF16), shape((half, chunk, width), F32)),
+        (narrow, shape((tokens, 3 * part), BF16), shape((8, width), F32))
+        + (shape((half, 4 * rows, width), BF16), shape((half, 4 * rows, width), F32)),
         [
             pltpu.VMEM((tokens, part), F32),
             pltpu.VMEM((part, tokens), F32),
@@ -999,19 +1016,12 @@
             pltpu.VMEM((width, hidden), F32),
         ],
         8 * tokens * width * hidden, 2 * tokens * hidden,
-        *second, xg, after(vectors, attended),
+        *second, xg, vectors, small,
         mib=16,
     )
     other_u = exchange(sent_u, "dp", owners, 0)
-    down_rows = w_down.shape[0]
-    sent_d, kept_d = call(
-        down_kernel,
-        (shape((half, down_rows, width), BF16), shape((half, down_rows, width), F32)),
-        [pltpu.VMEM((hidden, width), F32)],
-        2 * tokens * width * hidden, 0,
-        after(active, other_a), xg,
-    )
-    other_d = exchange(sent_d, "dp", owners, 0)
+    sent_a, kept_a = fold(kept_a, other_a)
+    other_a = exchange(sent_a, "dp", owners, 1)
     sent_x, kept_x = call(
         join_kernel,
         (shape((2, local, 2 * width), BF16), shape((2, local, 2 * width), F32)),
@@ -1020,41 +1030,47 @@
         xg, attended, full_out, active, full_down, vectors,
         grad_proj, full_qkv, grad_hidden, full_up,
     )
-    steps = log2(owners)
-    for bit in range(1, steps):
-        sent_a, kept_a = fold(kept_a, other_a)
-        other_a = exchange(sent_a, "dp", owners, bit)
+    down_rows = w_down.shape[0]
+    sent_d, kept_d = call(
+        down_kernel,
+        (shape((half, down_rows, width), BF16), shape((half, down_rows, width), F32)),
+        [pltpu.VMEM((hidden, width), F32)],
+        2 * tokens * width * hidden, 0,
+        active, xg,
+    )
+    other_x = exchange(after(sent_x, other_u, other_a), "seq", groups, 0)
+    other_u, other_x, sent_d, = lax.optimization_barrier((other_u, other_x, sent_d,))
+    other_d = exchange(sent_d, "dp", owners, 0)
+    sent_u, kept_u = fold(kept_u, other_u)
+    other_u = exchange(sent_u, "dp", owners, 1)
+    sent_a, kept_a = fold(kept_a, other_a)
+    other_a = exchange(sent_a, "dp", owners, 2)
+    sent_x, kept_x = fold(kept_x, other_x)
+    other_x = exchange(sent_x, "seq", groups, 1)
+    sent_d, kept_d = fold(kept_d, other_d)
+    other_u, other_a, sent_d, kept_d, = lax.optimization_barrier((other_u, other_a, sent_d, kept_d,))
+    sent_u, kept_u = fold(kept_u, other_u)
+    other_u = exchange(sent_u, "dp", owners, 2)
     grad_a = finish(kept_a, other_a)
-    other_x = exchange(sent_x, "seq", groups, 0)
-    sent_x, kept_x = fold(kept_x, other_x)
-    other_out = exchange(sent_x[..., :width], "seq", groups, 1)
-    other_grad = exchange(after(sent_x[..., width:], other_out), "seq", groups, 1)
-    outputs = finish(kept_x[..., :width], other_out).astype(BF16)[None]
-    grad_inputs = finish(kept_x[..., width:], other_grad).astype(BF16)[None]
-    for bit in range(1, steps):
-        sent_u, kept_u = fold(kept_u, other_u)
-        sent_u = sent_u if bit == 1 else after(sent_u, other_out)
-        other_u = exchange(sent_u, "dp", owners, bit)
-    grad_u, near_d = finish(kept_u, other_u), None
-    for bit in range(1, steps):
-        sent_d, kept_d = fold(kept_d, other_d)
-        other_d = exchange(sent_d, "dp", owners, bit)
-        near_d = near_d if bit > 1 else other_d
-    grad_d = finish(kept_d, other_d)
-    own_wout = lax.ppermute(
-        grad_a[3 * rows : 4 * rows, :], ("dp", "seq"), [(target[f], f) for f in range(devices)]
-    )
+    own_wout = lax.ppermute(grad_a[3 * rows :, :], ("dp", "seq"), [(target[f], f) for f in range(devices)])
+    other_d = exchange(sent_d, "dp", owners, 1)
+    other_u, other_d, other_x, = lax.optimization_barrier((other_u, other_d, other_x,))
+    grad_u = finish(kept_u, other_u)
+    sent_d, kept_d = fold(kept_d, other_d)
     block = shape((2, 2 * rows, 3 * part + hidden), BF16)
-    sent, kept = call(deal_kernel, (block, block), [], 0, 0, grad_a, after(grad_u, other_grad, near_d))
+    sent, kept = call(deal_kernel, (block, block), [], 0, 0, grad_a, grad_u)
     near = exchange(sent, "seq", groups, 0)
+    other_d = exchange(sent_d, "dp", owners, 2)
+    both = finish(kept_x, after(other_x, near))
+    outputs, grad_inputs = (v.astype(BF16)[None] for v in (both[:, :width], both[:, width:]))
     far = exchange(jnp.stack([kept[1], near[1]]), "seq", groups, 1)
     vector = shape((rows,), F32)
-    own_wqkv, own_wup, own_wout, own_bqkv, own_bias, twin_bias, own_bup, *own = call(
+    own_wqkv, own_wup, own_wout, own_bqkv, own_bias, twin_bias, own_bup, *own, grad_d = call(
         collect_kernel,
         (shape(w_qkv.shape, F32), shape(w_up.shape, F32), shape(w_out.shape, F32))
-        + (shape(b_qkv.shape, F32), vector, vector, shape(b_up.shape, F32), vector, vector, vector, vector),
+        + (shape(b_qkv.shape, F32), vector, vector, shape(b_up.shape, F32), vector, vector, vector, vector, shape(w_down.shape, F32)),
         [pltpu.VMEM((groups, 2 * rows, 3 * part + hidden), F32)],
-        0, 0, kept, near, far, grad_a, grad_u, own_wout,
+        0, 0, kept, near, far, grad_u, own_wout, kept_d, other_d,
     )
     return (
         outputs,

time: 106 us -> 98.6 us (0.930)
  waiting for transfers between devices: 42 us -> 33.6 us
  other arithmetic: 3.83 us -> 1.07 us
  local copies, waits for them, and re-layouts: 2.7 us -> 4.7 us
  starting transfers between devices: 34.3 us -> 35.6 us
    ppermute x24 -> x23, waiting for transfers between devices: 42 us -> 33.6 us  [exchange(): return lax.ppermute(value, axis, [(i, i ^ 1 << bit) for i in range(size)])]
    ppermute x24 -> x23, starting transfers between devices: 33.7 us -> 35 us  [exchange(): return lax.ppermute(value, axis, [(i, i ^ 1 << bit) for i in range(size)])]
    unnamed x10 -> x11, local copies, waits for them, and re-layouts: 1.74 us -> 2.82 us
    broadcast_in_dim x1 -> x0, other arithmetic: 1.08 us -> none  [shards(): x = jnp.concatenate([after(inputs[0], far), cotangent[0]], axis=1)[None]]
  transfers between devices with their start and end apart: 25 -> 24, of which waited for: 15 -> 14; matrix products, arithmetic and copies ran while one was open for 3% -> 4% of each run, Pallas kernels for 18% -> 19%
where the time goes in v3:
time: 98.6 us; the launch traced here: 98.3 us
  starting transfers between devices  35.6 us (36%)
  waiting for transfers between devices  33.6 us (34%)
  Pallas kernels  22.1 us (22%)
  local copies, waits for them, and re-layouts  4.7 us (5%)
  between operations  1.17 us (1%)
  other arithmetic  1.07 us (1%)
    ppermute x23, starting transfers between devices, exchange(): return lax.ppermute(value, axis, [(i, i ^ 1 << bit) for i in range(size)])  35 us
    ppermute x23, waiting for transfers between devices, exchange(): return lax.ppermute(value, axis, [(i, i ^ 1 << bit) for i in range(size)])  33.6 us
    pallas_call x11, Pallas kernels, call(): pl.pallas_call(kernel, out_shape=tuple(outs), in_specs=whole(len(operands...  22.1 us
    unnamed x11, local copies, waits for them, and re-layouts  2.82 us
  transfers between devices with their start and end apart: 24, of which 14 were waited for; matrix products, arithmetic and copies ran while one was open for 4% of the time, Pallas kernels for 19%

profile of v3, /device:TPU:0, one launch (start us, length us, event | category | flops | bytes accessed | tf_op | source)
XLA Modules:
  0.0 98.3 jit_solution(14389633421879663446)
XLA Ops:
  0.7 2.1 %shard_map.272 = (bf16[2,16,1536]{2,1,0:T(8,128)(2,1)}, bf16[2,16,1536]{2,1,0:T(8,128)(2,1)}, bf16[1,256,1024]{2,1,0:T(8,128)(2,1)}) custom-call(bf16[1,256,512]{2,1,0:T(8,128)(2,1)} %refs_0_.1, bf16[1,256,512]{2,1,0:T(8,128)(2,1)} %refs_1_.1, bf16[16,1536]{1,0:T(8,128)(2,1)} %refs_2_.1, bf16[16,2048]{1,0:T(8,128)(2,1)} %refs_3_.1, bf16[16,512]{1,0:T(8,128)(2,1)} %refs_4_.1, ...), custom_call_target="tpu_custom_call" | custom-call | flops 1 | bytes 1 | tf_op jit(solution)/shard_map/pallas_call | solution.py:497
  4.5 2.9 %collective-permute-start.1 = (bf16[2,16,1536]{2,1,0:T(8,128)(2,1)S(1)}, bf16[2,16,1536]{2,1,0:T(8,128)(2,1)S(1)}, u32[]{:S(2)}, u32[]{:S(2)}) collective-permute-start(bf16[2,16,1536]{2,1,0:T(8,128)(2,1)S(1)} %pad_maximum_fusion.3), channel_id=1, source_target_pairs={{0,2},{1,3},{2,0},{3,1},{4,6},{5,7},{6,4},{7,5},{8,10},{9,11},{10,... | collective-permute-start | bytes 294920 | tf_op jit(solution)/shard_map/ppermute | solution.py:27
  7.4 3.1 %collective-permute-done.1.far_ref = bf16[2,16,1536]{2,1,0:T(8,128)(2,1)S(1)} collective-permute-done((bf16[2,16,1536]{2,1,0:T(8,128)(2,1)S(1)}, bf16[2,16,1536]{2,1,0:T(8,128)(2,1)S(1)}, u32[]{:S(2)}, u32[]{:S(2)}) %collective-permute-start.1) | collective-permute-done | bytes 98336 | tf_op jit(solution)/shard_map/ppermute | solution.py:27
  10.5 1.7 %collective-permute-start.5 = (bf16[1,256,1024]{2,1,0:T(8,128)(2,1)}, bf16[1,256,1024]{2,1,0:T(8,128)(2,1)S(1)}, u32[]{:S(2)}, u32[]{:S(2)}) collective-permute-start(bf16[1,256,1024]{2,1,0:T(8,128)(2,1)} %get-tuple-element.84), channel_id=1, source_target_pairs={{0,2},{1,3},{2,0},{3,1},{4,6},{5,7},{6,4},{7,5},{8,10},{9,11},{10,... | collective-permute-start | bytes 1572872 | tf_op jit(solution)/shard_map/ppermute | solution.py:27
  14.1 2.7 %collective-permute-start.2 = (bf16[128,512]{1,0:T(8,128)(2,1)S(1)}, bf16[128,512]{1,0:T(8,128)(2,1)S(1)}, u32[]{:S(2)}, u32[]{:S(2)}) collective-permute-start(bf16[128,512]{1,0:T(8,128)(2,1)S(1)} %get-tuple-element.80.mine_ref), channel_id=1, source_target_pairs={{0,16},{4,20},{8,24},{12,28},{16,0},{20,4},{24,8},{28,12},{1,17},{... | collective-permute-start | bytes 393224 | tf_op jit(solution)/shard_map/ppermute | solution.py:27
  16.8 5.6 %collective-permute-done.2.other_ref = bf16[128,512]{1,0:T(8,128)(2,1)S(1)} collective-permute-done((bf16[128,512]{1,0:T(8,128)(2,1)S(1)}, bf16[128,512]{1,0:T(8,128)(2,1)S(1)}, u32[]{:S(2)}, u32[]{:S(2)}) %collective-permute-start.2) | collective-permute-done | bytes 131104 | tf_op jit(solution)/shard_map/ppermute | solution.py:27
  23.1 3.4 %collective-permute-start.4 = (bf16[1,128,512]{2,1,0:T(8,128)(2,1)S(1)}, bf16[1,128,512]{2,1,0:T(8,128)(2,1)S(1)}, u32[]{:S(2)}, u32[]{:S(2)}) collective-permute-start(bf16[1,128,512]{2,1,0:T(8,128)(2,1)S(1)} %bitcast.13), channel_id=1, source_target_pairs={{0,16},{4,20},{8,24},{12,28},{16,0},{20,4},{24,8},{28,12},{1,17},{... | collective-permute-start | bytes 393224 | tf_op jit(solution)/shard_map/ppermute | solution.py:27
  27.6 2.3 %collective-permute-done.4 = bf16[1,128,512]{2,1,0:T(8,128)(2,1)S(1)} collective-permute-done((bf16[1,128,512]{2,1,0:T(8,128)(2,1)S(1)}, bf16[1,128,512]{2,1,0:T(8,128)(2,1)S(1)}, u32[]{:S(2)}, u32[]{:S(2)}) %collective-permute-start.4) | collective-permute-done | bytes 131104 | tf_op jit(solution)/shard_map/ppermute | solution.py:27
  32.5 2.9 %collective-permute-start.8 = (bf16[2,128,512]{2,1,0:T(8,128)(2,1)S(1)}, bf16[2,128,512]{2,1,0:T(8,128)(2,1)S(1)}, u32[]{:S(2)}, u32[]{:S(2)}) collective-permute-start(bf16[2,128,512]{2,1,0:T(8,128)(2,1)S(1)} %pad_maximum_fusion.1), channel_id=1, source_target_pairs={{0,8},{4,12},{8,0},{12,4},{16,24},{20,28},{24,16},{28,20},{1,9},{5... | collective-permute-start | bytes 786440 | tf_op jit(solution)/shard_map/ppermute | solution.py:27
  35.3 4.7 %collective-permute-done.6.other_ref = bf16[272,512]{1,0:T(8,128)(2,1)S(1)} collective-permute-done((bf16[272,512]{1,0:T(8,128)(2,1)S(1)}, bf16[272,512]{1,0:T(8,128)(2,1)S(1)}, u32[]{:S(2)}, u32[]{:S(2)}) %collective-permute-start.6) | collective-permute-done | bytes 278560 | tf_op jit(solution)/shard_map/ppermute | solution.py:27
  40.0 2.1 %shard_map.276 = (bf16[1024,1024]{1,0:T(8,128)(2,1)S(1)}, bf16[1024,512]{1,0:T(8,128)(2,1)S(1)}, bf16[1024,128]{1,0:T(8,128)(2,1)S(1)}, bf16[128,1024]{1,0:T(8,1...) custom-call(bf16[272,512]{1,0:T(8,128)(2,1)S(1)} %shard_map.275.firs, ...), custom_call_target="tpu_custom_call" | custom-call | flops 1 | bytes 1 | tf_op jit(solution)/shard_map/pallas_call | solution.py:497
  43.7 9.7 %shard_map.277 = (bf16[1024,128]{1,0:T(8,128)(2,1)S(1)}, bf16[1024,384]{1,0:T(8,128)(2,1)S(1)}, f32[8,512]{1,0:T(8,128)S(1)}, bf16[4,64,512]{2,1,0:T(8,128)(2,1)S(1)}, f32[4,64,512]{2,1,0:T(8,128)S(1)}) custom-call(bf16[1024,1024]{1,0:T(8,128)(2,1)S(1)} %get-tuple-element.87.xg_ref, bf16[1024,512]{1,0:T(8,128)(2,1)S(1)} %get-tuple-element.88.na_ref, ...), custom_call_target="tpu_custom_call" | custom-call | flops 1 | bytes 1 | tf_op jit(solution)/shard_map/pallas_call | solution.py:497
  54.0 2.0 %collective-permute-done.9.other_ref = bf16[4,128,512]{2,1,0:T(8,128)(2,1)S(1)} collective-permute-done((bf16[4,128,512]{2,1,0:T(8,128)(2,1)S(1)}, bf16[4,128,512]{2,1,0:T(8,128)(2,1)S(1)}, u32[]{:S(2)}, u32[]{:S(2)}) %collective-permute-start.9) | collective-permute-done | bytes 524320 | tf_op jit(solution)/shard_map/ppermute | solution.py:27
  56.0 3.9 %shard_map.278 = (bf16[1024,512]{1,0:T(8,128)(2,1)S(1)}, bf16[1024,512]{1,0:T(8,128)(2,1)S(1)}, bf16[512,512]{1,0:T(8,128)(2,1)S(1)}, bf16[512,512]{1,0:T(8,128)...) custom-call(bf16[4,128,512]{2,1,0:T(8,128)(2,1)S(1)} %pad_maximum_fusion.second_ref, ...), custom_call_target="tpu_custom_call" | custom-call | flops 1 | bytes 1 | tf_op jit(solution)/shard_map/pallas_call | solution.py:497
  59.9 2.5 %collective-permute-start.10 = (bf16[4,80,512]{2,1,0:T(8,128)(2,1)S(1)}, bf16[4,80,512]{2,1,0:T(8,128)(2,1)S(1)}, u32[]{:S(2)}, u32[]{:S(2)}) collective-permute-start(bf16[4,80,512]{2,1,0:T(8,128)(2,1)S(1)} %get-tuple-element.109), channel_id=1, source_target_pairs={{0,4},{4,0},{8,12},{12,8},{16,20},{20,16},{24,28},{28,24},{1,5},{5... | collective-permute-start | bytes 983048 | tf_op jit(solution)/shard_map/ppermute | solution.py:27
  62.5 2.9 %collective-permute-start.12 = (bf16[2,64,512]{2,1,0:T(8,128)(2,1)S(1)}, bf16[2,64,512]{2,1,0:T(8,128)(2,1)S(1)}, u32[]{:S(2)}, u32[]{:S(2)}) collective-permute-start(bf16[2,64,512]{2,1,0:T(8,128)(2,1)S(1)} %slice.140), channel_id=1, source_target_pairs={{0,8},{4,12},{8,0},{12,4},{16,24},{20,28},{24,16},{28,20},{1,9},{5... | collective-permute-start | bytes 393224 | tf_op jit(solution)/shard_map/ppermute | solution.py:27
  65.4 2.5 %shard_map.279 = (bf16[2,256,1024]{2,1,0:T(8,128)(2,1)S(1)}, f32[2,256,1024]{2,1,0:T(8,128)S(1)}) custom-call(bf16[1024,1024]{1,0:T(8,128)(2,1)S(1)} %get-tuple-element.87.xg_ref, bf16[1024,128]{1,0:T(8,128)(2,1)S(1)} %get-tuple-element.98.att_ref, bf16[128,512]{1,0:T(8,128)(2,1)S(1)} %get-tuple-element.99.wo_ref, ...), custom_call_target="tpu_custom_call" | custom-call | flops 1 | bytes 1 | tf_op jit(solution)/shard_map/pallas_call | solution.py:497
  68.5 2.2 %collective-permute-start.15 = (bf16[1,64,512]{2,1,0:T(8,128)(2,1)S(1)}, bf16[1,64,512]{2,1,0:T(8,128)(2,1)S(1)}, u32[]{:S(2)}, u32[]{:S(2)}) collective-permute-start(bf16[1,64,512]{2,1,0:T(8,128)(2,1)S(1)} %slice.143), channel_id=1, source_target_pairs={{0,16},{4,20},{8,24},{12,28},{16,0},{20,4},{24,8},{28,12},{1,17},{... | collective-permute-start | bytes 196616 | tf_op jit(solution)/shard_map/ppermute | solution.py:27
  71.6 2.5 %collective-permute-start.14 = (bf16[2,80,512]{2,1,0:T(8,128)(2,1)S(1)}, bf16[2,80,512]{2,1,0:T(8,128)(2,1)S(1)}, u32[]{:S(2)}, u32[]{:S(2)}) collective-permute-start(bf16[2,80,512]{2,1,0:T(8,128)(2,1)S(1)} %slice.138), channel_id=1, source_target_pairs={{0,8},{4,12},{8,0},{12,4},{16,24},{20,28},{24,16},{28,20},{1,9},{5... | collective-permute-start | bytes 491528 | tf_op jit(solution)/shard_map/ppermute | solution.py:27
  76.7 5.6 %collective-permute-done.16 = bf16[4,64,512]{2,1,0:T(8,128)(2,1)S(1)} collective-permute-done((bf16[4,64,512]{2,1,0:T(8,128)(2,1)S(1)}, bf16[4,64,512]{2,1,0:T(8,128)(2,1)S(1)}, u32[]{:S(2)}, u32[]{:S(2)}) %collective-permute-start.16) | collective-permute-done | bytes 262176 | tf_op jit(solution)/shard_map/ppermute | solution.py:27
  82.5 1.7 %collective-permute-start.17 = (bf16[1,80,512]{2,1,0:T(8,128)(2,1)S(1)}, bf16[1,80,512]{2,1,0:T(8,128)(2,1)S(1)}, u32[]{:S(2)}, u32[]{:S(2)}) collective-permute-start(bf16[1,80,512]{2,1,0:T(8,128)(2,1)S(1)} %slice.141), channel_id=1, source_target_pairs={{0,16},{4,20},{8,24},{12,28},{16,0},{20,4},{24,8},{28,12},{1,17},{... | collective-permute-start | bytes 245768 | tf_op jit(solution)/shard_map/ppermute | solution.py:27
  85.2 3.4 %collective-permute-done.17 = bf16[1,80,512]{2,1,0:T(8,128)(2,1)S(1)} collective-permute-done((bf16[1,80,512]{2,1,0:T(8,128)(2,1)S(1)}, bf16[1,80,512]{2,1,0:T(8,128)(2,1)S(1)}, u32[]{:S(2)}, u32[]{:S(2)}) %collective-permute-start.17) | collective-permute-done | bytes 81952 | tf_op jit(solution)/shard_map/ppermute | solution.py:27
  90.0 1.7 %collective-permute-start.23 = (bf16[1,64,512]{2,1,0:T(8,128)(2,1)S(1)}, bf16[1,64,512]{2,1,0:T(8,128)(2,1)S(1)}, u32[]{:S(2)}, u32[]{:S(2)}) collective-permute-start(bf16[1,64,512]{2,1,0:T(8,128)(2,1)S(1)} %slice.142), channel_id=1, source_target_pairs={{0,16},{4,20},{8,24},{12,28},{16,0},{20,4},{24,8},{28,12},{1,17},{... | collective-permute-start | bytes 196616 | tf_op jit(solution)/shard_map/ppermute | solution.py:27
  93.2 3.7 %collective-permute-done.23.down_other_ref = bf16[1,64,512]{2,1,0:T(8,128)(2,1)S(1)} collective-permute-done((bf16[1,64,512]{2,1,0:T(8,128)(2,1)S(1)}, bf16[1,64,512]{2,1,0:T(8,128)(2,1)S(1)}, u32[]{:S(2)}, u32[]{:S(2)}) %collective-permute-start.23) | collective-permute-done | bytes 65568 | tf_op jit(solution)/shard_map/ppermute | solution.py:27
  (76 shorter events, 19.6 us)
Async XLA Ops:
  2.8 1.7 %collective-permute-start = (bf16[2,16,1536]{2,1,0:T(8,128)(2,1)}, bf16[2,16,1536]{2,1,0:T(8,128)(2,1)S(1)}, u32[]{:S(2)}, u32[]{:S(2)}) collective-permute-start(bf16[2,16,1536]{2,1,0:T(8,128)(2,1)} %get-tuple-element.79), channel_id=1, source_target_pairs={{0,1},{1,0},{2,3},{3,2},{4,5},{5,4},{6,7},{7,6},{8,9},{9,8},{10,11... | collective-permute-start | bytes 294920 | tf_op jit(solution)/shard_map/ppermute | solution.py:27
  4.5 6.1 %collective-permute-start.1 = (bf16[2,16,1536]{2,1,0:T(8,128)(2,1)S(1)}, bf16[2,16,1536]{2,1,0:T(8,128)(2,1)S(1)}, u32[]{:S(2)}, u32[]{:S(2)}) collective-permute-start(bf16[2,16,1536]{2,1,0:T(8,128)(2,1)S(1)} %pad_maximum_fusion.3), channel_id=1, source_target_pairs={{0,2},{1,3},{2,0},{3,1},{4,6},{5,7},{6,4},{7,5},{8,10},{9,11},{10,... | collective-permute-start | bytes 294920 | tf_op jit(solution)/shard_map/ppermute | solution.py:27
  10.5 20.2 %collective-permute-start.5 = (bf16[1,256,1024]{2,1,0:T(8,128)(2,1)}, bf16[1,256,1024]{2,1,0:T(8,128)(2,1)S(1)}, u32[]{:S(2)}, u32[]{:S(2)}) collective-permute-start(bf16[1,256,1024]{2,1,0:T(8,128)(2,1)} %get-tuple-element.84), channel_id=1, source_target_pairs={{0,2},{1,3},{2,0},{3,1},{4,6},{5,7},{6,4},{7,5},{8,10},{9,11},{10,... | collective-permute-start | bytes 1572872 | tf_op jit(solution)/shard_map/ppermute | solution.py:27
  14.1 8.2 %collective-permute-start.2 = (bf16[128,512]{1,0:T(8,128)(2,1)S(1)}, bf16[128,512]{1,0:T(8,128)(2,1)S(1)}, u32[]{:S(2)}, u32[]{:S(2)}) collective-permute-start(bf16[128,512]{1,0:T(8,128)(2,1)S(1)} %get-tuple-element.80.mine_ref), channel_id=1, source_target_pairs={{0,16},{4,20},{8,24},{12,28},{16,0},{20,4},{24,8},{28,12},{1,17},{... | collective-permute-start | bytes 393224 | tf_op jit(solution)/shard_map/ppermute | solution.py:27
  22.4 8.4 %collective-permute-start.3 = (bf16[176,512]{1,0:T(8,128)(2,1)S(1)}, bf16[176,512]{1,0:T(8,128)(2,1)S(1)}, u32[]{:S(2)}, u32[]{:S(2)}) collective-permute-start(bf16[176,512]{1,0:T(8,128)(2,1)S(1)} %shard_map.274.mine_ref), channel_id=1, source_target_pairs={{0,8},{4,12},{8,0},{12,4},{16,24},{20,28},{24,16},{28,20},{1,9},{5... | collective-permute-start | bytes 540680 | tf_op jit(solution)/shard_map/ppermute | solution.py:27
  23.1 6.8 %collective-permute-start.4 = (bf16[1,128,512]{2,1,0:T(8,128)(2,1)S(1)}, bf16[1,128,512]{2,1,0:T(8,128)(2,1)S(1)}, u32[]{:S(2)}, u32[]{:S(2)}) collective-permute-start(bf16[1,128,512]{2,1,0:T(8,128)(2,1)S(1)} %bitcast.13), channel_id=1, source_target_pairs={{0,16},{4,20},{8,24},{12,28},{16,0},{20,4},{24,8},{28,12},{1,17},{... | collective-permute-start | bytes 393224 | tf_op jit(solution)/shard_map/ppermute | solution.py:27
  30.8 9.2 %collective-permute-start.7 = (bf16[2,256,1024]{2,1,0:T(8,128)(2,1)S(1)}, bf16[2,256,1024]{2,1,0:T(8,128)(2,1)S(1)}, u32[]{:S(2)}, u32[]{:S(2)}) collective-permute-start(bf16[2,256,1024]{2,1,0:T(8,128)(2,1)S(1)} %constant_dynamic-update-slice_fusion.x_ref), channel_id=1, source_target_pairs={{0,1},{1,0},{2,3},{3,2},{4,5},{5,4},{6,7},{7,6},{8,9},{9,8},{10,11... | collective-permute-start | bytes 3145736 | tf_op jit(solution)/shard_map/ppermute | solution.py:27
  30.9 9.1 %collective-permute-start.6 = (bf16[272,512]{1,0:T(8,128)(2,1)S(1)}, bf16[272,512]{1,0:T(8,128)(2,1)S(1)}, u32[]{:S(2)}, u32[]{:S(2)}) collective-permute-start(bf16[272,512]{1,0:T(8,128)(2,1)S(1)} %shard_map.275.first_ref), channel_id=1, source_target_pairs={{0,4},{4,0},{8,12},{12,8},{16,20},{20,16},{24,28},{28,24},{1,5},{5... | collective-permute-start | bytes 835592 | tf_op jit(solution)/shard_map/ppermute | solution.py:27
  32.5 9.6 %collective-permute-start.8 = (bf16[2,128,512]{2,1,0:T(8,128)(2,1)S(1)}, bf16[2,128,512]{2,1,0:T(8,128)(2,1)S(1)}, u32[]{:S(2)}, u32[]{:S(2)}) collective-permute-start(bf16[2,128,512]{2,1,0:T(8,128)(2,1)S(1)} %pad_maximum_fusion.1), channel_id=1, source_target_pairs={{0,8},{4,12},{8,0},{12,4},{16,24},{20,28},{24,16},{28,20},{1,9},{5... | collective-permute-start | bytes 786440 | tf_op jit(solution)/shard_map/ppermute | solution.py:27
  42.2 13.8 %collective-permute-start.9 = (bf16[4,128,512]{2,1,0:T(8,128)(2,1)S(1)}, bf16[4,128,512]{2,1,0:T(8,128)(2,1)S(1)}, u32[]{:S(2)}, u32[]{:S(2)}) collective-permute-start(bf16[4,128,512]{2,1,0:T(8,128)(2,1)S(1)} %pad_maximum_fusion.second_ref), channel_id=1, source_target_pairs={{0,4},{4,0},{8,12},{12,8},{16,20},{20,16},{24,28},{28,24},{1,5},{5... | collective-permute-start | bytes 1572872 | tf_op jit(solution)/shard_map/ppermute | solution.py:27
  53.4 9.0 %collective-permute-start.11 = (bf16[4,64,512]{2,1,0:T(8,128)(2,1)S(1)}, bf16[4,64,512]{2,1,0:T(8,128)(2,1)S(1)}, u32[]{:S(2)}, u32[]{:S(2)}) collective-permute-start(bf16[4,64,512]{2,1,0:T(8,128)(2,1)S(1)} %get-tuple-element.112), channel_id=1, source_target_pairs={{0,4},{4,0},{8,12},{12,8},{16,20},{20,16},{24,28},{28,24},{1,5},{5... | collective-permute-start | bytes 786440 | tf_op jit(solution)/shard_map/ppermute | solution.py:27
  59.9 8.5 %collective-permute-start.10 = (bf16[4,80,512]{2,1,0:T(8,128)(2,1)S(1)}, bf16[4,80,512]{2,1,0:T(8,128)(2,1)S(1)}, u32[]{:S(2)}, u32[]{:S(2)}) collective-permute-start(bf16[4,80,512]{2,1,0:T(8,128)(2,1)S(1)} %get-tuple-element.109), channel_id=1, source_target_pairs={{0,4},{4,0},{8,12},{12,8},{16,20},{20,16},{24,28},{28,24},{1,5},{5... | collective-permute-start | bytes 983048 | tf_op jit(solution)/shard_map/ppermute | solution.py:27
  62.5 5.8 %collective-permute-start.12 = (bf16[2,64,512]{2,1,0:T(8,128)(2,1)S(1)}, bf16[2,64,512]{2,1,0:T(8,128)(2,1)S(1)}, u32[]{:S(2)}, u32[]{:S(2)}) collective-permute-start(bf16[2,64,512]{2,1,0:T(8,128)(2,1)S(1)} %slice.140), channel_id=1, source_target_pairs={{0,8},{4,12},{8,0},{12,4},{16,24},{20,28},{24,16},{28,20},{1,9},{5... | collective-permute-start | bytes 393224 | tf_op jit(solution)/shard_map/ppermute | solution.py:27
  68.4 3.1 %collective-permute-start.13 = (bf16[2,256,1024]{2,1,0:T(8,128)(2,1)S(1)}, bf16[2,256,1024]{2,1,0:T(8,128)(2,1)S(1)}, u32[]{:S(2)}, u32[]{:S(2)}) collective-permute-start(bf16[2,256,1024]{2,1,0:T(8,128)(2,1)S(1)} %get-tuple-element.113), channel_id=1, source_target_pairs={{0,1},{1,0},{2,3},{3,2},{4,5},{5,4},{6,7},{7,6},{8,9},{9,8},{10,11... | collective-permute-start | bytes 3145736 | tf_op jit(solution)/shard_map/ppermute | solution.py:27
  68.5 13.9 %collective-permute-start.15 = (bf16[1,64,512]{2,1,0:T(8,128)(2,1)S(1)}, bf16[1,64,512]{2,1,0:T(8,128)(2,1)S(1)}, u32[]{:S(2)}, u32[]{:S(2)}) collective-permute-start(bf16[1,64,512]{2,1,0:T(8,128)(2,1)S(1)} %slice.143), channel_id=1, source_target_pairs={{0,16},{4,20},{8,24},{12,28},{16,0},{20,4},{24,8},{28,12},{1,17},{... | collective-permute-start | bytes 196616 | tf_op jit(solution)/shard_map/ppermute | solution.py:27
  71.6 10.8 %collective-permute-start.14 = (bf16[2,80,512]{2,1,0:T(8,128)(2,1)S(1)}, bf16[2,80,512]{2,1,0:T(8,128)(2,1)S(1)}, u32[]{:S(2)}, u32[]{:S(2)}) collective-permute-start(bf16[2,80,512]{2,1,0:T(8,128)(2,1)S(1)} %slice.138), channel_id=1, source_target_pairs={{0,8},{4,12},{8,0},{12,4},{16,24},{20,28},{24,16},{28,20},{1,9},{5... | collective-permute-start | bytes 491528 | tf_op jit(solution)/shard_map/ppermute | solution.py:27
  74.1 8.2 %collective-permute-start.16 = (bf16[4,64,512]{2,1,0:T(8,128)(2,1)S(1)}, bf16[4,64,512]{2,1,0:T(8,128)(2,1)S(1)}, u32[]{:S(2)}, u32[]{:S(2)}) collective-permute-start(bf16[4,64,512]{2,1,0:T(8,128)(2,1)S(1)} %get-tuple-element.119), channel_id=1, source_target_pairs={{0,4},{4,0},{8,12},{12,8},{16,20},{20,16},{24,28},{28,24},{1,5},{5... | collective-permute-start | bytes 786440 | tf_op jit(solution)/shard_map/ppermute | solution.py:27
  76.1 13.7 %collective-permute-start.19 = (bf16[1,256,1024]{2,1,0:T(8,128)(2,1)S(1)}, bf16[1,256,1024]{2,1,0:T(8,128)(2,1)S(1)}, u32[]{:S(2)}, u32[]{:S(2)}) collective-permute-start(bf16[1,256,1024]{2,1,0:T(8,128)(2,1)S(1)} %slice.137), channel_id=1, source_target_pairs={{0,2},{1,3},{2,0},{3,1},{4,6},{5,7},{6,4},{7,5},{8,10},{9,11},{10,... | collective-permute-start | bytes 1572872 | tf_op jit(solution)/shard_map/ppermute | solution.py:27
  82.5 6.2 %collective-permute-start.17 = (bf16[1,80,512]{2,1,0:T(8,128)(2,1)S(1)}, bf16[1,80,512]{2,1,0:T(8,128)(2,1)S(1)}, u32[]{:S(2)}, u32[]{:S(2)}) collective-permute-start(bf16[1,80,512]{2,1,0:T(8,128)(2,1)S(1)} %slice.141), channel_id=1, source_target_pairs={{0,16},{4,20},{8,24},{12,28},{16,0},{20,4},{24,8},{28,12},{1,17},{... | collective-permute-start | bytes 245768 | tf_op jit(solution)/shard_map/ppermute | solution.py:27
  84.2 5.6 %collective-permute-start.18 = (bf16[2,64,512]{2,1,0:T(8,128)(2,1)S(1)}, bf16[2,64,512]{2,1,0:T(8,128)(2,1)S(1)}, u32[]{:S(2)}, u32[]{:S(2)}) collective-permute-start(bf16[2,64,512]{2,1,0:T(8,128)(2,1)S(1)} %slice.139), channel_id=1, source_target_pairs={{0,8},{4,12},{8,0},{12,4},{16,24},{20,28},{24,16},{28,20},{1,9},{5... | collective-permute-start | bytes 393224 | tf_op jit(solution)/shard_map/ppermute | solution.py:27
  84.5 8.6 %collective-permute-start.22 = (f32[16,512]{1,0:T(8,128)S(1)}, f32[16,512]{1,0:T(8,128)S(1)}, u32[]{:S(2)}, u32[]{:S(2)}) collective-permute-start(f32[16,512]{1,0:T(8,128)S(1)} %slice_bitcast_fusion.2), channel_id=1, source_target_pairs={{0,0},{8,1},{16,2},{24,3},{4,4},{12,5},{20,6},{28,7},{1,8},{9,9},{... | collective-permute-start | bytes 98312 | tf_op jit(solution)/shard_map/ppermute | solution.py:1055
  89.9 1.9 %collective-permute-start.20 = (bf16[2,32,896]{2,1,0:T(8,128)(2,1)S(1)}, bf16[2,32,896]{2,1,0:T(8,128)(2,1)S(1)}, u32[]{:S(2)}, u32[]{:S(2)}) collective-permute-start(bf16[2,32,896]{2,1,0:T(8,128)(2,1)S(1)} %get-tuple-element.125), channel_id=1, source_target_pairs={{0,1},{1,0},{2,3},{3,2},{4,5},{5,4},{6,7},{7,6},{8,9},{9,8},{10,11... | collective-permute-start | bytes 344072 | tf_op jit(solution)/shard_map/ppermute | solution.py:27
  90.0 6.8 %collective-permute-start.23 = (bf16[1,64,512]{2,1,0:T(8,128)(2,1)S(1)}, bf16[1,64,512]{2,1,0:T(8,128)(2,1)S(1)}, u32[]{:S(2)}, u32[]{:S(2)}) collective-permute-start(bf16[1,64,512]{2,1,0:T(8,128)(2,1)S(1)} %slice.142), channel_id=1, source_target_pairs={{0,16},{4,20},{8,24},{12,28},{16,0},{20,4},{24,8},{28,12},{1,17},{... | collective-permute-start | bytes 196616 | tf_op jit(solution)/shard_map/ppermute | solution.py:27
  91.9 5.3 %collective-permute-start.21 = (bf16[2,32,896]{2,1,0:T(8,128)(2,1)S(1)}, bf16[2,32,896]{2,1,0:T(8,128)(2,1)S(1)}, u32[]{:S(2)}, u32[]{:S(2)}) collective-permute-start(bf16[2,32,896]{2,1,0:T(8,128)(2,1)S(1)} %pad_maximum_fusion.2), channel_id=1, source_target_pairs={{0,2},{1,3},{2,0},{3,1},{4,6},{5,7},{6,4},{7,5},{8,10},{9,11},{10,... | collective-permute-start | bytes 344072 | tf_op jit(solution)/shard_map/ppermute | solution.py:27
  (5 other events, 108.4 us)

commit v4 on v3

--- a/solution.py
+++ b/solution.py
@@ -868,7 +868,7 @@
     )
     for step in range(4):
         group = me ^ step
-        ref = (kept_ref, sent_ref)[step % 2].at[step // 2]
+        ref = (kept_ref, sent_ref)[step // 2].at[step % 2]
         lanes = pl.ds(pl.multiple_of(group * part, part), part)
         for c in range(3):
             ref[:rows, c * part : (c + 1) * part] = a_ref[c * rows : (c + 1) * rows, lanes].astype(kind)
@@ -888,7 +888,7 @@
     width = qkv_ref.shape[1] // 3
     part = width // 4
     piece = 4 * rows
-    for step, block in enumerate((kept_ref.at[0], near_ref.at[0], far_ref.at[0], far_ref.at[1])):
+    for step, block in enumerate((kept_ref.at[0], far_ref.at[0], near_ref.at[0], far_ref.at[1])):
         block_ref[me ^ step] = block[...].astype(F32)
     for g in range(4):
         for c in range(3):
@@ -1059,11 +1059,11 @@
     sent_d, kept_d = fold(kept_d, other_d)
     block = shape((2, 2 * rows, 3 * part + hidden), BF16)
     sent, kept = call(deal_kernel, (block, block), [], 0, 0, grad_a, grad_u)
-    near = exchange(sent, "seq", groups, 0)
+    near = exchange(sent, "seq", groups, 1)
     other_d = exchange(sent_d, "dp", owners, 2)
-    both = finish(kept_x, after(other_x, near))
+    both = finish(kept_x, other_x)
     outputs, grad_inputs = (v.astype(BF16)[None] for v in (both[:, :width], both[:, width:]))
-    far = exchange(jnp.stack([kept[1], near[1]]), "seq", groups, 1)
+    far = exchange(jnp.stack([kept[1], near[1]]), "seq", groups, 0)
     vector = shape((rows,), F32)
     own_wqkv, own_wup, own_wout, own_bqkv, own_bias, twin_bias, own_bup, *own, grad_d = call(
         collect_kernel,

time: 98.6 us -> 97.9 us (level)
  transfers between devices with their start and end apart: 24 -> 24, of which waited for: 14 -> 14; matrix products, arithmetic and copies ran while one was open for 4% -> 4% of each run, Pallas kernels for 19% -> 20%
where the time goes in v4:
time: 97.9 us; the launch traced here: 97.6 us
  starting transfers between devices  35.6 us (36%)
  waiting for transfers between devices  32.9 us (34%)
  Pallas kernels  22.1 us (23%)
  local copies, waits for them, and re-layouts  4.7 us (5%)
  between operations  1.16 us (1%)
  other arithmetic  1.06 us (1%)
    ppermute x23, starting transfers between devices, exchange(): return lax.ppermute(value, axis, [(i, i ^ 1 << bit) for i in range(size)])  35 us
    ppermute x23, waiting for transfers between devices, exchange(): return lax.ppermute(value, axis, [(i, i ^ 1 << bit) for i in range(size)])  32.9 us
    pallas_call x11, Pallas kernels, call(): pl.pallas_call(kernel, out_shape=tuple(outs), in_specs=whole(len(operands...  22.1 us
    unnamed x11, local copies, waits for them, and re-layouts  2.82 us
  transfers between devices with their start and end apart: 24, of which 14 were waited for; matrix products, arithmetic and copies ran while one was open for 4% of the time, Pallas kernels for 20%

profile of v4, /device:TPU:0, one launch (start us, length us, event | category | flops | bytes accessed | tf_op | source)
XLA Modules:
  0.0 97.6 jit_solution(4078657976081796355)
XLA Ops:
  0.7 2.1 %shard_map.272 = (bf16[2,16,1536]{2,1,0:T(8,128)(2,1)}, bf16[2,16,1536]{2,1,0:T(8,128)(2,1)}, bf16[1,256,1024]{2,1,0:T(8,128)(2,1)}) custom-call(bf16[1,256,512]{2,1,0:T(8,128)(2,1)} %refs_0_.1, bf16[1,256,512]{2,1,0:T(8,128)(2,1)} %refs_1_.1, bf16[16,1536]{1,0:T(8,128)(2,1)} %refs_2_.1, bf16[16,2048]{1,0:T(8,128)(2,1)} %refs_3_.1, bf16[16,512]{1,0:T(8,128)(2,1)} %refs_4_.1, ...), custom_call_target="tpu_custom_call" | custom-call | flops 1 | bytes 1 | tf_op jit(solution)/shard_map/pallas_call | solution.py:497
  4.5 2.9 %collective-permute-start.1 = (bf16[2,16,1536]{2,1,0:T(8,128)(2,1)S(1)}, bf16[2,16,1536]{2,1,0:T(8,128)(2,1)S(1)}, u32[]{:S(2)}, u32[]{:S(2)}) collective-permute-start(bf16[2,16,1536]{2,1,0:T(8,128)(2,1)S(1)} %pad_maximum_fusion.3), channel_id=1, source_target_pairs={{0,2},{1,3},{2,0},{3,1},{4,6},{5,7},{6,4},{7,5},{8,10},{9,11},{10,... | collective-permute-start | bytes 294920 | tf_op jit(solution)/shard_map/ppermute | solution.py:27
  7.4 3.1 %collective-permute-done.1.far_ref = bf16[2,16,1536]{2,1,0:T(8,128)(2,1)S(1)} collective-permute-done((bf16[2,16,1536]{2,1,0:T(8,128)(2,1)S(1)}, bf16[2,16,1536]{2,1,0:T(8,128)(2,1)S(1)}, u32[]{:S(2)}, u32[]{:S(2)}) %collective-permute-start.1) | collective-permute-done | bytes 98336 | tf_op jit(solution)/shard_map/ppermute | solution.py:27
  10.5 1.7 %collective-permute-start.5 = (bf16[1,256,1024]{2,1,0:T(8,128)(2,1)}, bf16[1,256,1024]{2,1,0:T(8,128)(2,1)S(1)}, u32[]{:S(2)}, u32[]{:S(2)}) collective-permute-start(bf16[1,256,1024]{2,1,0:T(8,128)(2,1)} %get-tuple-element.83), channel_id=1, source_target_pairs={{0,2},{1,3},{2,0},{3,1},{4,6},{5,7},{6,4},{7,5},{8,10},{9,11},{10,... | collective-permute-start | bytes 1572872 | tf_op jit(solution)/shard_map/ppermute | solution.py:27
  14.1 2.7 %collective-permute-start.2 = (bf16[128,512]{1,0:T(8,128)(2,1)S(1)}, bf16[128,512]{1,0:T(8,128)(2,1)S(1)}, u32[]{:S(2)}, u32[]{:S(2)}) collective-permute-start(bf16[128,512]{1,0:T(8,128)(2,1)S(1)} %get-tuple-element.79.mine_ref), channel_id=1, source_target_pairs={{0,16},{4,20},{8,24},{12,28},{16,0},{20,4},{24,8},{28,12},{1,17},{... | collective-permute-start | bytes 393224 | tf_op jit(solution)/shard_map/ppermute | solution.py:27
  16.8 5.6 %collective-permute-done.2.other_ref = bf16[128,512]{1,0:T(8,128)(2,1)S(1)} collective-permute-done((bf16[128,512]{1,0:T(8,128)(2,1)S(1)}, bf16[128,512]{1,0:T(8,128)(2,1)S(1)}, u32[]{:S(2)}, u32[]{:S(2)}) %collective-permute-start.2) | collective-permute-done | bytes 131104 | tf_op jit(solution)/shard_map/ppermute | solution.py:27
  23.1 3.4 %collective-permute-start.4 = (bf16[1,128,512]{2,1,0:T(8,128)(2,1)S(1)}, bf16[1,128,512]{2,1,0:T(8,128)(2,1)S(1)}, u32[]{:S(2)}, u32[]{:S(2)}) collective-permute-start(bf16[1,128,512]{2,1,0:T(8,128)(2,1)S(1)} %bitcast.13), channel_id=1, source_target_pairs={{0,16},{4,20},{8,24},{12,28},{16,0},{20,4},{24,8},{28,12},{1,17},{... | collective-permute-start | bytes 393224 | tf_op jit(solution)/shard_map/ppermute | solution.py:27
  27.6 2.3 %collective-permute-done.4 = bf16[1,128,512]{2,1,0:T(8,128)(2,1)S(1)} collective-permute-done((bf16[1,128,512]{2,1,0:T(8,128)(2,1)S(1)}, bf16[1,128,512]{2,1,0:T(8,128)(2,1)S(1)}, u32[]{:S(2)}, u32[]{:S(2)}) %collective-permute-start.4) | collective-permute-done | bytes 131104 | tf_op jit(solution)/shard_map/ppermute | solution.py:27
  30.9 1.6 %collective-permute-start.6 = (bf16[272,512]{1,0:T(8,128)(2,1)S(1)}, bf16[272,512]{1,0:T(8,128)(2,1)S(1)}, u32[]{:S(2)}, u32[]{:S(2)}) collective-permute-start(bf16[272,512]{1,0:T(8,128)(2,1)S(1)} %shard_map.275.first_ref), channel_id=1, source_target_pairs={{0,4},{4,0},{8,12},{12,8},{16,20},{20,16},{24,28},{28,24},{1,5},{5... | collective-permute-start | bytes 835592 | tf_op jit(solution)/shard_map/ppermute | solution.py:27
  32.5 2.9 %collective-permute-start.8 = (bf16[2,128,512]{2,1,0:T(8,128)(2,1)S(1)}, bf16[2,128,512]{2,1,0:T(8,128)(2,1)S(1)}, u32[]{:S(2)}, u32[]{:S(2)}) collective-permute-start(bf16[2,128,512]{2,1,0:T(8,128)(2,1)S(1)} %pad_maximum_fusion.1), channel_id=1, source_target_pairs={{0,8},{4,12},{8,0},{12,4},{16,24},{20,28},{24,16},{28,20},{1,9},{5... | collective-permute-start | bytes 786440 | tf_op jit(solution)/shard_map/ppermute | solution.py:27
  35.3 4.7 %collective-permute-done.6.other_ref = bf16[272,512]{1,0:T(8,128)(2,1)S(1)} collective-permute-done((bf16[272,512]{1,0:T(8,128)(2,1)S(1)}, bf16[272,512]{1,0:T(8,128)(2,1)S(1)}, u32[]{:S(2)}, u32[]{:S(2)}) %collective-permute-start.6) | collective-permute-done | bytes 278560 | tf_op jit(solution)/shard_map/ppermute | solution.py:27
  40.0 2.1 %shard_map.276 = (bf16[1024,1024]{1,0:T(8,128)(2,1)S(1)}, bf16[1024,512]{1,0:T(8,128)(2,1)S(1)}, bf16[1024,128]{1,0:T(8,128)(2,1)S(1)}, bf16[128,1024]{1,0:T(8,1...) custom-call(bf16[272,512]{1,0:T(8,128)(2,1)S(1)} %shard_map.275.firs, ...), custom_call_target="tpu_custom_call" | custom-call | flops 1 | bytes 1 | tf_op jit(solution)/shard_map/pallas_call | solution.py:497
  43.7 9.7 %shard_map.277 = (bf16[1024,128]{1,0:T(8,128)(2,1)S(1)}, bf16[1024,384]{1,0:T(8,128)(2,1)S(1)}, f32[8,512]{1,0:T(8,128)S(1)}, bf16[4,64,512]{2,1,0:T(8,128)(2,1)S(1)}, f32[4,64,512]{2,1,0:T(8,128)S(1)}) custom-call(bf16[1024,1024]{1,0:T(8,128)(2,1)S(1)} %get-tuple-element.86.xg_ref, bf16[1024,512]{1,0:T(8,128)(2,1)S(1)} %get-tuple-element.87.na_ref, ...), custom_call_target="tpu_custom_call" | custom-call | flops 1 | bytes 1 | tf_op jit(solution)/shard_map/pallas_call | solution.py:497
  54.0 2.0 %collective-permute-done.9.other_ref = bf16[4,128,512]{2,1,0:T(8,128)(2,1)S(1)} collective-permute-done((bf16[4,128,512]{2,1,0:T(8,128)(2,1)S(1)}, bf16[4,128,512]{2,1,0:T(8,128)(2,1)S(1)}, u32[]{:S(2)}, u32[]{:S(2)}) %collective-permute-start.9) | collective-permute-done | bytes 524320 | tf_op jit(solution)/shard_map/ppermute | solution.py:27
  56.0 3.9 %shard_map.278 = (bf16[1024,512]{1,0:T(8,128)(2,1)S(1)}, bf16[1024,512]{1,0:T(8,128)(2,1)S(1)}, bf16[512,512]{1,0:T(8,128)(2,1)S(1)}, bf16[512,512]{1,0:T(8,128)...) custom-call(bf16[4,128,512]{2,1,0:T(8,128)(2,1)S(1)} %pad_maximum_fusion.second_ref, ...), custom_call_target="tpu_custom_call" | custom-call | flops 1 | bytes 1 | tf_op jit(solution)/shard_map/pallas_call | solution.py:497
  59.9 2.5 %collective-permute-start.10 = (bf16[4,80,512]{2,1,0:T(8,128)(2,1)S(1)}, bf16[4,80,512]{2,1,0:T(8,128)(2,1)S(1)}, u32[]{:S(2)}, u32[]{:S(2)}) collective-permute-start(bf16[4,80,512]{2,1,0:T(8,128)(2,1)S(1)} %get-tuple-element.108), channel_id=1, source_target_pairs={{0,4},{4,0},{8,12},{12,8},{16,20},{20,16},{24,28},{28,24},{1,5},{5... | collective-permute-start | bytes 983048 | tf_op jit(solution)/shard_map/ppermute | solution.py:27
  62.5 2.9 %collective-permute-start.12 = (bf16[2,64,512]{2,1,0:T(8,128)(2,1)S(1)}, bf16[2,64,512]{2,1,0:T(8,128)(2,1)S(1)}, u32[]{:S(2)}, u32[]{:S(2)}) collective-permute-start(bf16[2,64,512]{2,1,0:T(8,128)(2,1)S(1)} %slice.140), channel_id=1, source_target_pairs={{0,8},{4,12},{8,0},{12,4},{16,24},{20,28},{24,16},{28,20},{1,9},{5... | collective-permute-start | bytes 393224 | tf_op jit(solution)/shard_map/ppermute | solution.py:27
  65.4 2.5 %shard_map.279 = (bf16[2,256,1024]{2,1,0:T(8,128)(2,1)S(1)}, f32[2,256,1024]{2,1,0:T(8,128)S(1)}) custom-call(bf16[1024,1024]{1,0:T(8,128)(2,1)S(1)} %get-tuple-element.86.xg_ref, bf16[1024,128]{1,0:T(8,128)(2,1)S(1)} %get-tuple-element.97.att_ref, bf16[128,512]{1,0:T(8,128)(2,1)S(1)} %get-tuple-element.98.wo_ref, ...), custom_call_target="tpu_custom_call" | custom-call | flops 1 | bytes 1 | tf_op jit(solution)/shard_map/pallas_call | solution.py:497
  68.5 2.2 %collective-permute-start.15 = (bf16[1,64,512]{2,1,0:T(8,128)(2,1)S(1)}, bf16[1,64,512]{2,1,0:T(8,128)(2,1)S(1)}, u32[]{:S(2)}, u32[]{:S(2)}) collective-permute-start(bf16[1,64,512]{2,1,0:T(8,128)(2,1)S(1)} %slice.143), channel_id=1, source_target_pairs={{0,16},{4,20},{8,24},{12,28},{16,0},{20,4},{24,8},{28,12},{1,17},{... | collective-permute-start | bytes 196616 | tf_op jit(solution)/shard_map/ppermute | solution.py:27
  71.6 2.5 %collective-permute-start.14 = (bf16[2,80,512]{2,1,0:T(8,128)(2,1)S(1)}, bf16[2,80,512]{2,1,0:T(8,128)(2,1)S(1)}, u32[]{:S(2)}, u32[]{:S(2)}) collective-permute-start(bf16[2,80,512]{2,1,0:T(8,128)(2,1)S(1)} %slice.138), channel_id=1, source_target_pairs={{0,8},{4,12},{8,0},{12,4},{16,24},{20,28},{24,16},{28,20},{1,9},{5... | collective-permute-start | bytes 491528 | tf_op jit(solution)/shard_map/ppermute | solution.py:27
  76.7 5.6 %collective-permute-done.16 = bf16[4,64,512]{2,1,0:T(8,128)(2,1)S(1)} collective-permute-done((bf16[4,64,512]{2,1,0:T(8,128)(2,1)S(1)}, bf16[4,64,512]{2,1,0:T(8,128)(2,1)S(1)}, u32[]{:S(2)}, u32[]{:S(2)}) %collective-permute-start.16) | collective-permute-done | bytes 262176 | tf_op jit(solution)/shard_map/ppermute | solution.py:27
  82.5 1.7 %collective-permute-start.17 = (bf16[1,80,512]{2,1,0:T(8,128)(2,1)S(1)}, bf16[1,80,512]{2,1,0:T(8,128)(2,1)S(1)}, u32[]{:S(2)}, u32[]{:S(2)}) collective-permute-start(bf16[1,80,512]{2,1,0:T(8,128)(2,1)S(1)} %slice.141), channel_id=1, source_target_pairs={{0,16},{4,20},{8,24},{12,28},{16,0},{20,4},{24,8},{28,12},{1,17},{... | collective-permute-start | bytes 245768 | tf_op jit(solution)/shard_map/ppermute | solution.py:27
  85.2 3.4 %collective-permute-done.17 = bf16[1,80,512]{2,1,0:T(8,128)(2,1)S(1)} collective-permute-done((bf16[1,80,512]{2,1,0:T(8,128)(2,1)S(1)}, bf16[1,80,512]{2,1,0:T(8,128)(2,1)S(1)}, u32[]{:S(2)}, u32[]{:S(2)}) %collective-permute-start.17) | collective-permute-done | bytes 81952 | tf_op jit(solution)/shard_map/ppermute | solution.py:27
  92.2 2.7 %collective-permute-done.20.near_ref = bf16[2,32,896]{2,1,0:T(8,128)(2,1)S(1)} collective-permute-done((bf16[2,32,896]{2,1,0:T(8,128)(2,1)S(1)}, bf16[2,32,896]{2,1,0:T(8,128)(2,1)S(1)}, u32[]{:S(2)}, u32[]{:S(2)}) %collective-permute-start.20) | collective-permute-done | bytes 114720 | tf_op jit(solution)/shard_map/ppermute | solution.py:27
  (76 shorter events, 19.9 us)
Async XLA Ops:
  2.8 1.7 %collective-permute-start = (bf16[2,16,1536]{2,1,0:T(8,128)(2,1)}, bf16[2,16,1536]{2,1,0:T(8,128)(2,1)S(1)}, u32[]{:S(2)}, u32[]{:S(2)}) collective-permute-start(bf16[2,16,1536]{2,1,0:T(8,128)(2,1)} %get-tuple-element.78), channel_id=1, source_target_pairs={{0,1},{1,0},{2,3},{3,2},{4,5},{5,4},{6,7},{7,6},{8,9},{9,8},{10,11... | collective-permute-start | bytes 294920 | tf_op jit(solution)/shard_map/ppermute | solution.py:27
  4.5 6.1 %collective-permute-start.1 = (bf16[2,16,1536]{2,1,0:T(8,128)(2,1)S(1)}, bf16[2,16,1536]{2,1,0:T(8,128)(2,1)S(1)}, u32[]{:S(2)}, u32[]{:S(2)}) collective-permute-start(bf16[2,16,1536]{2,1,0:T(8,128)(2,1)S(1)} %pad_maximum_fusion.3), channel_id=1, source_target_pairs={{0,2},{1,3},{2,0},{3,1},{4,6},{5,7},{6,4},{7,5},{8,10},{9,11},{10,... | collective-permute-start | bytes 294920 | tf_op jit(solution)/shard_map/ppermute | solution.py:27
  10.5 20.2 %collective-permute-start.5 = (bf16[1,256,1024]{2,1,0:T(8,128)(2,1)}, bf16[1,256,1024]{2,1,0:T(8,128)(2,1)S(1)}, u32[]{:S(2)}, u32[]{:S(2)}) collective-permute-start(bf16[1,256,1024]{2,1,0:T(8,128)(2,1)} %get-tuple-element.83), channel_id=1, source_target_pairs={{0,2},{1,3},{2,0},{3,1},{4,6},{5,7},{6,4},{7,5},{8,10},{9,11},{10,... | collective-permute-start | bytes 1572872 | tf_op jit(solution)/shard_map/ppermute | solution.py:27
  14.1 8.2 %collective-permute-start.2 = (bf16[128,512]{1,0:T(8,128)(2,1)S(1)}, bf16[128,512]{1,0:T(8,128)(2,1)S(1)}, u32[]{:S(2)}, u32[]{:S(2)}) collective-permute-start(bf16[128,512]{1,0:T(8,128)(2,1)S(1)} %get-tuple-element.79.mine_ref), channel_id=1, source_target_pairs={{0,16},{4,20},{8,24},{12,28},{16,0},{20,4},{24,8},{28,12},{1,17},{... | collective-permute-start | bytes 393224 | tf_op jit(solution)/shard_map/ppermute | solution.py:27
  22.4 8.4 %collective-permute-start.3 = (bf16[176,512]{1,0:T(8,128)(2,1)S(1)}, bf16[176,512]{1,0:T(8,128)(2,1)S(1)}, u32[]{:S(2)}, u32[]{:S(2)}) collective-permute-start(bf16[176,512]{1,0:T(8,128)(2,1)S(1)} %shard_map.274.mine_ref), channel_id=1, source_target_pairs={{0,8},{4,12},{8,0},{12,4},{16,24},{20,28},{24,16},{28,20},{1,9},{5... | collective-permute-start | bytes 540680 | tf_op jit(solution)/shard_map/ppermute | solution.py:27
  23.1 6.8 %collective-permute-start.4 = (bf16[1,128,512]{2,1,0:T(8,128)(2,1)S(1)}, bf16[1,128,512]{2,1,0:T(8,128)(2,1)S(1)}, u32[]{:S(2)}, u32[]{:S(2)}) collective-permute-start(bf16[1,128,512]{2,1,0:T(8,128)(2,1)S(1)} %bitcast.13), channel_id=1, source_target_pairs={{0,16},{4,20},{8,24},{12,28},{16,0},{20,4},{24,8},{28,12},{1,17},{... | collective-permute-start | bytes 393224 | tf_op jit(solution)/shard_map/ppermute | solution.py:27
  30.8 9.2 %collective-permute-start.7 = (bf16[2,256,1024]{2,1,0:T(8,128)(2,1)S(1)}, bf16[2,256,1024]{2,1,0:T(8,128)(2,1)S(1)}, u32[]{:S(2)}, u32[]{:S(2)}) collective-permute-start(bf16[2,256,1024]{2,1,0:T(8,128)(2,1)S(1)} %constant_dynamic-update-slice_fusion.x_ref), channel_id=1, source_target_pairs={{0,1},{1,0},{2,3},{3,2},{4,5},{5,4},{6,7},{7,6},{8,9},{9,8},{10,11... | collective-permute-start | bytes 3145736 | tf_op jit(solution)/shard_map/ppermute | solution.py:27
  30.9 9.1 %collective-permute-start.6 = (bf16[272,512]{1,0:T(8,128)(2,1)S(1)}, bf16[272,512]{1,0:T(8,128)(2,1)S(1)}, u32[]{:S(2)}, u32[]{:S(2)}) collective-permute-start(bf16[272,512]{1,0:T(8,128)(2,1)S(1)} %shard_map.275.first_ref), channel_id=1, source_target_pairs={{0,4},{4,0},{8,12},{12,8},{16,20},{20,16},{24,28},{28,24},{1,5},{5... | collective-permute-start | bytes 835592 | tf_op jit(solution)/shard_map/ppermute | solution.py:27
  32.5 9.6 %collective-permute-start.8 = (bf16[2,128,512]{2,1,0:T(8,128)(2,1)S(1)}, bf16[2,128,512]{2,1,0:T(8,128)(2,1)S(1)}, u32[]{:S(2)}, u32[]{:S(2)}) collective-permute-start(bf16[2,128,512]{2,1,0:T(8,128)(2,1)S(1)} %pad_maximum_fusion.1), channel_id=1, source_target_pairs={{0,8},{4,12},{8,0},{12,4},{16,24},{20,28},{24,16},{28,20},{1,9},{5... | collective-permute-start | bytes 786440 | tf_op jit(solution)/shard_map/ppermute | solution.py:27
  42.2 13.8 %collective-permute-start.9 = (bf16[4,128,512]{2,1,0:T(8,128)(2,1)S(1)}, bf16[4,128,512]{2,1,0:T(8,128)(2,1)S(1)}, u32[]{:S(2)}, u32[]{:S(2)}) collective-permute-start(bf16[4,128,512]{2,1,0:T(8,128)(2,1)S(1)} %pad_maximum_fusion.second_ref), channel_id=1, source_target_pairs={{0,4},{4,0},{8,12},{12,8},{16,20},{20,16},{24,28},{28,24},{1,5},{5... | collective-permute-start | bytes 1572872 | tf_op jit(solution)/shard_map/ppermute | solution.py:27
  53.4 9.0 %collective-permute-start.11 = (bf16[4,64,512]{2,1,0:T(8,128)(2,1)S(1)}, bf16[4,64,512]{2,1,0:T(8,128)(2,1)S(1)}, u32[]{:S(2)}, u32[]{:S(2)}) collective-permute-start(bf16[4,64,512]{2,1,0:T(8,128)(2,1)S(1)} %get-tuple-element.111), channel_id=1, source_target_pairs={{0,4},{4,0},{8,12},{12,8},{16,20},{20,16},{24,28},{28,24},{1,5},{5... | collective-permute-start | bytes 786440 | tf_op jit(solution)/shard_map/ppermute | solution.py:27
  59.9 8.5 %collective-permute-start.10 = (bf16[4,80,512]{2,1,0:T(8,128)(2,1)S(1)}, bf16[4,80,512]{2,1,0:T(8,128)(2,1)S(1)}, u32[]{:S(2)}, u32[]{:S(2)}) collective-permute-start(bf16[4,80,512]{2,1,0:T(8,128)(2,1)S(1)} %get-tuple-element.108), channel_id=1, source_target_pairs={{0,4},{4,0},{8,12},{12,8},{16,20},{20,16},{24,28},{28,24},{1,5},{5... | collective-permute-start | bytes 983048 | tf_op jit(solution)/shard_map/ppermute | solution.py:27
  62.5 5.8 %collective-permute-start.12 = (bf16[2,64,512]{2,1,0:T(8,128)(2,1)S(1)}, bf16[2,64,512]{2,1,0:T(8,128)(2,1)S(1)}, u32[]{:S(2)}, u32[]{:S(2)}) collective-permute-start(bf16[2,64,512]{2,1,0:T(8,128)(2,1)S(1)} %slice.140), channel_id=1, source_target_pairs={{0,8},{4,12},{8,0},{12,4},{16,24},{20,28},{24,16},{28,20},{1,9},{5... | collective-permute-start | bytes 393224 | tf_op jit(solution)/shard_map/ppermute | solution.py:27
  68.4 3.1 %collective-permute-start.13 = (bf16[2,256,1024]{2,1,0:T(8,128)(2,1)S(1)}, bf16[2,256,1024]{2,1,0:T(8,128)(2,1)S(1)}, u32[]{:S(2)}, u32[]{:S(2)}) collective-permute-start(bf16[2,256,1024]{2,1,0:T(8,128)(2,1)S(1)} %get-tuple-element.112), channel_id=1, source_target_pairs={{0,1},{1,0},{2,3},{3,2},{4,5},{5,4},{6,7},{7,6},{8,9},{9,8},{10,11... | collective-permute-start | bytes 3145736 | tf_op jit(solution)/shard_map/ppermute | solution.py:27
  68.5 13.9 %collective-permute-start.15 = (bf16[1,64,512]{2,1,0:T(8,128)(2,1)S(1)}, bf16[1,64,512]{2,1,0:T(8,128)(2,1)S(1)}, u32[]{:S(2)}, u32[]{:S(2)}) collective-permute-start(bf16[1,64,512]{2,1,0:T(8,128)(2,1)S(1)} %slice.143), channel_id=1, source_target_pairs={{0,16},{4,20},{8,24},{12,28},{16,0},{20,4},{24,8},{28,12},{1,17},{... | collective-permute-start | bytes 196616 | tf_op jit(solution)/shard_map/ppermute | solution.py:27
  71.6 10.8 %collective-permute-start.14 = (bf16[2,80,512]{2,1,0:T(8,128)(2,1)S(1)}, bf16[2,80,512]{2,1,0:T(8,128)(2,1)S(1)}, u32[]{:S(2)}, u32[]{:S(2)}) collective-permute-start(bf16[2,80,512]{2,1,0:T(8,128)(2,1)S(1)} %slice.138), channel_id=1, source_target_pairs={{0,8},{4,12},{8,0},{12,4},{16,24},{20,28},{24,16},{28,20},{1,9},{5... | collective-permute-start | bytes 491528 | tf_op jit(solution)/shard_map/ppermute | solution.py:27
  74.1 8.2 %collective-permute-start.16 = (bf16[4,64,512]{2,1,0:T(8,128)(2,1)S(1)}, bf16[4,64,512]{2,1,0:T(8,128)(2,1)S(1)}, u32[]{:S(2)}, u32[]{:S(2)}) collective-permute-start(bf16[4,64,512]{2,1,0:T(8,128)(2,1)S(1)} %get-tuple-element.118), channel_id=1, source_target_pairs={{0,4},{4,0},{8,12},{12,8},{16,20},{20,16},{24,28},{28,24},{1,5},{5... | collective-permute-start | bytes 786440 | tf_op jit(solution)/shard_map/ppermute | solution.py:27
  76.1 13.7 %collective-permute-start.19 = (bf16[1,256,1024]{2,1,0:T(8,128)(2,1)S(1)}, bf16[1,256,1024]{2,1,0:T(8,128)(2,1)S(1)}, u32[]{:S(2)}, u32[]{:S(2)}) collective-permute-start(bf16[1,256,1024]{2,1,0:T(8,128)(2,1)S(1)} %slice.137), channel_id=1, source_target_pairs={{0,2},{1,3},{2,0},{3,1},{4,6},{5,7},{6,4},{7,5},{8,10},{9,11},{10,... | collective-permute-start | bytes 1572872 | tf_op jit(solution)/shard_map/ppermute | solution.py:27
  82.5 6.2 %collective-permute-start.17 = (bf16[1,80,512]{2,1,0:T(8,128)(2,1)S(1)}, bf16[1,80,512]{2,1,0:T(8,128)(2,1)S(1)}, u32[]{:S(2)}, u32[]{:S(2)}) collective-permute-start(bf16[1,80,512]{2,1,0:T(8,128)(2,1)S(1)} %slice.141), channel_id=1, source_target_pairs={{0,16},{4,20},{8,24},{12,28},{16,0},{20,4},{24,8},{28,12},{1,17},{... | collective-permute-start | bytes 245768 | tf_op jit(solution)/shard_map/ppermute | solution.py:27
  84.2 5.6 %collective-permute-start.18 = (bf16[2,64,512]{2,1,0:T(8,128)(2,1)S(1)}, bf16[2,64,512]{2,1,0:T(8,128)(2,1)S(1)}, u32[]{:S(2)}, u32[]{:S(2)}) collective-permute-start(bf16[2,64,512]{2,1,0:T(8,128)(2,1)S(1)} %slice.139), channel_id=1, source_target_pairs={{0,8},{4,12},{8,0},{12,4},{16,24},{20,28},{24,16},{28,20},{1,9},{5... | collective-permute-start | bytes 393224 | tf_op jit(solution)/shard_map/ppermute | solution.py:27
  84.5 11.3 %collective-permute-start.22 = (f32[16,512]{1,0:T(8,128)S(1)}, f32[16,512]{1,0:T(8,128)S(1)}, u32[]{:S(2)}, u32[]{:S(2)}) collective-permute-start(f32[16,512]{1,0:T(8,128)S(1)} %slice_bitcast_fusion.2), channel_id=1, source_target_pairs={{0,0},{8,1},{16,2},{24,3},{4,4},{12,5},{20,6},{28,7},{1,8},{9,9},{... | collective-permute-start | bytes 98312 | tf_op jit(solution)/shard_map/ppermute | solution.py:1055
  90.0 4.9 %collective-permute-start.20 = (bf16[2,32,896]{2,1,0:T(8,128)(2,1)S(1)}, bf16[2,32,896]{2,1,0:T(8,128)(2,1)S(1)}, u32[]{:S(2)}, u32[]{:S(2)}) collective-permute-start(bf16[2,32,896]{2,1,0:T(8,128)(2,1)S(1)} %get-tuple-element.125), channel_id=1, source_target_pairs={{0,2},{1,3},{2,0},{3,1},{4,6},{5,7},{6,4},{7,5},{8,10},{9,11},{10,... | collective-permute-start | bytes 344072 | tf_op jit(solution)/shard_map/ppermute | solution.py:27
  90.6 5.9 %collective-permute-start.23 = (bf16[1,64,512]{2,1,0:T(8,128)(2,1)S(1)}, bf16[1,64,512]{2,1,0:T(8,128)(2,1)S(1)}, u32[]{:S(2)}, u32[]{:S(2)}) collective-permute-start(bf16[1,64,512]{2,1,0:T(8,128)(2,1)S(1)} %slice.142), channel_id=1, source_target_pairs={{0,16},{4,20},{8,24},{12,28},{16,0},{20,4},{24,8},{28,12},{1,17},{... | collective-permute-start | bytes 196616 | tf_op jit(solution)/shard_map/ppermute | solution.py:27
  94.9 1.6 %collective-permute-start.21 = (bf16[2,32,896]{2,1,0:T(8,128)(2,1)S(1)}, bf16[2,32,896]{2,1,0:T(8,128)(2,1)S(1)}, u32[]{:S(2)}, u32[]{:S(2)}) collective-permute-start(bf16[2,32,896]{2,1,0:T(8,128)(2,1)S(1)} %pad_maximum_fusion.2), channel_id=1, source_target_pairs={{0,1},{1,0},{2,3},{3,2},{4,5},{5,4},{6,7},{7,6},{8,9},{9,8},{10,11... | collective-permute-start | bytes 344072 | tf_op jit(solution)/shard_map/ppermute | solution.py:27
  (5 other events, 108.4 us)

commit v5 on v4

--- a/solution.py
+++ b/solution.py
@@ -988,7 +988,7 @@
         [], 2 * tokens * width * 4 * part, 0,
         *first, *x_pair, cosine, sine, jnp.asarray(table),
     )
-    second = jnp.concatenate([second, after(second_other, normed_a)], 0)
+    second = jnp.concatenate([second, after(second_other, first[1])], 0)
     second = (second, exchange(second, "dp", owners, 0))
     chunk = 5 * rows
     attended, grad_proj, small, sent_a, kept_a = call(
@@ -1022,6 +1022,14 @@
     other_u = exchange(sent_u, "dp", owners, 0)
     sent_a, kept_a = fold(kept_a, other_a)
     other_a = exchange(sent_a, "dp", owners, 1)
+    down_rows = w_down.shape[0]
+    sent_d, kept_d = call(
+        down_kernel,
+        (shape((half, down_rows, width), BF16), shape((half, down_rows, width), F32)),
+        [pltpu.VMEM((hidden, width), F32)],
+        2 * tokens * width * hidden, 0,
+        active, xg,
+    )
     sent_x, kept_x = call(
         join_kernel,
         (shape((2, local, 2 * width), BF16), shape((2, local, 2 * width), F32)),
@@ -1029,14 +1037,6 @@
         4 * tokens * width * hidden, 0,
         xg, attended, full_out, active, full_down, vectors,
         grad_proj, full_qkv, grad_hidden, full_up,
-    )
-    down_rows = w_down.shape[0]
-    sent_d, kept_d = call(
-        down_kernel,
-        (shape((half, down_rows, width), BF16), shape((half, down_rows, width), F32)),
-        [pltpu.VMEM((hidden, width), F32)],
-        2 * tokens * width * hidden, 0,
-        active, xg,
     )
     other_x = exchange(after(sent_x, other_u, other_a), "seq", groups, 0)
     other_u, other_x, sent_d, = lax.optimization_barrier((other_u, other_x, sent_d,))

time: 97.9 us -> 97.6 us (level)
  starting transfers between devices: 35.6 us -> 31.1 us
  waiting for transfers between devices: 32.9 us -> 37.2 us
    ppermute x23, starting transfers between devices: 35 us -> 30.5 us  [exchange(): return lax.ppermute(value, axis, [(i, i ^ 1 << bit) for i in range(size)])]
    ppermute x23, waiting for transfers between devices: 32.9 us -> 37.2 us  [exchange(): return lax.ppermute(value, axis, [(i, i ^ 1 << bit) for i in range(size)])]
  transfers between devices with their start and end apart: 24 -> 24, of which waited for: 14 -> 13; matrix products, arithmetic and copies ran while one was open for 4% -> 4% of each run, Pallas kernels for 20% -> 20%
where the time goes in v5:
time: 97.6 us; the launch traced here: 97.3 us
  waiting for transfers between devices  37.2 us (38%)
  starting transfers between devices  31.1 us (32%)
  Pallas kernels  22.1 us (23%)
  local copies, waits for them, and re-layouts  4.7 us (5%)
  between operations  1.13 us (1%)
  other arithmetic  1.08 us (1%)
    ppermute x23, waiting for transfers between devices, exchange(): return lax.ppermute(value, axis, [(i, i ^ 1 << bit) for i in range(size)])  37.2 us
    ppermute x23, starting transfers between devices, exchange(): return lax.ppermute(value, axis, [(i, i ^ 1 << bit) for i in range(size)])  30.5 us
    pallas_call x11, Pallas kernels, call(): pl.pallas_call(kernel, out_shape=tuple(outs), in_specs=whole(len(operands...  22.1 us
    unnamed x11, local copies, waits for them, and re-layouts  2.82 us
  transfers between devices with their start and end apart: 24, of which 13 were waited for; matrix products, arithmetic and copies ran while one was open for 4% of the time, Pallas kernels for 20%

profile of v5, /device:TPU:0, one launch (start us, length us, event | category | flops | bytes accessed | tf_op | source)
XLA Modules:
  0.0 97.3 jit_solution(13212220448238407896)
XLA Ops:
  0.7 2.1 %shard_map.272 = (bf16[2,16,1536]{2,1,0:T(8,128)(2,1)}, bf16[2,16,1536]{2,1,0:T(8,128)(2,1)}, bf16[1,256,1024]{2,1,0:T(8,128)(2,1)}) custom-call(bf16[1,256,512]{2,1,0:T(8,128)(2,1)} %refs_0_.1, bf16[1,256,512]{2,1,0:T(8,128)(2,1)} %refs_1_.1, bf16[16,1536]{1,0:T(8,128)(2,1)} %refs_2_.1, bf16[16,2048]{1,0:T(8,128)(2,1)} %refs_3_.1, bf16[16,512]{1,0:T(8,128)(2,1)} %refs_4_.1, ...), custom_call_target="tpu_custom_call" | custom-call | flops 1 | bytes 1 | tf_op jit(solution)/shard_map/pallas_call | solution.py:497
  4.5 2.9 %collective-permute-start.1 = (bf16[2,16,1536]{2,1,0:T(8,128)(2,1)S(1)}, bf16[2,16,1536]{2,1,0:T(8,128)(2,1)S(1)}, u32[]{:S(2)}, u32[]{:S(2)}) collective-permute-start(bf16[2,16,1536]{2,1,0:T(8,128)(2,1)S(1)} %pad_maximum_fusion.3), channel_id=1, source_target_pairs={{0,2},{1,3},{2,0},{3,1},{4,6},{5,7},{6,4},{7,5},{8,10},{9,11},{10,... | collective-permute-start | bytes 294920 | tf_op jit(solution)/shard_map/ppermute | solution.py:27
  7.4 3.1 %collective-permute-done.1.far_ref = bf16[2,16,1536]{2,1,0:T(8,128)(2,1)S(1)} collective-permute-done((bf16[2,16,1536]{2,1,0:T(8,128)(2,1)S(1)}, bf16[2,16,1536]{2,1,0:T(8,128)(2,1)S(1)}, u32[]{:S(2)}, u32[]{:S(2)}) %collective-permute-start.1) | collective-permute-done | bytes 98336 | tf_op jit(solution)/shard_map/ppermute | solution.py:27
  10.5 1.7 %collective-permute-start.5 = (bf16[1,256,1024]{2,1,0:T(8,128)(2,1)}, bf16[1,256,1024]{2,1,0:T(8,128)(2,1)S(1)}, u32[]{:S(2)}, u32[]{:S(2)}) collective-permute-start(bf16[1,256,1024]{2,1,0:T(8,128)(2,1)} %get-tuple-element.83), channel_id=1, source_target_pairs={{0,2},{1,3},{2,0},{3,1},{4,6},{5,7},{6,4},{7,5},{8,10},{9,11},{10,... | collective-permute-start | bytes 1572872 | tf_op jit(solution)/shard_map/ppermute | solution.py:27
  14.1 2.7 %collective-permute-start.2 = (bf16[128,512]{1,0:T(8,128)(2,1)S(1)}, bf16[128,512]{1,0:T(8,128)(2,1)S(1)}, u32[]{:S(2)}, u32[]{:S(2)}) collective-permute-start(bf16[128,512]{1,0:T(8,128)(2,1)S(1)} %get-tuple-element.79.mine_ref), channel_id=1, source_target_pairs={{0,16},{4,20},{8,24},{12,28},{16,0},{20,4},{24,8},{28,12},{1,17},{... | collective-permute-start | bytes 393224 | tf_op jit(solution)/shard_map/ppermute | solution.py:27
  16.7 5.6 %collective-permute-done.2.other_ref = bf16[128,512]{1,0:T(8,128)(2,1)S(1)} collective-permute-done((bf16[128,512]{1,0:T(8,128)(2,1)S(1)}, bf16[128,512]{1,0:T(8,128)(2,1)S(1)}, u32[]{:S(2)}, u32[]{:S(2)}) %collective-permute-start.2) | collective-permute-done | bytes 131104 | tf_op jit(solution)/shard_map/ppermute | solution.py:27
  23.1 3.4 %collective-permute-start.4 = (bf16[1,128,512]{2,1,0:T(8,128)(2,1)S(1)}, bf16[1,128,512]{2,1,0:T(8,128)(2,1)S(1)}, u32[]{:S(2)}, u32[]{:S(2)}) collective-permute-start(bf16[1,128,512]{2,1,0:T(8,128)(2,1)S(1)} %bitcast.13), channel_id=1, source_target_pairs={{0,16},{4,20},{8,24},{12,28},{16,0},{20,4},{24,8},{28,12},{1,17},{... | collective-permute-start | bytes 393224 | tf_op jit(solution)/shard_map/ppermute | solution.py:27
  27.5 2.3 %collective-permute-done.4 = bf16[1,128,512]{2,1,0:T(8,128)(2,1)S(1)} collective-permute-done((bf16[1,128,512]{2,1,0:T(8,128)(2,1)S(1)}, bf16[1,128,512]{2,1,0:T(8,128)(2,1)S(1)}, u32[]{:S(2)}, u32[]{:S(2)}) %collective-permute-start.4) | collective-permute-done | bytes 131104 | tf_op jit(solution)/shard_map/ppermute | solution.py:27
  30.9 1.6 %collective-permute-start.6 = (bf16[272,512]{1,0:T(8,128)(2,1)S(1)}, bf16[272,512]{1,0:T(8,128)(2,1)S(1)}, u32[]{:S(2)}, u32[]{:S(2)}) collective-permute-start(bf16[272,512]{1,0:T(8,128)(2,1)S(1)} %shard_map.275.first_ref), channel_id=1, source_target_pairs={{0,4},{4,0},{8,12},{12,8},{16,20},{20,16},{24,28},{28,24},{1,5},{5... | collective-permute-start | bytes 835592 | tf_op jit(solution)/shard_map/ppermute | solution.py:27
  32.4 2.9 %collective-permute-start.8 = (bf16[2,128,512]{2,1,0:T(8,128)(2,1)S(1)}, bf16[2,128,512]{2,1,0:T(8,128)(2,1)S(1)}, u32[]{:S(2)}, u32[]{:S(2)}) collective-permute-start(bf16[2,128,512]{2,1,0:T(8,128)(2,1)S(1)} %pad_maximum_fusion.1), channel_id=1, source_target_pairs={{0,8},{4,12},{8,0},{12,4},{16,24},{20,28},{24,16},{28,20},{1,9},{5... | collective-permute-start | bytes 786440 | tf_op jit(solution)/shard_map/ppermute | solution.py:27
  35.3 6.7 %collective-permute-done.8 = bf16[2,128,512]{2,1,0:T(8,128)(2,1)S(1)} collective-permute-done((bf16[2,128,512]{2,1,0:T(8,128)(2,1)S(1)}, bf16[2,128,512]{2,1,0:T(8,128)(2,1)S(1)}, u32[]{:S(2)}, u32[]{:S(2)}) %collective-permute-start.8) | collective-permute-done | bytes 262176 | tf_op jit(solution)/shard_map/ppermute | solution.py:27
  42.7 2.0 %shard_map.276 = (bf16[1024,1024]{1,0:T(8,128)(2,1)S(1)}, bf16[1024,512]{1,0:T(8,128)(2,1)S(1)}, bf16[1024,128]{1,0:T(8,128)(2,1)S(1)}, bf16[128,1024]{1,0:T(8,1...) custom-call(bf16[272,512]{1,0:T(8,128)(2,1)S(1)} %shard_map.275.firs, ...), custom_call_target="tpu_custom_call" | custom-call | flops 1 | bytes 1 | tf_op jit(solution)/shard_map/pallas_call | solution.py:497
  44.7 9.7 %shard_map.277 = (bf16[1024,128]{1,0:T(8,128)(2,1)S(1)}, bf16[1024,384]{1,0:T(8,128)(2,1)S(1)}, f32[8,512]{1,0:T(8,128)S(1)}, bf16[4,64,512]{2,1,0:T(8,128)(2,1)S(1)}, f32[4,64,512]{2,1,0:T(8,128)S(1)}) custom-call(bf16[1024,1024]{1,0:T(8,128)(2,1)S(1)} %get-tuple-element.86.xg_ref, bf16[1024,512]{1,0:T(8,128)(2,1)S(1)} %get-tuple-element.87.na_ref, ...), custom_call_target="tpu_custom_call" | custom-call | flops 1 | bytes 1 | tf_op jit(solution)/shard_map/pallas_call | solution.py:497
  56.0 3.9 %shard_map.278 = (bf16[1024,512]{1,0:T(8,128)(2,1)S(1)}, bf16[1024,512]{1,0:T(8,128)(2,1)S(1)}, bf16[512,512]{1,0:T(8,128)(2,1)S(1)}, bf16[512,512]{1,0:T(8,128)...) custom-call(bf16[4,128,512]{2,1,0:T(8,128)(2,1)S(1)} %pad_maximum_fusion.second_ref, ...), custom_call_target="tpu_custom_call" | custom-call | flops 1 | bytes 1 | tf_op jit(solution)/shard_map/pallas_call | solution.py:497
  60.5 2.0 %collective-permute-done.11 = bf16[4,64,512]{2,1,0:T(8,128)(2,1)S(1)} collective-permute-done((bf16[4,64,512]{2,1,0:T(8,128)(2,1)S(1)}, bf16[4,64,512]{2,1,0:T(8,128)(2,1)S(1)}, u32[]{:S(2)}, u32[]{:S(2)}) %collective-permute-start.11) | collective-permute-done | bytes 262176 | tf_op jit(solution)/shard_map/ppermute | solution.py:27
  62.6 2.1 %collective-permute-start.12 = (bf16[2,64,512]{2,1,0:T(8,128)(2,1)S(1)}, bf16[2,64,512]{2,1,0:T(8,128)(2,1)S(1)}, u32[]{:S(2)}, u32[]{:S(2)}) collective-permute-start(bf16[2,64,512]{2,1,0:T(8,128)(2,1)S(1)} %slice.140), channel_id=1, source_target_pairs={{0,8},{4,12},{8,0},{12,4},{16,24},{20,28},{24,16},{28,20},{1,9},{5... | collective-permute-start | bytes 393224 | tf_op jit(solution)/shard_map/ppermute | solution.py:27
  64.7 2.5 %shard_map.279 = (bf16[2,256,1024]{2,1,0:T(8,128)(2,1)S(1)}, f32[2,256,1024]{2,1,0:T(8,128)S(1)}) custom-call(bf16[1024,1024]{1,0:T(8,128)(2,1)S(1)} %get-tuple-element.86.xg_ref, bf16[1024,128]{1,0:T(8,128)(2,1)S(1)} %get-tuple-element.97.att_ref, bf16[128,512]{1,0:T(8,128)(2,1)S(1)} %get-tuple-element.98.wo_ref, ...), custom_call_target="tpu_custom_call" | custom-call | flops 1 | bytes 1 | tf_op jit(solution)/shard_map/pallas_call | solution.py:497
  67.2 2.0 %collective-permute-done.10 = bf16[4,80,512]{2,1,0:T(8,128)(2,1)S(1)} collective-permute-done((bf16[4,80,512]{2,1,0:T(8,128)(2,1)S(1)}, bf16[4,80,512]{2,1,0:T(8,128)(2,1)S(1)}, u32[]{:S(2)}, u32[]{:S(2)}) %collective-permute-start.10) | collective-permute-done | bytes 327712 | tf_op jit(solution)/shard_map/ppermute | solution.py:27
  70.0 1.8 %collective-permute-start.15 = (bf16[1,64,512]{2,1,0:T(8,128)(2,1)S(1)}, bf16[1,64,512]{2,1,0:T(8,128)(2,1)S(1)}, u32[]{:S(2)}, u32[]{:S(2)}) collective-permute-start(bf16[1,64,512]{2,1,0:T(8,128)(2,1)S(1)} %slice.143), channel_id=1, source_target_pairs={{0,16},{4,20},{8,24},{12,28},{16,0},{20,4},{24,8},{28,12},{1,17},{... | collective-permute-start | bytes 196616 | tf_op jit(solution)/shard_map/ppermute | solution.py:27
  72.0 1.8 %collective-permute-start.14 = (bf16[2,80,512]{2,1,0:T(8,128)(2,1)S(1)}, bf16[2,80,512]{2,1,0:T(8,128)(2,1)S(1)}, u32[]{:S(2)}, u32[]{:S(2)}) collective-permute-start(bf16[2,80,512]{2,1,0:T(8,128)(2,1)S(1)} %slice.138), channel_id=1, source_target_pairs={{0,8},{4,12},{8,0},{12,4},{16,24},{20,28},{24,16},{28,20},{1,9},{5... | collective-permute-start | bytes 491528 | tf_op jit(solution)/shard_map/ppermute | solution.py:27
  76.0 5.9 %collective-permute-done.16 = bf16[4,64,512]{2,1,0:T(8,128)(2,1)S(1)} collective-permute-done((bf16[4,64,512]{2,1,0:T(8,128)(2,1)S(1)}, bf16[4,64,512]{2,1,0:T(8,128)(2,1)S(1)}, u32[]{:S(2)}, u32[]{:S(2)}) %collective-permute-start.16) | collective-permute-done | bytes 262176 | tf_op jit(solution)/shard_map/ppermute | solution.py:27
  82.2 1.7 %collective-permute-start.17 = (bf16[1,80,512]{2,1,0:T(8,128)(2,1)S(1)}, bf16[1,80,512]{2,1,0:T(8,128)(2,1)S(1)}, u32[]{:S(2)}, u32[]{:S(2)}) collective-permute-start(bf16[1,80,512]{2,1,0:T(8,128)(2,1)S(1)} %slice.141), channel_id=1, source_target_pairs={{0,16},{4,20},{8,24},{12,28},{16,0},{20,4},{24,8},{28,12},{1,17},{... | collective-permute-start | bytes 245768 | tf_op jit(solution)/shard_map/ppermute | solution.py:27
  84.9 3.4 %collective-permute-done.17 = bf16[1,80,512]{2,1,0:T(8,128)(2,1)S(1)} collective-permute-done((bf16[1,80,512]{2,1,0:T(8,128)(2,1)S(1)}, bf16[1,80,512]{2,1,0:T(8,128)(2,1)S(1)}, u32[]{:S(2)}, u32[]{:S(2)}) %collective-permute-start.17) | collective-permute-done | bytes 81952 | tf_op jit(solution)/shard_map/ppermute | solution.py:27
  91.6 3.2 %collective-permute-done.20.near_ref = bf16[2,32,896]{2,1,0:T(8,128)(2,1)S(1)} collective-permute-done((bf16[2,32,896]{2,1,0:T(8,128)(2,1)S(1)}, bf16[2,32,896]{2,1,0:T(8,128)(2,1)S(1)}, u32[]{:S(2)}, u32[]{:S(2)}) %collective-permute-start.20) | collective-permute-done | bytes 114720 | tf_op jit(solution)/shard_map/ppermute | solution.py:27
  (76 shorter events, 19.2 us)
Async XLA Ops:
  2.8 1.7 %collective-permute-start = (bf16[2,16,1536]{2,1,0:T(8,128)(2,1)}, bf16[2,16,1536]{2,1,0:T(8,128)(2,1)S(1)}, u32[]{:S(2)}, u32[]{:S(2)}) collective-permute-start(bf16[2,16,1536]{2,1,0:T(8,128)(2,1)} %get-tuple-element.78), channel_id=1, source_target_pairs={{0,1},{1,0},{2,3},{3,2},{4,5},{5,4},{6,7},{7,6},{8,9},{9,8},{10,11... | collective-permute-start | bytes 294920 | tf_op jit(solution)/shard_map/ppermute | solution.py:27
  4.5 6.1 %collective-permute-start.1 = (bf16[2,16,1536]{2,1,0:T(8,128)(2,1)S(1)}, bf16[2,16,1536]{2,1,0:T(8,128)(2,1)S(1)}, u32[]{:S(2)}, u32[]{:S(2)}) collective-permute-start(bf16[2,16,1536]{2,1,0:T(8,128)(2,1)S(1)} %pad_maximum_fusion.3), channel_id=1, source_target_pairs={{0,2},{1,3},{2,0},{3,1},{4,6},{5,7},{6,4},{7,5},{8,10},{9,11},{10,... | collective-permute-start | bytes 294920 | tf_op jit(solution)/shard_map/ppermute | solution.py:27
  10.5 20.2 %collective-permute-start.5 = (bf16[1,256,1024]{2,1,0:T(8,128)(2,1)}, bf16[1,256,1024]{2,1,0:T(8,128)(2,1)S(1)}, u32[]{:S(2)}, u32[]{:S(2)}) collective-permute-start(bf16[1,256,1024]{2,1,0:T(8,128)(2,1)} %get-tuple-element.83), channel_id=1, source_target_pairs={{0,2},{1,3},{2,0},{3,1},{4,6},{5,7},{6,4},{7,5},{8,10},{9,11},{10,... | collective-permute-start | bytes 1572872 | tf_op jit(solution)/shard_map/ppermute | solution.py:27
  14.1 8.2 %collective-permute-start.2 = (bf16[128,512]{1,0:T(8,128)(2,1)S(1)}, bf16[128,512]{1,0:T(8,128)(2,1)S(1)}, u32[]{:S(2)}, u32[]{:S(2)}) collective-permute-start(bf16[128,512]{1,0:T(8,128)(2,1)S(1)} %get-tuple-element.79.mine_ref), channel_id=1, source_target_pairs={{0,16},{4,20},{8,24},{12,28},{16,0},{20,4},{24,8},{28,12},{1,17},{... | collective-permute-start | bytes 393224 | tf_op jit(solution)/shard_map/ppermute | solution.py:27
  22.3 8.4 %collective-permute-start.3 = (bf16[176,512]{1,0:T(8,128)(2,1)S(1)}, bf16[176,512]{1,0:T(8,128)(2,1)S(1)}, u32[]{:S(2)}, u32[]{:S(2)}) collective-permute-start(bf16[176,512]{1,0:T(8,128)(2,1)S(1)} %shard_map.274.mine_ref), channel_id=1, source_target_pairs={{0,8},{4,12},{8,0},{12,4},{16,24},{20,28},{24,16},{28,20},{1,9},{5... | collective-permute-start | bytes 540680 | tf_op jit(solution)/shard_map/ppermute | solution.py:27
  23.1 6.8 %collective-permute-start.4 = (bf16[1,128,512]{2,1,0:T(8,128)(2,1)S(1)}, bf16[1,128,512]{2,1,0:T(8,128)(2,1)S(1)}, u32[]{:S(2)}, u32[]{:S(2)}) collective-permute-start(bf16[1,128,512]{2,1,0:T(8,128)(2,1)S(1)} %bitcast.13), channel_id=1, source_target_pairs={{0,16},{4,20},{8,24},{12,28},{16,0},{20,4},{24,8},{28,12},{1,17},{... | collective-permute-start | bytes 393224 | tf_op jit(solution)/shard_map/ppermute | solution.py:27
  30.7 11.9 %collective-permute-start.7 = (bf16[2,256,1024]{2,1,0:T(8,128)(2,1)S(1)}, bf16[2,256,1024]{2,1,0:T(8,128)(2,1)S(1)}, u32[]{:S(2)}, u32[]{:S(2)}) collective-permute-start(bf16[2,256,1024]{2,1,0:T(8,128)(2,1)S(1)} %constant_dynamic-update-slice_fusion.x_ref), channel_id=1, source_target_pairs={{0,1},{1,0},{2,3},{3,2},{4,5},{5,4},{6,7},{7,6},{8,9},{9,8},{10,11... | collective-permute-start | bytes 3145736 | tf_op jit(solution)/shard_map/ppermute | solution.py:27
  30.9 11.1 %collective-permute-start.6 = (bf16[272,512]{1,0:T(8,128)(2,1)S(1)}, bf16[272,512]{1,0:T(8,128)(2,1)S(1)}, u32[]{:S(2)}, u32[]{:S(2)}) collective-permute-start(bf16[272,512]{1,0:T(8,128)(2,1)S(1)} %shard_map.275.first_ref), channel_id=1, source_target_pairs={{0,4},{4,0},{8,12},{12,8},{16,20},{20,16},{24,28},{28,24},{1,5},{5... | collective-permute-start | bytes 835592 | tf_op jit(solution)/shard_map/ppermute | solution.py:27
  32.4 9.6 %collective-permute-start.8 = (bf16[2,128,512]{2,1,0:T(8,128)(2,1)S(1)}, bf16[2,128,512]{2,1,0:T(8,128)(2,1)S(1)}, u32[]{:S(2)}, u32[]{:S(2)}) collective-permute-start(bf16[2,128,512]{2,1,0:T(8,128)(2,1)S(1)} %pad_maximum_fusion.1), channel_id=1, source_target_pairs={{0,8},{4,12},{8,0},{12,4},{16,24},{20,28},{24,16},{28,20},{1,9},{5... | collective-permute-start | bytes 786440 | tf_op jit(solution)/shard_map/ppermute | solution.py:27
  42.1 13.9 %collective-permute-start.9 = (bf16[4,128,512]{2,1,0:T(8,128)(2,1)S(1)}, bf16[4,128,512]{2,1,0:T(8,128)(2,1)S(1)}, u32[]{:S(2)}, u32[]{:S(2)}) collective-permute-start(bf16[4,128,512]{2,1,0:T(8,128)(2,1)S(1)} %pad_maximum_fusion.second_ref), channel_id=1, source_target_pairs={{0,4},{4,0},{8,12},{12,8},{16,20},{20,16},{24,28},{28,24},{1,5},{5... | collective-permute-start | bytes 1572872 | tf_op jit(solution)/shard_map/ppermute | solution.py:27
  54.4 8.1 %collective-permute-start.11 = (bf16[4,64,512]{2,1,0:T(8,128)(2,1)S(1)}, bf16[4,64,512]{2,1,0:T(8,128)(2,1)S(1)}, u32[]{:S(2)}, u32[]{:S(2)}) collective-permute-start(bf16[4,64,512]{2,1,0:T(8,128)(2,1)S(1)} %get-tuple-element.111), channel_id=1, source_target_pairs={{0,4},{4,0},{8,12},{12,8},{16,20},{20,16},{24,28},{28,24},{1,5},{5... | collective-permute-start | bytes 786440 | tf_op jit(solution)/shard_map/ppermute | solution.py:27
  59.9 9.3 %collective-permute-start.10 = (bf16[4,80,512]{2,1,0:T(8,128)(2,1)S(1)}, bf16[4,80,512]{2,1,0:T(8,128)(2,1)S(1)}, u32[]{:S(2)}, u32[]{:S(2)}) collective-permute-start(bf16[4,80,512]{2,1,0:T(8,128)(2,1)S(1)} %get-tuple-element.108), channel_id=1, source_target_pairs={{0,4},{4,0},{8,12},{12,8},{16,20},{20,16},{24,28},{28,24},{1,5},{5... | collective-permute-start | bytes 983048 | tf_op jit(solution)/shard_map/ppermute | solution.py:27
  62.6 6.6 %collective-permute-start.12 = (bf16[2,64,512]{2,1,0:T(8,128)(2,1)S(1)}, bf16[2,64,512]{2,1,0:T(8,128)(2,1)S(1)}, u32[]{:S(2)}, u32[]{:S(2)}) collective-permute-start(bf16[2,64,512]{2,1,0:T(8,128)(2,1)S(1)} %slice.140), channel_id=1, source_target_pairs={{0,8},{4,12},{8,0},{12,4},{16,24},{20,28},{24,16},{28,20},{1,9},{5... | collective-permute-start | bytes 393224 | tf_op jit(solution)/shard_map/ppermute | solution.py:27
  69.2 2.7 %collective-permute-start.13 = (bf16[2,256,1024]{2,1,0:T(8,128)(2,1)S(1)}, bf16[2,256,1024]{2,1,0:T(8,128)(2,1)S(1)}, u32[]{:S(2)}, u32[]{:S(2)}) collective-permute-start(bf16[2,256,1024]{2,1,0:T(8,128)(2,1)S(1)} %get-tuple-element.112), channel_id=1, source_target_pairs={{0,1},{1,0},{2,3},{3,2},{4,5},{5,4},{6,7},{7,6},{8,9},{9,8},{10,11... | collective-permute-start | bytes 3145736 | tf_op jit(solution)/shard_map/ppermute | solution.py:27
  70.0 12.0 %collective-permute-start.15 = (bf16[1,64,512]{2,1,0:T(8,128)(2,1)S(1)}, bf16[1,64,512]{2,1,0:T(8,128)(2,1)S(1)}, u32[]{:S(2)}, u32[]{:S(2)}) collective-permute-start(bf16[1,64,512]{2,1,0:T(8,128)(2,1)S(1)} %slice.143), channel_id=1, source_target_pairs={{0,16},{4,20},{8,24},{12,28},{16,0},{20,4},{24,8},{28,12},{1,17},{... | collective-permute-start | bytes 196616 | tf_op jit(solution)/shard_map/ppermute | solution.py:27
  72.0 10.1 %collective-permute-start.14 = (bf16[2,80,512]{2,1,0:T(8,128)(2,1)S(1)}, bf16[2,80,512]{2,1,0:T(8,128)(2,1)S(1)}, u32[]{:S(2)}, u32[]{:S(2)}) collective-permute-start(bf16[2,80,512]{2,1,0:T(8,128)(2,1)S(1)} %slice.138), channel_id=1, source_target_pairs={{0,8},{4,12},{8,0},{12,4},{16,24},{20,28},{24,16},{28,20},{1,9},{5... | collective-permute-start | bytes 491528 | tf_op jit(solution)/shard_map/ppermute | solution.py:27
  73.8 8.2 %collective-permute-start.16 = (bf16[4,64,512]{2,1,0:T(8,128)(2,1)S(1)}, bf16[4,64,512]{2,1,0:T(8,128)(2,1)S(1)}, u32[]{:S(2)}, u32[]{:S(2)}) collective-permute-start(bf16[4,64,512]{2,1,0:T(8,128)(2,1)S(1)} %get-tuple-element.118), channel_id=1, source_target_pairs={{0,4},{4,0},{8,12},{12,8},{16,20},{20,16},{24,28},{28,24},{1,5},{5... | collective-permute-start | bytes 786440 | tf_op jit(solution)/shard_map/ppermute | solution.py:27
  75.5 14.2 %collective-permute-start.19 = (bf16[1,256,1024]{2,1,0:T(8,128)(2,1)S(1)}, bf16[1,256,1024]{2,1,0:T(8,128)(2,1)S(1)}, u32[]{:S(2)}, u32[]{:S(2)}) collective-permute-start(bf16[1,256,1024]{2,1,0:T(8,128)(2,1)S(1)} %slice.137), channel_id=1, source_target_pairs={{0,2},{1,3},{2,0},{3,1},{4,6},{5,7},{6,4},{7,5},{8,10},{9,11},{10,... | collective-permute-start | bytes 1572872 | tf_op jit(solution)/shard_map/ppermute | solution.py:27
  82.2 6.2 %collective-permute-start.17 = (bf16[1,80,512]{2,1,0:T(8,128)(2,1)S(1)}, bf16[1,80,512]{2,1,0:T(8,128)(2,1)S(1)}, u32[]{:S(2)}, u32[]{:S(2)}) collective-permute-start(bf16[1,80,512]{2,1,0:T(8,128)(2,1)S(1)} %slice.141), channel_id=1, source_target_pairs={{0,16},{4,20},{8,24},{12,28},{16,0},{20,4},{24,8},{28,12},{1,17},{... | collective-permute-start | bytes 245768 | tf_op jit(solution)/shard_map/ppermute | solution.py:27
  83.9 5.8 %collective-permute-start.18 = (bf16[2,64,512]{2,1,0:T(8,128)(2,1)S(1)}, bf16[2,64,512]{2,1,0:T(8,128)(2,1)S(1)}, u32[]{:S(2)}, u32[]{:S(2)}) collective-permute-start(bf16[2,64,512]{2,1,0:T(8,128)(2,1)S(1)} %slice.139), channel_id=1, source_target_pairs={{0,8},{4,12},{8,0},{12,4},{16,24},{20,28},{24,16},{28,20},{1,9},{5... | collective-permute-start | bytes 393224 | tf_op jit(solution)/shard_map/ppermute | solution.py:27
  84.2 11.5 %collective-permute-start.22 = (f32[16,512]{1,0:T(8,128)S(1)}, f32[16,512]{1,0:T(8,128)S(1)}, u32[]{:S(2)}, u32[]{:S(2)}) collective-permute-start(f32[16,512]{1,0:T(8,128)S(1)} %slice_bitcast_fusion.2), channel_id=1, source_target_pairs={{0,0},{8,1},{16,2},{24,3},{4,4},{12,5},{20,6},{28,7},{1,8},{9,9},{... | collective-permute-start | bytes 98312 | tf_op jit(solution)/shard_map/ppermute | solution.py:1055
  89.9 4.9 %collective-permute-start.20 = (bf16[2,32,896]{2,1,0:T(8,128)(2,1)S(1)}, bf16[2,32,896]{2,1,0:T(8,128)(2,1)S(1)}, u32[]{:S(2)}, u32[]{:S(2)}) collective-permute-start(bf16[2,32,896]{2,1,0:T(8,128)(2,1)S(1)} %get-tuple-element.125), channel_id=1, source_target_pairs={{0,2},{1,3},{2,0},{3,1},{4,6},{5,7},{6,4},{7,5},{8,10},{9,11},{10,... | collective-permute-start | bytes 344072 | tf_op jit(solution)/shard_map/ppermute | solution.py:27
  90.5 5.7 %collective-permute-start.23 = (bf16[1,64,512]{2,1,0:T(8,128)(2,1)S(1)}, bf16[1,64,512]{2,1,0:T(8,128)(2,1)S(1)}, u32[]{:S(2)}, u32[]{:S(2)}) collective-permute-start(bf16[1,64,512]{2,1,0:T(8,128)(2,1)S(1)} %slice.142), channel_id=1, source_target_pairs={{0,16},{4,20},{8,24},{12,28},{16,0},{20,4},{24,8},{28,12},{1,17},{... | collective-permute-start | bytes 196616 | tf_op jit(solution)/shard_map/ppermute | solution.py:27
  94.8 1.4 %collective-permute-start.21 = (bf16[2,32,896]{2,1,0:T(8,128)(2,1)S(1)}, bf16[2,32,896]{2,1,0:T(8,128)(2,1)S(1)}, u32[]{:S(2)}, u32[]{:S(2)}) collective-permute-start(bf16[2,32,896]{2,1,0:T(8,128)(2,1)S(1)} %pad_maximum_fusion.2), channel_id=1, source_target_pairs={{0,1},{1,0},{2,3},{3,2},{4,5},{5,4},{6,7},{7,6},{8,9},{9,8},{10,11... | collective-permute-start | bytes 344072 | tf_op jit(solution)/shard_map/ppermute | solution.py:27
  (5 other events, 60.5 us)
